TPU v7x, 32 devices: a whole 2x2x4 slice. The times are simulated.
32 devices in a mesh: inner: 4 (over x, core), outer: 8 (over z, y).
Axes of the slice: x: 2, y: 2, z: 4, core: 2. Of those that a mesh axis runs over, the one named last changes fastest.
Arguments:
- queries: bfloat16 [4096, 2048], P(('outer', 'inner')), may hold values from -6 to 6
- keys: bfloat16 [4096, 2048], P(('outer', 'inner')), may hold values from -6 to 6
- values: bfloat16 [4096, 2048], P(('outer', 'inner')), may hold values from -6 to 6
- out_grad: bfloat16 [4096, 2048], P(('outer', 'inner')), may hold values from -6 to 6
- positions: int32 [4096], P(('outer', 'inner')), may hold values from 0 to 8191
Outputs:
- attended: bfloat16 [4096, 2048], P(('outer', 'inner'))
- query_grad: bfloat16 [4096, 2048], P(('outer', 'inner'))
- key_grad: bfloat16 [4096, 2048], P(('outer', 'inner'))
- value_gradient: bfloat16 [4096, 2048], P(('outer', 'inner'))
All inputs are finite; a program needn't handle non-finite values.
Results may differ from a plain program's by a relative error of at most 0.0064.
Values sent between devices are 32-bit elements; how exact they have to be, the bound alone decides.
No kernel may reach another device: no remote copies, remote signals or barrier semaphores. Data moves between devices by JAX's collectives and lax.ppermute only.
A program may use at most 256 MiB of HBM per device.

v0:
```python
import math

import jax
import jax.numpy as jnp
from jax import lax
from jax.sharding import PartitionSpec as P

D_HEAD = 128


def carried_in(value, axis, join, neutral, backward):
    count, mine = (lax.axis_size(axis), lax.axis_index(axis))
    pieces = lax.all_gather(value, axis)
    if backward:
        pieces = pieces[::-1]
        mine = count - 1 - mine
    so_far = jnp.full_like(value, 0) + jnp.asarray(neutral, value.dtype)

    def step(position, so_far):
        longer = join(so_far, pieces[position])
        return jnp.where(position < mine, longer, so_far)

    return lax.fori_loop(0, count - 1, step, so_far)


def rotary_tables(positions, head_dim):
    half_dim = head_dim // 2
    spacing = jnp.arange(half_dim).astype(jnp.float32) * (-2.0 * math.log(500000.0) / head_dim)
    angle = positions.astype(jnp.float32)[:, None] * jnp.exp(spacing)[None, :]
    return (jnp.cos(angle)[:, None, :], jnp.sin(angle)[:, None, :])


def rotate(rows, cosine, sine):
    half_dim = rows.shape[-1] // 2
    first = rows[..., :half_dim].astype(jnp.float32)
    second = rows[..., half_dim:].astype(jnp.float32)
    return jnp.concatenate(
        [first * cosine - second * sine, second * cosine + first * sine], axis=-1
    )


def unrotate(rows, cosine, sine):
    half_dim = rows.shape[-1] // 2
    first = rows[..., :half_dim]
    second = rows[..., half_dim:]
    return jnp.concatenate(
        [first * cosine + second * sine, second * cosine - first * sine], axis=-1
    )


def add_states(earlier, later):
    return earlier + later


def outer_sums(keys_group, queries_group):
    zero_part = jnp.zeros_like(keys_group)
    keys_earlier = carried_in(keys_group, "outer", add_states, zero_part, False)
    queries_later = carried_in(queries_group, "outer", add_states, zero_part, True)
    return (keys_earlier, queries_later)


def shards(queries, keys, values, out_grad, positions):
    rows_here = queries.shape[0]
    head_dim = D_HEAD
    heads_count = queries.shape[1] // head_dim
    total_tokens = rows_here * lax.axis_size("inner") * lax.axis_size("outer")
    scale_factor = (head_dim * total_tokens) ** (-0.5)
    cosine, sine = rotary_tables(positions, head_dim)
    shaped = (rows_here, heads_count, head_dim)
    rotated_query = rotate(queries.reshape(shaped), cosine, sine).astype(jnp.bfloat16)
    rotated_key = rotate(keys.reshape(shaped), cosine, sine).astype(jnp.bfloat16)
    value_row_block = values.reshape(shaped)
    gradient_row_block = out_grad.reshape(shaped)
    key_value_state = jnp.einsum(
        "pob,poj->obj", rotated_key, value_row_block, preferred_element_type=jnp.float32
    )
    query_state = jnp.einsum(
        "pob,poj->obj", rotated_query, gradient_row_block, preferred_element_type=jnp.float32
    )
    own_place = lax.axis_index("inner")
    piece = (
        lax.all_gather(key_value_state[None], "inner", axis=0, tiled=True),
        lax.all_gather(query_state[None], "inner", axis=0, tiled=True),
    )
    count = piece[0].shape[0]
    order = jnp.arange(count, dtype=jnp.int32)
    earlier = (order < own_place)[:, None, None, None]
    later = (order > own_place)[:, None, None, None]
    keys_before = jnp.sum(jnp.where(earlier, piece[0], 0.0), axis=0)
    queries_after = jnp.sum(jnp.where(later, piece[1], 0.0), axis=0)
    keys_group = jnp.sum(piece[0], axis=0)
    queries_group = jnp.sum(piece[1], axis=0)
    keys_earlier, queries_later = outer_sums(keys_group, queries_group)
    preceding_state = (keys_earlier + keys_before).astype(jnp.bfloat16)
    following_state = (queries_later + queries_after).astype(jnp.bfloat16)
    causal = (jnp.arange(rows_here)[:, None] >= jnp.arange(rows_here)[None, :])[None]
    score_matrix = jnp.where(
        causal,
        jnp.einsum("thd,shd->hts", rotated_query, rotated_key, preferred_element_type=jnp.float32),
        0.0,
    ).astype(jnp.bfloat16)
    score_gradient = jnp.where(
        causal,
        jnp.einsum(
            "thd,shd->hts", gradient_row_block, value_row_block, preferred_element_type=jnp.float32
        ),
        0.0,
    ).astype(jnp.bfloat16)
    attended = scale_factor * (
        jnp.einsum(
            "rgb,brf->grf", score_matrix, value_row_block, preferred_element_type=jnp.float32
        )
        + jnp.einsum(
            "axz,xzo->axo", rotated_query, preceding_state, preferred_element_type=jnp.float32
        )
    )
    rotated_query_gradient = scale_factor * (
        jnp.einsum("rgb,brf->grf", score_gradient, rotated_key, preferred_element_type=jnp.float32)
        + jnp.einsum(
            "xge,gme->xgm", gradient_row_block, preceding_state, preferred_element_type=jnp.float32
        )
    )
    rotated_key_gradient = scale_factor * (
        jnp.einsum(
            "uox,oul->xul", score_gradient, rotated_query, preferred_element_type=jnp.float32
        )
        + jnp.einsum(
            "olb,lfb->olf", value_row_block, following_state, preferred_element_type=jnp.float32
        )
    )
    value_gradient = scale_factor * (
        jnp.einsum(
            "uox,oul->xul", score_matrix, gradient_row_block, preferred_element_type=jnp.float32
        )
        + jnp.einsum(
            "tyg,yge->tye", rotated_key, following_state, preferred_element_type=jnp.float32
        )
    )
    flat = (rows_here, heads_count * head_dim)
    return (
        attended.astype(jnp.bfloat16).reshape(flat),
        unrotate(rotated_query_gradient, cosine, sine).astype(jnp.bfloat16).reshape(flat),
        unrotate(rotated_key_gradient, cosine, sine).astype(jnp.bfloat16).reshape(flat),
        value_gradient.astype(jnp.bfloat16).reshape(flat),
    )


def solution(mesh):
    placed = (
        P(("outer", "inner"), None),
        P(("outer", "inner"), None),
        P(("outer", "inner"), None),
        P(("outer", "inner"), None),
        P(("outer", "inner")),
    )
    return jax.shard_map(
        shards,
        mesh=mesh,
        in_specs=placed,
        out_specs=(
            P(("outer", "inner"), None),
            P(("outer", "inner"), None),
            P(("outer", "inner"), None),
            P(("outer", "inner"), None),
        ),
        check_vma=False,
    )
```

profile of v0, /device:TPU:0, one launch (start us, length us, event | category | flops | bytes accessed | tf_op | source)
XLA Modules:
  0.0 394.6 jit_solution(2992144211153113958)
XLA Ops:
  13.8 37.3 %all-gather.13.cloned.1.call-done = f32[64,128,128]{2,1,0:T(8,128)} async-done(((f32[16,128,128]{2,1,0:T(8,128)}), f32[64,128,128]{2,1,0:T(8,128)}) %all-gather.13.cloned.1.call-update) | async-done | bytes 4194320 | tf_op jit(solution)/shard_map/all_gather | solution.py:83
  51.0 4.4 %select_reduce_fusion = (f32[16,128,128]{2,1,0:T(8,128)}, f32[16,128,128]{2,1,0:T(8,128)}) fusion(f32[4,16,128,128]{3,2,1,0:T(8,128)} %bitcast.90, pred[4]{0:T(512)(128)(4,1)S(1)} %iota_compare_fusion.1), kind=kLoop, calls=%fused_computation.2 | loop fusion | flops 2621440 | bytes 6291460 | tf_op jit(solution)/shard_map/reduce_sum | solution.py:90
  62.5 118.0 %all-gather.15.cloned.1.call-done = f32[128,128,128]{2,1,0:T(8,128)} async-done(((f32[16,128,128]{2,1,0:T(8,128)}), f32[128,128,128]{2,1,0:T(8,128)}) %all-gather.15.cloned.1.call-update) | async-done | bytes 8388624 | tf_op jit(solution)/shard_map/all_gather | solution.py:13
  180.5 7.7 %rev.3 = f32[8,16,128,128]{3,2,1,0:T(8,128)} reverse(f32[8,16,128,128]{3,2,1,0:T(8,128)} %bitcast.85), dimensions={0} | reverse | bytes 16777216 | tf_op jit(solution)/shard_map/rev | solution.py:15
  188.3 11.3 %while.29 = (s32[]{:T(128)}, f32[16,128,128]{2,1,0:T(8,128)S(1)}, s32[]{:T(128)}, f32[8,16,128,128]{3,2,1,0:T(8,128)}, s32[]{:T(128)}, /*index=5*/s32[]{:T(128)}) while((s32[]{:T(128)}, f32[16,128,128]{2,1,0:T(8,128)S(1)}, s32[]{:T(128)}, f32[8,16,128,128]{3,2,1,0:T(8,128)}, s32[]{:T(128)}, /*index=5*/s32[]{:T(128)}) %tuple.77), condition=%wide.region_6.7_spmd.clone, body=%wide.region_5.6_spmd.clone.sunk | while | flops 786436 | bytes 3145821 | solution.py:23
  191.5 1.6 add_select_fusion.5
  193.1 1.6 add_select_fusion.5
  194.7 1.6 add_select_fusion.5
  201.8 1.7 fusion.5
  206.8 32.6 %all-gather.9.cloned.1.call-done = f32[64,128,128]{2,1,0:T(8,128)} async-done(((f32[16,128,128]{2,1,0:T(8,128)}), f32[64,128,128]{2,1,0:T(8,128)}) %all-gather.9.cloned.1.call-update) | async-done | bytes 4194320 | tf_op jit(solution)/shard_map/all_gather | solution.py:82
  239.4 4.4 %select_reduce_fusion.1 = (f32[16,128,128]{2,1,0:T(8,128)}, f32[16,128,128]{2,1,0:T(8,128)}) fusion(f32[4,16,128,128]{3,2,1,0:T(8,128)} %bitcast.91, pred[4]{0:T(512)(128)(4,1)S(1)} %iota_compare_fusion.2), kind=kLoop, calls=%fused_computation.3 | loop fusion | flops 2621440 | bytes 6291460 | tf_op jit(solution)/shard_map/reduce_sum | solution.py:89
  244.3 1.7 convolution_bitcast_fusion.1
  247.2 2.0 copy.88
  249.2 2.3 pad_maximum_fusion.3
  251.5 2.1 copy.82
  253.6 2.1 copy.87
  255.7 2.5 convolution_bitcast_fusion.3
  258.3 110.6 %all-gather.11.cloned.1.call-done = f32[128,128,128]{2,1,0:T(8,128)} async-done(((f32[16,128,128]{2,1,0:T(8,128)}), f32[128,128,128]{2,1,0:T(8,128)}) %all-gather.11.cloned.1.call-update) | async-done | bytes 8388624 | tf_op jit(solution)/shard_map/all_gather | solution.py:13
  368.9 11.3 %while.28 = (s32[]{:T(128)}, f32[16,128,128]{2,1,0:T(8,128)S(1)}, s32[]{:T(128)}, f32[8,16,128,128]{3,2,1,0:T(8,128)}, s32[]{:T(128)}, /*index=5*/s32[]{:T(128)}) while((s32[]{:T(128)}, f32[16,128,128]{2,1,0:T(8,128)S(1)}, s32[]{:T(128)}, f32[8,16,128,128]{3,2,1,0:T(8,128)}, s32[]{:T(128)}, /*index=5*/s32[]{:T(128)}) %tuple.91), condition=%wide.region_2.3_spmd.clone, body=%wide.region_1.2_spmd.clone.sunk | while | flops 786436 | bytes 3145821 | solution.py:23
  370.5 1.6 add_select_fusion.4
  373.7 1.6 add_select_fusion.4
  375.3 1.6 add_select_fusion.4
  377.0 1.6 add_select_fusion.4
  384.5 2.0 copy.86
  (69 shorter events, 37.5 us)
Async XLA Ops:
  7.2 52.7 %copy-start = (bf16[128,2048]{1,0:T(8,128)(2,1)S(1)}, bf16[128,2048]{1,0:T(8,128)(2,1)}, u32[]{:S(2)}) copy-start(bf16[128,2048]{1,0:T(8,128)(2,1)} %param.11) | copy-start | bytes 1572868
  7.2 43.8 %all-gather.13.cloned.1.call-start = ((), (), s32[]{:S(2)}) async-start(), calls=%async_computation.2 | async-start | bytes 5242880 | tf_op jit(solution)/shard_map/all_gather | solution.py:83
  13.7 166.9 %all-gather.15.cloned.1.call-start = ((), (), s32[]{:S(2)}) async-start(), calls=%async_computation.3 | async-start | bytes 9437184 | tf_op jit(solution)/shard_map/all_gather | solution.py:13
  55.4 183.9 %all-gather.9.cloned.1.call-start = ((), (), s32[]{:S(2)}) async-start(), calls=%async_computation | async-start | bytes 5242880 | tf_op jit(solution)/shard_map/all_gather | solution.py:82
  60.4 0.8 copy-start.6
  199.6 3.9 copy-start.8
  201.0 0.8 copy-start.4
  206.6 162.3 %all-gather.11.cloned.1.call-start = ((), (), s32[]{:S(2)}) async-start(), calls=%async_computation.1 | async-start | bytes 9437184 | tf_op jit(solution)/shard_map/all_gather | solution.py:13
  244.3 1.8 copy-start.3
  380.2 2.2 copy-start.7
  381.6 0.8 copy-start.1
  382.7 3.8 copy-start.2
  382.7 3.8 copy-start.5
Sparse Core Ops, SparseCore 0:
  13.8 37.1 all-gather.12
  55.6 124.9 all-gather.14
  206.7 32.6 all-gather.8
  243.9 124.9 all-gather.10
where the time goes:
time: 396 us; the launch traced here: 395 us
  waiting for transfers between devices  299 us (76%)
  other arithmetic  40.3 us (10%)
  local copies, waits for them, and re-layouts  27.5 us (7%)
  between operations  14 us (4%)
  matrix products  13.6 us (3%)
    all_gather x2, waiting for transfers between devices, carried_in(): pieces = lax.all_gather(value, axis)  229 us
    all_gather x1, waiting for transfers between devices, shards(): lax.all_gather(query_state[None], 'inner', axis=0, tiled=True)  37.3 us
    all_gather x1, waiting for transfers between devices, shards(): lax.all_gather(key_value_state[None], 'inner', axis=0, tiled=True)  32.6 us
    select_n x14, other arithmetic, step(): return jnp.where(position < mine, longer, so_far)  22.2 us
    unnamed x28, local copies, waits for them, and re-layouts  14.6 us
  transfers between devices with their start and end apart: 4, of which 4 were waited for; matrix products, arithmetic and copies ran while one was open for 5% of the time, Pallas kernels for 0%

commit v1 on v0

v1 whole, which is shorter than its diff:
```python
import functools
import math

import jax
import jax.numpy as jnp
from jax import lax
from jax.experimental import pallas as pl
from jax.experimental.pallas import tpu as pltpu
from jax.sharding import Mesh, PartitionSpec as P

D = 128
F32 = jnp.float32
BF16 = jnp.bfloat16
VMEM_LIMIT = 24 * 1024 * 1024


def rotary_tables(positions):
    half = D // 2
    spacing = jnp.arange(half).astype(F32) * (-2.0 * math.log(500000.0) / D)
    spacing = jnp.concatenate([spacing, spacing])
    sign = jnp.concatenate([-jnp.ones((half,), F32), jnp.ones((half,), F32)])
    angle = positions.astype(F32)[:, None] * jnp.exp(spacing)[None, :]
    return jnp.cos(angle), jnp.sin(angle) * sign[None, :]


def rotate(rows, cosine, sine):
    wide = rows.astype(F32)
    return wide * cosine + pltpu.roll(wide, D // 2, 1) * sine


def unrotate(rows, cosine, sine):
    return rows * cosine - pltpu.roll(rows, D // 2, 1) * sine


def dot(a, b, ca, cb):
    return lax.dot_general(a, b, (((ca,), (cb,)), ((), ())), preferred_element_type=F32)


def states_kernel(half_ref, q_ref, k_ref, v_ref, g_ref, cos_ref, sin_ref, out_ref):
    del half_ref
    cosine, sine = cos_ref[...], sin_ref[...]
    for h in range(out_ref.shape[0]):
        cols = slice(h * D, (h + 1) * D)
        krot = rotate(k_ref[:, cols], cosine, sine).astype(BF16)
        qrot = rotate(q_ref[:, cols], cosine, sine).astype(BF16)
        out_ref[h, 0] = dot(krot, v_ref[:, cols], 0, 0)
        out_ref[h, 1] = dot(qrot, g_ref[:, cols], 0, 0)


def states(half, q, k, v, g, cosine, sine, heads):
    rows = q.shape[0]
    steps = 2
    per = heads // steps
    wide = pl.BlockSpec((rows, per * D), lambda i, half: (0, half[0] * steps + i))
    table = pl.BlockSpec((rows, D), lambda i, half: (0, 0))
    return pl.pallas_call(
        states_kernel,
        grid_spec=pltpu.PrefetchScalarGridSpec(
            num_scalar_prefetch=1,
            grid=(steps,),
            in_specs=[wide] * 4 + [table] * 2,
            out_specs=pl.BlockSpec((per, 2, D, D), lambda i, half: (i, 0, 0, 0)),
        ),
        out_shape=jax.ShapeDtypeStruct((heads, 2, D, D), F32),
        compiler_params=pltpu.CompilerParams(vmem_limit_bytes=VMEM_LIMIT),
        cost_estimate=pl.CostEstimate(
            flops=4 * heads * rows * D * D, bytes_accessed=4 * rows * heads * D * 2 + heads * 2 * D * D * 4,
            transcendentals=0,
        ),
        name="block_states",
    )(half, q, k, v, g, cosine, sine)


def local_kernel(q_ref, k_ref, v_ref, g_ref, cos_ref, sin_ref, rot_ref, sc_ref):
    cosine, sine = cos_ref[...], sin_ref[...]
    rows = q_ref.shape[0]
    keep = lax.broadcasted_iota(jnp.int32, (rows, rows), 0) >= lax.broadcasted_iota(
        jnp.int32, (rows, rows), 1
    )
    kept = lax.broadcasted_iota(jnp.int32, (rows, rows), 0) <= lax.broadcasted_iota(
        jnp.int32, (rows, rows), 1
    )
    for h in range(rot_ref.shape[0]):
        cols = slice(h * D, (h + 1) * D)
        krot = rotate(k_ref[:, cols], cosine, sine).astype(BF16)
        qrot = rotate(q_ref[:, cols], cosine, sine).astype(BF16)
        v, g = v_ref[:, cols], g_ref[:, cols]
        rot_ref[h, 0] = qrot
        rot_ref[h, 1] = krot
        sc_ref[h, 0] = jnp.where(keep, dot(qrot, krot, 1, 1), 0.0).astype(BF16)
        sc_ref[h, 1] = jnp.where(keep, dot(g, v, 1, 1), 0.0).astype(BF16)
        sc_ref[h, 2] = jnp.where(kept, dot(krot, qrot, 1, 1), 0.0).astype(BF16)
        sc_ref[h, 3] = jnp.where(kept, dot(v, g, 1, 1), 0.0).astype(BF16)


def local_scores(q, k, v, g, cosine, sine, heads):
    rows = q.shape[0]
    per = 4
    wide = pl.BlockSpec((rows, per * D), lambda i: (0, i))
    table = pl.BlockSpec((rows, D), lambda i: (0, 0))
    return pl.pallas_call(
        local_kernel,
        grid=(heads // per,),
        in_specs=[wide] * 4 + [table] * 2,
        out_specs=[
            pl.BlockSpec((per, 2, rows, D), lambda i: (i, 0, 0, 0)),
            pl.BlockSpec((per, 4, rows, rows), lambda i: (i, 0, 0, 0)),
        ],
        out_shape=[
            jax.ShapeDtypeStruct((heads, 2, rows, D), BF16),
            jax.ShapeDtypeStruct((heads, 4, rows, rows), BF16),
        ],
        compiler_params=pltpu.CompilerParams(vmem_limit_bytes=VMEM_LIMIT),
        cost_estimate=pl.CostEstimate(
            flops=8 * heads * rows * D * D, bytes_accessed=10 * rows * heads * D * 2, transcendentals=0
        ),
        name="local_scores",
    )(q, k, v, g, cosine, sine)


def outputs_kernel(scale, prior, half_ref, st_ref, rot_ref, sc_ref, v_ref, g_ref, cos_ref, sin_ref, *refs):
    del half_ref
    att_ref, qg_ref, kg_ref, vg_ref = refs[prior:]
    cosine, sine = cos_ref[...], sin_ref[...]
    for h in range(rot_ref.shape[0]):
        cols = slice(h * D, (h + 1) * D)
        v, g = v_ref[:, cols], g_ref[:, cols]
        qrot, krot = rot_ref[h, 0], rot_ref[h, 1]
        before = st_ref[h, 0].astype(BF16)
        after = st_ref[h, 1].astype(BF16)
        att = dot(sc_ref[h, 0], v, 1, 0) + dot(qrot, before, 1, 0)
        rqg = dot(sc_ref[h, 1], krot, 1, 0) + dot(g, before, 1, 1)
        rkg = dot(sc_ref[h, 3], qrot, 1, 0) + dot(v, after, 1, 1)
        vg = dot(sc_ref[h, 2], g, 1, 0) + dot(krot, after, 1, 0)
        att_ref[:, cols] = (scale * att).astype(BF16)
        qg_ref[:, cols] = unrotate(scale * rqg, cosine, sine).astype(BF16)
        kg_ref[:, cols] = unrotate(scale * rkg, cosine, sine).astype(BF16)
        vg_ref[:, cols] = (scale * vg).astype(BF16)


def outputs(scale, half, st, rot, sc, v, g, cosine, sine, prior):
    rows, width = v.shape
    heads = st.shape[0]
    steps = 2
    per = heads // steps
    wide = pl.BlockSpec((rows, per * D), lambda i, half: (0, half[0] * steps + i))
    table = pl.BlockSpec((rows, D), lambda i, half: (0, 0))
    by_head = lambda i, half: (half[0] * steps + i, 0, 0, 0)
    return pl.pallas_call(
        functools.partial(outputs_kernel, scale, len(prior)),
        grid_spec=pltpu.PrefetchScalarGridSpec(
            num_scalar_prefetch=1,
            grid=(steps,),
            in_specs=[
                pl.BlockSpec((per, 2, D, D), lambda i, half: (i, 0, 0, 0)),
                pl.BlockSpec((per, 2, rows, D), by_head),
                pl.BlockSpec((per, 4, rows, rows), by_head),
                wide,
                wide,
                table,
                table,
            ]
            + [pl.BlockSpec(memory_space=pl.ANY)] * len(prior),
            out_specs=[wide] * 4,
        ),
        out_shape=[jax.ShapeDtypeStruct((rows, width), BF16)] * 4,
        input_output_aliases={8 + i: i for i in range(len(prior))},
        compiler_params=pltpu.CompilerParams(vmem_limit_bytes=VMEM_LIMIT),
        cost_estimate=pl.CostEstimate(
            flops=16 * heads * rows * D * D, bytes_accessed=12 * rows * heads * D * 2, transcendentals=0
        ),
        name="block_outputs",
    )(half, st, rot, sc, v, g, cosine, sine, *prior)


GROUP = ("zl", "y", "x")


def swap(value, axis):
    return lax.ppermute(value, axis, [(0, 1), (1, 0)])


def shards(q, k, v, g, positions):
    rows, width = q.shape
    heads = width // D
    part = heads // 2
    tokens = rows
    for axis in ("x", "core", "zh", "zl", "y"):
        tokens = tokens * lax.axis_size(axis)
    scale = (D * tokens) ** (-0.5)
    cosine, sine = rotary_tables(positions)
    core = lax.axis_index("core")
    mine, theirs = core.reshape(1), (1 - core).reshape(1)

    far = states(theirs, q, k, v, g, cosine, sine, part)
    near_other = swap(far, "core")
    near = states(mine, q, k, v, g, cosine, sine, part)
    chip = near + near_other

    members = lax.axis_size(GROUP)
    place = lax.axis_index(GROUP)
    cut = D * part // members
    pieces = chip.reshape(part, 2, D // cut, cut, D).swapaxes(1, 2).reshape(members, 2, cut, D)
    held = lax.all_to_all(pieces, GROUP, 0, 0, tiled=True)

    keys, queries = held[:, 0], held[:, 1]
    keys_all, queries_all = jnp.sum(keys, axis=0), jnp.sum(queries, axis=0)
    groups = lax.axis_size("zh")
    group = lax.axis_index("zh")
    if groups == 2:
        passed = swap(jnp.where(group == 0, keys_all, queries_all), "zh")
        keys_in = jnp.where(group == 1, passed, 0.0)
        queries_in = jnp.where(group == 0, passed, 0.0)
    else:
        both = lax.all_gather(jnp.stack([keys_all, queries_all]), "zh")
        order = jnp.arange(groups)[:, None, None]
        keys_in = jnp.sum(jnp.where(order < group, both[:, 0], 0.0), axis=0)
        queries_in = jnp.sum(jnp.where(order > group, both[:, 1], 0.0), axis=0)
    rot, sc = local_scores(q, k, v, g, cosine, sine, heads)
    before, total = [], keys_in
    for j in range(members):
        before.append(total)
        total = total + keys[j]
    after, total = [], queries_in
    for j in reversed(range(members)):
        after.insert(0, total)
        total = total + queries[j]
    back = jnp.stack([jnp.stack(before), jnp.stack(after)], axis=1)
    chip_state = lax.all_to_all(back, GROUP, 0, 0, tiled=True)
    chip_state = (
        chip_state.reshape(part, D // cut, 2, cut, D).swapaxes(1, 2).reshape(part, 2, D, D)
    )

    side = jnp.arange(2)[None, :, None, None]
    to_mine = chip_state + jnp.where(side == 1 - core, near_other, 0.0)
    to_theirs = chip_state + jnp.where(side == core, near, 0.0)
    far_state = swap(to_theirs, "core")
    first = outputs(scale, mine, to_mine, rot, sc, v, g, cosine, sine, ())
    return tuple(outputs(scale, theirs, far_state, rot, sc, v, g, cosine, sine, tuple(first)))


def solution(mesh):
    inner, outer = mesh.shape["inner"], mesh.shape["outer"]
    x = inner // 2
    y = x if outer % x == 0 else 1
    z = outer // y
    zl = 2 if z % 2 == 0 else 1
    whole = Mesh(mesh.devices.reshape(x, 2, z // zl, zl, y), ("x", "core", "zh", "zl", "y"))
    rows = ("zh", "zl", "y", "x", "core")
    return jax.shard_map(
        shards,
        mesh=whole,
        in_specs=(P(rows, None),) * 4 + (P(rows),),
        out_specs=(P(rows, None),) * 4,
        check_vma=False,
    )
```

time: 396 us -> 76.4 us (0.19)
  waiting for transfers between devices: 299 us -> 32.2 us
  other arithmetic: 40.3 us -> 15.2 us
  local copies, waits for them, and re-layouts: 27.5 us -> 5.17 us
  matrix products: 13.6 us -> 0 us
  starting transfers between devices: 0.34 us -> 13.6 us
  between operations: 14 us -> 0.81 us
  Pallas kernels: 0 us -> 8.29 us
    all_gather x4 -> x0, waiting for transfers between devices: 298 us -> none  [the longest x2 229 us: carried_in(): pieces = lax.all_gather(value, axis)]
    all_to_all x0 -> x2, waiting for transfers between devices: none -> 27 us  [the longest x1 15 us: shards(): held = lax.all_to_all(pieces, GROUP, 0, 0, tiled=True)]
    select_n x14 -> x1, other arithmetic: 22.2 us -> 0.01 us  [shards(): passed = swap(jnp.where(group == 0, keys_all, queries_all), 'zh')]
    dot_general x12 -> x0, matrix products: 13.6 us -> none  [the longest x1 2.54 us: shards(): jnp.einsum('rgb,brf->grf', score_matrix, value_row_block, preferred_eleme...]
    all_to_all x0 -> x2, starting transfers between devices: none -> 10.4 us  [the longest x1 6.1 us: shards(): held = lax.all_to_all(pieces, GROUP, 0, 0, tiled=True)]
    unnamed x28 -> x21, local copies, waits for them, and re-layouts: 14.6 us -> 5.17 us
    pallas_call x0 -> x5, Pallas kernels: none -> 8.29 us  [the longest x2 4.11 us: outputs(): pl.pallas_call(functools.partial(outputs_kernel, scale, len(prior)), grid...]
    rev x1 -> x0, local copies, waits for them, and re-layouts: 7.73 us -> none  [carried_in(): pieces = pieces[::-1]]
  transfers between devices with their start and end apart: 4 -> 5, of which waited for: 4 -> 4; matrix products, arithmetic and copies ran while one was open for 5% -> 0% of each run, Pallas kernels for 0% -> 7%
where the time goes in v1:
time: 76.4 us; the launch traced here: 75.2 us
  waiting for transfers between devices  32.2 us (42%)
  other arithmetic  15.2 us (20%)
  starting transfers between devices  13.6 us (18%)
  Pallas kernels  8.29 us (11%)
  local copies, waits for them, and re-layouts  5.17 us (7%)
  between operations  0.81 us (1%)
    all_to_all x1, waiting for transfers between devices, shards(): held = lax.all_to_all(pieces, GROUP, 0, 0, tiled=True)  15 us
    all_to_all x1, waiting for transfers between devices, shards(): chip_state = lax.all_to_all(back, GROUP, 0, 0, tiled=True)  12 us
    unnamed x9, other arithmetic  7.16 us
    all_to_all x1, starting transfers between devices, shards(): held = lax.all_to_all(pieces, GROUP, 0, 0, tiled=True)  6.1 us
    ppermute x3, waiting for transfers between devices, swap(): return lax.ppermute(value, axis, [(0, 1), (1, 0)])  5.22 us
    unnamed x21, local copies, waits for them, and re-layouts  5.17 us
    all_to_all x1, starting transfers between devices, shards(): chip_state = lax.all_to_all(back, GROUP, 0, 0, tiled=True)  4.25 us
    pallas_call x2, Pallas kernels, outputs(): pl.pallas_call(functools.partial(outputs_kernel, scale, len(prior)), grid...  4.11 us
  transfers between devices with their start and end apart: 5, of which 4 were waited for; matrix products, arithmetic and copies ran while one was open for 0% of the time, Pallas kernels for 7%

profile of v1, /device:TPU:0, one launch (start us, length us, event | category | flops | bytes accessed | tf_op | source)
XLA Modules:
  0.0 75.2 jit_solution(11807469975906175815)
XLA Ops:
  1.4 1.0 %fusion = (f32[128,128]{1,0:T(8,128)S(1)}, f32[128,128]{1,0:T(8,128)S(1)}) fusion(f32[128]{0:T(128)} %constant.19.clone.1, f32[128]{0:T(128)S(1)} %maximum_exponential_fusion, f32[128]{0:T(128)S(1)} %convert_element_type.11), kind=kLoop, calls=%fused_computation.7 | loop fusion | flops 32768 | bytes 132608 | tf_op jit(solution)/shard_map/mul | solution.py:23
  2.4 1.0 %copy-done = bf16[128,2048]{1,0:T(8,128)(2,1)S(1)} copy-done((bf16[128,2048]{1,0:T(8,128)(2,1)S(1)}, bf16[128,2048]{1,0:T(8,128)(2,1)}, u32[]{:S(2)}) %copy-start) | copy-done | bytes 524312
  3.4 1.0 %copy-done.2 = bf16[128,2048]{1,0:T(8,128)(2,1)S(1)} copy-done((bf16[128,2048]{1,0:T(8,128)(2,1)S(1)}, bf16[128,2048]{1,0:T(8,128)(2,1)}, u32[]{:S(2)}) %copy-start.2) | copy-done | bytes 524312
  4.4 1.0 %copy-done.4 = bf16[128,2048]{1,0:T(8,128)(2,1)S(1)} copy-done((bf16[128,2048]{1,0:T(8,128)(2,1)S(1)}, bf16[128,2048]{1,0:T(8,128)(2,1)}, u32[]{:S(2)}) %copy-start.4) | copy-done | bytes 524312
  5.5 1.0 %copy-done.6 = bf16[128,2048]{1,0:T(8,128)(2,1)S(1)} copy-done((bf16[128,2048]{1,0:T(8,128)(2,1)S(1)}, bf16[128,2048]{1,0:T(8,128)(2,1)}, u32[]{:S(2)}) %copy-start.6) | copy-done | bytes 524312
  6.5 0.9 %block_states.3 = f32[8,2,128,128]{3,2,1,0:T(8,128)S(1)} custom-call(s32[1]{0:T(128)} %bitcast.half_ref, bf16[128,2048]{1,0:T(8,128)(2,1)S(1)} %copy-done.4, bf16[128,2048]{1,0:T(8,128)(2,1)S(1)} %copy-done.6, bf16[128,2048]{1,0:T(8,128)(2,1)S(1)} %copy-done, bf16[128,2048]{1,0:T(8,128)(2,1)S(1)} %copy-done.2, f32[128,128]{1,0:T(8,128)S(1)} %get-tuple-element.37.cos_ref, ...), custom_call_target="tpu_custom_call" | custom-call | flops 67108864 | bytes 2097152 | tf_op jit(solution)/shard_map/block_states/pallas_call | solution.py:56
  8.0 0.9 %block_states.2 = f32[8,2,128,128]{3,2,1,0:T(8,128)S(1)} custom-call(s32[1]{0:T(128)} %bitcast.1.half_ref, bf16[128,2048]{1,0:T(8,128)(2,1)S(1)} %copy-done.5, bf16[128,2048]{1,0:T(8,128)(2,1)S(1)} %copy-done.6, bf16[128,2048]{1,0:T(8,128)(2,1)S(1)} %copy-done.1, bf16[128,2048]{1,0:T(8,128)(2,1)S(1)} %copy-done.2, f32[128,128]{1,0:T(8,128)S(1)} %get-tuple-element.37.cos_ref, ...), custom_call_target="tpu_custom_call" | custom-call | flops 67108864 | bytes 2097152 | tf_op jit(solution)/shard_map/block_states/pallas_call | solution.py:56
  8.9 1.4 %collective-permute-done = f32[8,2,128,128]{3,2,1,0:T(8,128)S(1)} collective-permute-done((f32[8,2,128,128]{3,2,1,0:T(8,128)S(1)}, f32[8,2,128,128]{3,2,1,0:T(8,128)S(1)}, u32[]{:S(2)}, u32[]{:S(2)}) %collective-permute-start) | collective-permute-done | bytes 1048608 | tf_op jit(solution)/shard_map/ppermute | solution.py:180
  10.2 1.0 %copy-done.8 = f32[8,2,128,128]{3,2,1,0:T(8,128)} copy-done((f32[8,2,128,128]{3,2,1,0:T(8,128)}, f32[8,2,128,128]{3,2,1,0:T(8,128)S(1)}, u32[]{:S(2)}) %copy-start.8) | copy-done | bytes 1048600
  11.2 1.1 %add.51 = f32[8,2,128,128]{3,2,1,0:T(8,128)} add(f32[8,2,128,128]{3,2,1,0:T(8,128)S(1)} %block_states.2, f32[8,2,128,128]{3,2,1,0:T(8,128)S(1)} %collective-permute-done) | non-fusion elementwise | flops 262144 | bytes 3145728 | tf_op jit(solution)/shard_map/add | solution.py:198
  12.3 6.1 %all-to-all-start = ((f32[8,2,128,128]{3,2,1,0:T(8,128)}), f32[8,2,128,128]{3,2,1,0:T(8,128)}, u32[]{:S(2)}, u32[]{:S(2)}) async-start(f32[8,2,128,128]{3,2,1,0:T(8,128)} %add.51), calls=%async_computation | async-start | bytes 2097152 | tf_op jit(solution)/shard_map/all_to_all | solution.py:204
  18.4 15.0 %all-to-all-done = f32[8,2,128,128]{3,2,1,0:T(8,128)} async-done(((f32[8,2,128,128]{3,2,1,0:T(8,128)}), f32[8,2,128,128]{3,2,1,0:T(8,128)}, u32[]{:S(2)}, u32[]{:S(2)}) %all-to-all-start) | async-done | bytes 1048608 | tf_op jit(solution)/shard_map/all_to_all | solution.py:204
  33.4 1.3 %slice_reduce_fusion = (f32[128,128]{1,0:T(8,128)S(1)}, f32[128,128]{1,0:T(8,128)S(1)}) fusion(f32[8,2,128,128]{3,2,1,0:T(8,128)} %all-to-all-done), kind=kLoop, calls=%fused_computation.3 | loop fusion | flops 229376 | bytes 1179648 | tf_op jit(solution)/shard_map/reduce_sum | solution.py:207
  34.7 2.7 %collective-permute-start.1 = (f32[128,128]{1,0:T(8,128)S(1)}, f32[128,128]{1,0:T(8,128)S(1)}, u32[]{:S(2)}, u32[]{:S(2)}) collective-permute-start(f32[128,128]{1,0:T(8,128)S(1)} %broadcast_select_fusion), channel_id=1, source_target_pairs={{0,4},{4,0},{1,5},{5,1},{2,6},{6,2},{3,7},{7,3},{8,12},{12,8},{9,1... | collective-permute-start | bytes 196616 | tf_op jit(solution)/shard_map/ppermute | solution.py:180
  37.4 3.8 %collective-permute-done.1 = f32[128,128]{1,0:T(8,128)S(1)} collective-permute-done((f32[128,128]{1,0:T(8,128)S(1)}, f32[128,128]{1,0:T(8,128)S(1)}, u32[]{:S(2)}, u32[]{:S(2)}) %collective-permute-start.1) | collective-permute-done | bytes 65568 | tf_op jit(solution)/shard_map/ppermute | solution.py:180
  41.2 1.1 %bitcast_dynamic-update-slice_fusion.12 = (f32[8,128,128]{2,1,0:T(8,128)S(1)}, f32[128,128]{1,0:T(8,128)S(1)}, f32[8,128,128]{2,1,0:T(8,128)S(1)}, f32[128,128]{...) fusion(f32[8,128,128]{2,1,0:T(8,128)S(1)} %bitcast_dynamic-update-slice_fusion.13, ...), kind=kLoop, calls=%fused_computation.52 | loop fusion | flops 163839 | bytes 983042
  46.7 0.9 %fusion.12 = (f32[8,128,128]{2,1,0:T(8,128)S(1)}, f32[8,128,128]{2,1,0:T(8,128)S(1)}) fusion(f32[8,128,128]{2,1,0:T(8,128)S(1)} %bitcast_dynamic-update-slice_fusion.7, f32[8,2,128,128]{3,2,1,0:T(8,128)} %all-to-all-done, f32[128,128]{1,0:T(8,128)S(1)} %get-tuple-element.19, f32[8,128,128]{2,1,0:T(8,128)S(1)} %get-tuple-element.28, ...), kind=kLoop, calls=%fused_computation.27 | loop fusion | flops 49152 | bytes 458752 | tf_op jit(solution)/shard_map/stack | solution.py:228
  49.3 1.1 %pad_maximum_fusion = f32[8,2,128,128]{3,2,1,0:T(8,128)} fusion(f32[8,1,128,128]{3,2,1,0:T(8,128)S(1)} %bitcast.140, f32[8,1,128,128]{3,2,1,0:T(8,128)S(1)} %bitcast.141), kind=kLoop, calls=%fused_computation | loop fusion | flops 262144 | bytes 2097152 | tf_op jit(solution)/shard_map/stack | solution.py:228
  50.4 4.2 %all-to-all-start.1 = ((f32[8,2,128,128]{3,2,1,0:T(8,128)}), f32[8,2,128,128]{3,2,1,0:T(8,128)}, u32[]{:S(2)}, u32[]{:S(2)}) async-start(f32[8,2,128,128]{3,2,1,0:T(8,128)} %pad_maximum_fusion), calls=%async_computation.1 | async-start | bytes 2097152 | tf_op jit(solution)/shard_map/all_to_all | solution.py:229
  54.7 12.0 %all-to-all-done.1 = f32[8,2,128,128]{3,2,1,0:T(8,128)} async-done(((f32[8,2,128,128]{3,2,1,0:T(8,128)}), f32[8,2,128,128]{3,2,1,0:T(8,128)}, u32[]{:S(2)}, u32[]{:S(2)}) %all-to-all-start.1) | async-done | bytes 1048608 | tf_op jit(solution)/shard_map/all_to_all | solution.py:229
  66.7 1.9 %select_add_fusion = (f32[8,2,128,128]{3,2,1,0:T(8,128)S(1)}, f32[8,2,128,128]{3,2,1,0:T(8,128)S(1)}) fusion(f32[8,2,128,128]{3,2,1,0:T(8,128)} %all-to-all-done.1, f32[8,2,128,128]{3,2,1,0:T(8,128)} %copy-done.8, pred[2]{0:T(512)(128)(4,1)S(1)} %iota_compare_fusion, f32[8,2,128,128]{3,2,1,0:T(8,128)S(1)} %block_states.2, pred[2]{0:T(512)(128)(4,1)S(1)} %iota_compare_fusion.1), kind=kLoop, calls=%fused_computation.1 | loop fusion | flops 1048576 | bytes 5242884 | tf_op jit(solution)/shard_map/add | solution.py:235
  68.7 2.4 %local_scores.1 = (bf16[16,2,128,128]{3,2,1,0:T(8,128)(2,1)S(1)}, bf16[16,4,128,128]{3,2,1,0:T(8,128)(2,1)S(1)}) custom-call(bf16[128,2048]{1,0:T(8,128)(2,1)S(1)} %copy-done.5, bf16[128,2048]{1,0:T(8,128)(2,1)S(1)} %copy-done.7, bf16[128,2048]{1,0:T(8,128)(2,1)S(1)} %copy-done.1, bf16[128,2048]{1,0:T(8,128)(2,1)S(1)} %copy-done.3, ...), custom_call_target="tpu_custom_call" | custom-call | flops 268435456 | bytes 5242880 | tf_op jit(solution)/shard_map/local_scores/pallas_call | solution.py:101
  71.1 2.1 %block_outputs.2 = (bf16[128,2048]{1,0:T(8,128)(2,1)}, bf16[128,2048]{1,0:T(8,128)(2,1)}, bf16[128,2048]{1,0:T(8,128)(2,1)}, bf16[128,2048]{1,0:T(8,128)(2,1)}) custom-call(s32[1]{0:T(128)} %bitcast.1.half_ref, f32[8,2,128,128]{3,2,1,0:T(8,128)S(1)} %get-tuple-element.32.st_ref, bf16[16,2,128,128]{3,2,1,0:T(8,128)(2,1)S(1)} %get-tuple-element.10.rot_ref, ...), custom_call_target="tpu_custom_call" | custom-call | flops 268435456 | bytes 3145728 | tf_op jit(solution)/shard_map/block_outputs/pallas_call | solution.py:149
  73.2 2.0 %block_outputs.3 = (bf16[128,2048]{1,0:T(8,128)(2,1)}, bf16[128,2048]{1,0:T(8,128)(2,1)}, bf16[128,2048]{1,0:T(8,128)(2,1)}, bf16[128,2048]{1,0:T(8,128)(2,1)}) custom-call(s32[1]{0:T(128)} %bitcast.half_ref, f32[8,2,128,128]{3,2,1,0:T(8,128)S(1)} %collective-permute-done.2.st_ref, ...), custom_call_target="tpu_custom_call", output_to_operand_aliasing={{0}: (8, {}), {1}: (9, {}), {2}: (10, {}), {3}: (11, {})} | custom-call | flops 268435456 | bytes 3145728 | tf_op jit(solution)/shard_map/block_outputs/pallas_call | solution.py:149
  (34 shorter events, 7.5 us)
Async XLA Ops:
  2.4 1.0 %copy-start = (bf16[128,2048]{1,0:T(8,128)(2,1)S(1)}, bf16[128,2048]{1,0:T(8,128)(2,1)}, u32[]{:S(2)}) copy-start(bf16[128,2048]{1,0:T(8,128)(2,1)} %v_ref.9) | copy-start | bytes 1572868
  3.4 1.0 %copy-start.2 = (bf16[128,2048]{1,0:T(8,128)(2,1)S(1)}, bf16[128,2048]{1,0:T(8,128)(2,1)}, u32[]{:S(2)}) copy-start(bf16[128,2048]{1,0:T(8,128)(2,1)} %g_ref.9) | copy-start | bytes 1572868
  4.4 1.0 %copy-start.4 = (bf16[128,2048]{1,0:T(8,128)(2,1)S(1)}, bf16[128,2048]{1,0:T(8,128)(2,1)}, u32[]{:S(2)}) copy-start(bf16[128,2048]{1,0:T(8,128)(2,1)} %q_ref.5) | copy-start | bytes 1572868
  5.5 1.0 %copy-start.6 = (bf16[128,2048]{1,0:T(8,128)(2,1)S(1)}, bf16[128,2048]{1,0:T(8,128)(2,1)}, u32[]{:S(2)}) copy-start(bf16[128,2048]{1,0:T(8,128)(2,1)} %k_ref.5) | copy-start | bytes 1572868
  6.5 1.4 %copy-start.1 = (bf16[128,2048]{1,0:T(8,128)(2,1)S(1)}, bf16[128,2048]{1,0:T(8,128)(2,1)}, u32[]{:S(2)}) copy-start(bf16[128,2048]{1,0:T(8,128)(2,1)} %v_ref.9) | copy-start | bytes 1572868
  6.5 1.4 %copy-start.5 = (bf16[128,2048]{1,0:T(8,128)(2,1)S(1)}, bf16[128,2048]{1,0:T(8,128)(2,1)}, u32[]{:S(2)}) copy-start(bf16[128,2048]{1,0:T(8,128)(2,1)} %q_ref.5) | copy-start | bytes 1572868
  7.4 2.8 %collective-permute-start = (f32[8,2,128,128]{3,2,1,0:T(8,128)S(1)}, f32[8,2,128,128]{3,2,1,0:T(8,128)S(1)}, u32[]{:S(2)}, u32[]{:S(2)}) collective-permute-start(f32[8,2,128,128]{3,2,1,0:T(8,128)S(1)} %block_states.3), channel_id=1, source_target_pairs={{0,8},{8,0},{1,9},{9,1},{2,10},{10,2},{3,11},{11,3},{4,12},{12,4},... | collective-permute-start | bytes 3145736 | tf_op jit(solution)/shard_map/ppermute | solution.py:180
  10.2 1.0 %copy-start.8 = (f32[8,2,128,128]{3,2,1,0:T(8,128)}, f32[8,2,128,128]{3,2,1,0:T(8,128)S(1)}, u32[]{:S(2)}) copy-start(f32[8,2,128,128]{3,2,1,0:T(8,128)S(1)} %collective-permute-done) | copy-start | bytes 3145732
  12.3 21.1 %all-to-all-start = ((f32[8,2,128,128]{3,2,1,0:T(8,128)}), f32[8,2,128,128]{3,2,1,0:T(8,128)}, u32[]{:S(2)}, u32[]{:S(2)}) async-start(f32[8,2,128,128]{3,2,1,0:T(8,128)} %add.51), calls=%async_computation | async-start | bytes 2097152 | tf_op jit(solution)/shard_map/all_to_all | solution.py:204
  34.7 6.5 %collective-permute-start.1 = (f32[128,128]{1,0:T(8,128)S(1)}, f32[128,128]{1,0:T(8,128)S(1)}, u32[]{:S(2)}, u32[]{:S(2)}) collective-permute-start(f32[128,128]{1,0:T(8,128)S(1)} %broadcast_select_fusion), channel_id=1, source_target_pairs={{0,4},{4,0},{1,5},{5,1},{2,6},{6,2},{3,7},{7,3},{8,12},{12,8},{9,1... | collective-permute-start | bytes 196616 | tf_op jit(solution)/shard_map/ppermute | solution.py:180
  50.4 16.3 %all-to-all-start.1 = ((f32[8,2,128,128]{3,2,1,0:T(8,128)}), f32[8,2,128,128]{3,2,1,0:T(8,128)}, u32[]{:S(2)}, u32[]{:S(2)}) async-start(f32[8,2,128,128]{3,2,1,0:T(8,128)} %pad_maximum_fusion), calls=%async_computation.1 | async-start | bytes 2097152 | tf_op jit(solution)/shard_map/all_to_all | solution.py:229
  54.7 14.0 %copy-start.3 = (bf16[128,2048]{1,0:T(8,128)(2,1)S(1)}, bf16[128,2048]{1,0:T(8,128)(2,1)}, u32[]{:S(2)}) copy-start(bf16[128,2048]{1,0:T(8,128)(2,1)} %g_ref.9) | copy-start | bytes 1572868
  54.7 14.0 %copy-start.7 = (bf16[128,2048]{1,0:T(8,128)(2,1)S(1)}, bf16[128,2048]{1,0:T(8,128)(2,1)}, u32[]{:S(2)}) copy-start(bf16[128,2048]{1,0:T(8,128)(2,1)} %k_ref.5) | copy-start | bytes 1572868
  68.6 4.6 %collective-permute-start.2 = (f32[8,2,128,128]{3,2,1,0:T(8,128)S(1)}, f32[8,2,128,128]{3,2,1,0:T(8,128)S(1)}, u32[]{:S(2)}, u32[]{:S(2)}) collective-permute-start(f32[8,2,128,128]{3,2,1,0:T(8,128)S(1)} %get-tuple-element.33), channel_id=1, source_target_pairs={{0,8},{8,0},{1,9},{9,1},{2,10},{10,2},{3,11},{11,3},{4,12},{12,4},... | collective-permute-start | bytes 3145736 | tf_op jit(solution)/shard_map/ppermute | solution.py:180

commit v2 on v1

v2 whole, which is shorter than its diff:
```python
import functools
import math

import jax
import jax.numpy as jnp
from jax import lax
from jax.experimental import pallas as pl
from jax.experimental.pallas import tpu as pltpu
from jax.sharding import Mesh, PartitionSpec as P

D = 128
F32 = jnp.float32
BF16 = jnp.bfloat16
VMEM_LIMIT = 20 * 1024 * 1024
GROUP = ("zl", "y", "x")
CHUNKS = 1
HBM = pl.BlockSpec(memory_space=pltpu.HBM)
VMEM = pl.BlockSpec(memory_space=pltpu.VMEM)
SMEM = pl.BlockSpec(memory_space=pltpu.SMEM)


def in_hbm(shape):
    return pltpu.HBM(shape, F32)


def in_vmem(shape, dtype=F32):
    return pltpu.VMEM(shape, dtype)


def call(body, out_shape, in_specs, out_specs, scratch, flops, moved, name):
    return pl.pallas_call(
        body,
        out_shape=out_shape,
        in_specs=in_specs,
        out_specs=out_specs,
        scratch_shapes=scratch,
        compiler_params=pltpu.CompilerParams(vmem_limit_bytes=VMEM_LIMIT),
        cost_estimate=pl.CostEstimate(flops=flops, bytes_accessed=moved, transcendentals=0),
        name=name,
    )


def rotate(rows, cosine, sine):
    wide = rows.astype(F32)
    return wide * cosine + pltpu.roll(wide, D // 2, 1) * sine


def unrotate(rows, cosine, sine):
    return rows * cosine - pltpu.roll(rows, D // 2, 1) * sine


def dot(a, b, ca, cb):
    return lax.dot_general(a, b, (((ca,), (cb,)), ((), ())), preferred_element_type=F32)


def rotary_tables(positions):
    rows = positions.shape[1]
    half = D // 2
    lane = lax.broadcasted_iota(jnp.int32, (rows, D), 1)
    index = jnp.where(lane < half, lane, lane - half).astype(F32)
    frequency = jnp.exp(index * (-2.0 * math.log(500000.0) / D))
    place = jnp.broadcast_to(positions.astype(F32), (D, rows)).T
    angle = place * frequency
    sine = jnp.sin(angle)
    return jnp.cos(angle), jnp.where(lane < half, -sine, sine)


def states_body(first, chunk, heads, *refs):
    if first:
        half, pos, q, k, v, g, cos_ref, sin_ref, out_ref, qs, ks, vs, gs, sems = refs
    else:
        half, cos_ref, sin_ref, q, k, v, g, out_ref, qs, ks, vs, gs, sems = refs
    part = q.shape[1] // D // 2
    start = pl.multiple_of((half[0] * part + chunk * heads) * D, heads * D)
    copies = []
    for i, (src, dst) in enumerate(((k, ks), (v, vs), (q, qs), (g, gs))):
        copies.append(pltpu.make_async_copy(src.at[:, pl.ds(start, heads * D)], dst, sems.at[i]))
    for copy in copies:
        copy.start()
    if first:
        cosine, sine = rotary_tables(pos[...])
        cos_ref[...] = cosine
        sin_ref[...] = sine
    else:
        cosine, sine = cos_ref[...], sin_ref[...]
    per, cut = out_ref.shape[0] // heads, out_ref.shape[2]
    for side, (rows, others) in enumerate(((ks, vs), (qs, gs))):
        copies[2 * side].wait()
        copies[2 * side + 1].wait()
        for h in range(heads):
            cols = slice(h * D, (h + 1) * D)
            turned = rotate(rows[:, cols], cosine, sine).astype(BF16)
            state = dot(turned, others[:, cols], 0, 0)
            for i in range(per):
                out_ref[h * per + i, side] = state[i * cut : (i + 1) * cut]


def states(half, chunk, heads, members, q, k, v, g, tables, pos):
    rows = q.shape[0]
    cut = heads * D // members
    first = tables is None
    table = in_vmem((rows, D))
    result = in_vmem((members, 2, cut, D))
    body = functools.partial(states_body, first, chunk, heads)
    scratch = [pltpu.VMEM((rows, heads * D), BF16)] * 4 + [pltpu.SemaphoreType.DMA((4,))]
    work = (4 * heads * rows * D * D, heads * D * (8 * rows + 8 * D))
    if first:
        return call(body, [table, table, result], [SMEM, VMEM] + [HBM] * 4, [VMEM] * 3, scratch, *work, "block_states")(
            half, pos, q, k, v, g
        )
    return call(body, result, [SMEM, VMEM, VMEM] + [HBM] * 4, VMEM, scratch, *work, "block_states")(
        half, *tables, q, k, v, g
    )


def add_body(core, a_ref, b_ref, out_ref, kept_ref, give_ref, held, sems):
    last = held.shape[0]
    copies = [
        pltpu.make_async_copy(b_ref.at[:, 1 - core[0]], kept_ref, sems.at[last]),
        pltpu.make_async_copy(a_ref.at[:, core[0]], give_ref, sems.at[last + 1]),
    ]
    for j in range(held.shape[0]):
        held[j] = a_ref[j] + b_ref[j]
        copy = pltpu.make_async_copy(held.at[j], out_ref.at[j], sems.at[j])
        copy.start()
        copies.append(copy)
    copies[0].start()
    copies[1].start()
    for copy in copies:
        copy.wait()


def add(core, a, b):
    size = math.prod(a.shape)
    one_side = in_hbm(a.shape[:1] + a.shape[2:])
    return call(
        add_body, [in_hbm(a.shape), one_side, one_side], [SMEM, VMEM, VMEM], [HBM] * 3,
        [pltpu.VMEM(a.shape, F32), pltpu.SemaphoreType.DMA((a.shape[0] + 2,))], size, size * 12, "chip_sum",
    )(core, a, b)


def scan_body(group, held_ref, out_ref, send_ref, held, sems):
    members = held.shape[0]
    copies = [pltpu.make_async_copy(held_ref.at[j], held.at[j], sems.at[j]) for j in range(members)]
    for copy in copies:
        copy.start()
    total = jnp.zeros(held.shape[2:], F32)
    for j in range(members):
        copies[j].wait()
        out_ref[j, 0] = total
        total = total + held[j, 0]
    keys = total
    total = jnp.zeros(held.shape[2:], F32)
    for j in reversed(range(members)):
        out_ref[j, 1] = total
        total = total + held[j, 1]
    if send_ref.shape[0] == 1:
        send_ref[0] = jnp.where(group[0] == 0, keys, total)
    else:
        send_ref[0] = keys
        send_ref[1] = total


def scan(group, held, kinds):
    size = math.prod(held.shape)
    return call(
        scan_body, [in_vmem(held.shape), in_vmem((kinds,) + held.shape[2:])], [SMEM, HBM], [VMEM, VMEM],
        [pltpu.VMEM(held.shape, F32), pltpu.SemaphoreType.DMA((held.shape[0],))], size, size * 8, "chip_scan",
    )(group, held)


def offset_body(sums_ref, passed_ref, out_ref, held, sems):
    copies = []
    for j in range(held.shape[0]):
        held[j] = sums_ref[j] + passed_ref[...]
        copy = pltpu.make_async_copy(held.at[j], out_ref.at[j], sems.at[j])
        copy.start()
        copies.append(copy)
    for copy in copies:
        copy.wait()


def offset(sums, passed):
    size = math.prod(sums.shape)
    return call(
        offset_body, in_hbm(sums.shape), [VMEM, VMEM], HBM,
        [pltpu.VMEM(sums.shape, F32), pltpu.SemaphoreType.DMA((sums.shape[0],))], size, size * 8, "group_sum",
    )(sums, passed)


def local_kernel(q_ref, k_ref, v_ref, g_ref, cos_ref, sin_ref, rot_ref, sc_ref):
    cosine, sine = cos_ref[...], sin_ref[...]
    rows = q_ref.shape[0]
    row = lax.broadcasted_iota(jnp.int32, (rows, rows), 0)
    col = lax.broadcasted_iota(jnp.int32, (rows, rows), 1)
    for h in range(rot_ref.shape[0]):
        cols = slice(h * D, (h + 1) * D)
        krot = rotate(k_ref[:, cols], cosine, sine).astype(BF16)
        qrot = rotate(q_ref[:, cols], cosine, sine).astype(BF16)
        v, g = v_ref[:, cols], g_ref[:, cols]
        rot_ref[h, 0] = qrot
        rot_ref[h, 1] = krot
        sc_ref[h, 0] = jnp.where(row >= col, dot(qrot, krot, 1, 1), 0.0).astype(BF16)
        sc_ref[h, 1] = jnp.where(row >= col, dot(g, v, 1, 1), 0.0).astype(BF16)
        sc_ref[h, 2] = jnp.where(row <= col, dot(krot, qrot, 1, 1), 0.0).astype(BF16)
        sc_ref[h, 3] = jnp.where(row <= col, dot(v, g, 1, 1), 0.0).astype(BF16)


def local_scores(q, k, v, g, cosine, sine, heads):
    rows = q.shape[0]
    per = 4
    wide = pl.BlockSpec((rows, per * D), lambda i: (0, i))
    table = pl.BlockSpec((rows, D), lambda i: (0, 0))
    return pl.pallas_call(
        local_kernel,
        grid=(heads // per,),
        in_specs=[wide] * 4 + [table] * 2,
        out_specs=[
            pl.BlockSpec((per, 2, rows, D), lambda i: (i, 0, 0, 0)),
            pl.BlockSpec((per, 4, rows, rows), lambda i: (i, 0, 0, 0)),
        ],
        out_shape=[
            jax.ShapeDtypeStruct((heads, 2, rows, D), BF16),
            jax.ShapeDtypeStruct((heads, 4, rows, rows), BF16),
        ],
        compiler_params=pltpu.CompilerParams(vmem_limit_bytes=VMEM_LIMIT),
        cost_estimate=pl.CostEstimate(
            flops=8 * heads * rows * D * D, bytes_accessed=10 * rows * heads * D * 2, transcendentals=0
        ),
        name="local_scores",
    )(q, k, v, g, cosine, sine)


def outputs_kernel(scale, prior, where, st_ref, ex_ref, rot_ref, sc_ref, v_ref, g_ref, cos_ref, sin_ref, *refs):
    att_ref, qg_ref, kg_ref, vg_ref = refs[prior:]
    cosine, sine = cos_ref[...], sin_ref[...]
    heads = rot_ref.shape[0]
    per, cut = st_ref.shape[0] // heads, st_ref.shape[2]
    for h in range(heads):
        cols = slice(h * D, (h + 1) * D)
        v, g = v_ref[:, cols], g_ref[:, cols]
        qrot, krot = rot_ref[h, 0], rot_ref[h, 1]

        def state(side):
            whole = st_ref[h * per : (h + 1) * per, side].reshape(D, D)
            extra = ex_ref[h * per : (h + 1) * per].reshape(D, D)
            return (whole + jnp.where(where[1] == side, extra, 0.0)).astype(BF16)

        before, after = state(0), state(1)
        att = dot(sc_ref[h, 0], v, 1, 0) + dot(qrot, before, 1, 0)
        rqg = dot(sc_ref[h, 1], krot, 1, 0) + dot(g, before, 1, 1)
        rkg = dot(sc_ref[h, 3], qrot, 1, 0) + dot(v, after, 1, 1)
        vg = dot(sc_ref[h, 2], g, 1, 0) + dot(krot, after, 1, 0)
        att_ref[:, cols] = (scale * att).astype(BF16)
        qg_ref[:, cols] = unrotate(scale * rqg, cosine, sine).astype(BF16)
        kg_ref[:, cols] = unrotate(scale * rkg, cosine, sine).astype(BF16)
        vg_ref[:, cols] = (scale * vg).astype(BF16)


def outputs(scale, where, chunk, chunks, st, extra, rot, sc, v, g, tables, prior):
    rows, width = v.shape
    heads = width // D // 2 // chunks
    steps = 2
    per = heads // steps
    cut = st.shape[0] // steps
    base = lambda i, where: (where[0] * chunks + chunk) * steps + i
    wide = pl.BlockSpec((rows, per * D), lambda i, where: (0, base(i, where)))
    table = pl.BlockSpec((rows, D), lambda i, where: (0, 0))
    by_head = lambda i, where: (base(i, where), 0, 0, 0)
    return pl.pallas_call(
        functools.partial(outputs_kernel, scale, len(prior)),
        grid_spec=pltpu.PrefetchScalarGridSpec(
            num_scalar_prefetch=1,
            grid=(steps,),
            in_specs=[
                pl.BlockSpec((cut,) + st.shape[1:], lambda i, where: (i, 0, 0, 0)),
                pl.BlockSpec((cut,) + extra.shape[1:], lambda i, where: (i, 0, 0)),
                pl.BlockSpec((per, 2, rows, D), by_head),
                pl.BlockSpec((per, 4, rows, rows), by_head),
                wide,
                wide,
                table,
                table,
            ]
            + [pl.BlockSpec(memory_space=pl.ANY)] * len(prior),
            out_specs=[wide] * 4,
        ),
        out_shape=[jax.ShapeDtypeStruct((rows, width), BF16)] * 4,
        input_output_aliases={9 + i: i for i in range(len(prior))},
        compiler_params=pltpu.CompilerParams(vmem_limit_bytes=VMEM_LIMIT),
        cost_estimate=pl.CostEstimate(
            flops=16 * heads * rows * D * D, bytes_accessed=12 * rows * heads * D * 2, transcendentals=0
        ),
        name="block_outputs",
    )(where, st, extra, rot, sc, v, g, *tables, *prior)


def swap(value, axis):
    return lax.ppermute(value, axis, [(0, 1), (1, 0)])


def shards(q, k, v, g, positions):
    rows, width = q.shape
    heads = width // D
    part = heads // 2 // CHUNKS
    tokens = rows
    for axis in ("x", "core", "zh", "zl", "y"):
        tokens = tokens * lax.axis_size(axis)
    scale = (D * tokens) ** (-0.5)
    core, group = lax.axis_index("core"), lax.axis_index("zh")
    members, groups = lax.axis_size(GROUP), lax.axis_size("zh")
    mine, theirs = core.reshape(1), (1 - core).reshape(1)
    pos = positions.reshape(1, rows)
    chunks = range(CHUNKS)

    hq, hk, hv, hg = (pltpu.with_memory_space_constraint(a, pltpu.HBM) for a in (q, k, v, g))
    tables, far, near = None, [], []
    for c in chunks:
        made = states(theirs, c, part, members, hq, hk, hv, hg, tables, pos)
        if c == 0:
            tables, made = made[:2], made[2]
        far.append(made)
    near_other = [swap(value, "core") for value in far]
    for c in chunks:
        near.append(states(mine, c, part, members, hq, hk, hv, hg, tables, pos))
    chip, kept, give = zip(*(add(mine, near[c], near_other[c]) for c in chunks))
    chip, give, early = lax.optimization_barrier((chip, give, tables))
    held = [lax.all_to_all(chip[c], GROUP, 0, 0, tiled=True) for c in chunks]
    extra = [swap(give[c], "core") for c in chunks]
    rot, sc = local_scores(q, k, v, g, *early, heads)
    held, extra, rot, sc = lax.optimization_barrier((held, extra, rot, sc))

    back = []
    for c in chunks:
        sums, send = scan(group.reshape(1), held[c], 1 if groups == 2 else 2)
        side = jnp.arange(2)[:, None, None]
        if groups == 2:
            passed = jnp.where(side == 1 - group, swap(send, "zh"), 0.0)
        else:
            every = lax.all_gather(send, "zh")
            order = jnp.arange(groups)[:, None, None, None]
            wanted = jnp.where(side == 0, order < group, order > group)
            passed = jnp.sum(jnp.where(wanted, every, 0.0), axis=0)
        back.append(offset(sums, passed))
    whole = [lax.all_to_all(back[c], GROUP, 0, 0, tiled=True) for c in chunks]
    far_state = [swap(value, "core") for value in whole]

    slot = 1 - core
    made = ()
    for c in chunks:
        made = outputs(
            scale, jnp.stack([core, slot]), c, CHUNKS, whole[c], kept[c], rot, sc, v, g, tables, tuple(made)
        )
    for c in chunks:
        made = outputs(
            scale, jnp.stack([1 - core, slot]), c, CHUNKS, far_state[c], extra[c], rot, sc, v, g, tables, tuple(made)
        )
    return tuple(made)


def solution(mesh):
    inner, outer = mesh.shape["inner"], mesh.shape["outer"]
    x = inner // 2
    y = x if outer % x == 0 else 1
    z = outer // y
    zl = 2 if z % 2 == 0 else 1
    whole = Mesh(mesh.devices.reshape(x, 2, z // zl, zl, y), ("x", "core", "zh", "zl", "y"))
    rows = ("zh", "zl", "y", "x", "core")
    return jax.shard_map(
        shards,
        mesh=whole,
        in_specs=(P(rows, None),) * 4 + (P(rows),),
        out_specs=(P(rows, None),) * 4,
        check_vma=False,
    )
```

time: 76.4 us -> 61 us (0.80)
  waiting for transfers between devices: 32.2 us -> 13.8 us
  blocking collectives: 0 us -> 16.7 us
  other arithmetic: 15.2 us -> 0.23 us
  Pallas kernels: 8.29 us -> 15.9 us
  starting transfers between devices: 13.6 us -> 9.29 us
  local copies, waits for them, and re-layouts: 5.17 us -> 3.72 us
    all_to_all x2 -> x1, waiting for transfers between devices: 27 us -> 9.47 us  [shards(): held = [lax.all_to_all(chip[c], GROUP, 0, 0, tiled=True) for c in chunks]]
    all_to_all x0 -> x1, blocking collectives: none -> 16.7 us  [shards(): whole = [lax.all_to_all(back[c], GROUP, 0, 0, tiled=True) for c in chunks]]
    unnamed x9 -> x0, other arithmetic: 7.16 us -> none
    pallas_call x2 -> x5, Pallas kernels: 1.79 us -> 7.43 us  [the longest x1 1.77 us: states(): call(body, [table, table, result], [SMEM, VMEM] + [HBM] * 4, [VMEM] * 3,...]
    all_to_all x2 -> x1, starting transfers between devices: 10.4 us -> 6.12 us  [shards(): held = [lax.all_to_all(chip[c], GROUP, 0, 0, tiled=True) for c in chunks]]
    add x2 -> x0, other arithmetic: 2.99 us -> none  [the longest x1 1.88 us: shards(): to_mine = chip_state + jnp.where(side == 1 - core, near_other, 0.0)]
    pallas_call x2, Pallas kernels: 4.11 us -> 6.09 us  [outputs(): pl.pallas_call(functools.partial(outputs_kernel, scale, len(prior)), grid...]
    another operation x3 -> x2, other arithmetic: 2 us -> 0.15 us  [the longest x1 0.07 us: shards(): jnp.stack([1 - core, slot])]
  transfers between devices with their start and end apart: 5 -> 5, of which waited for: 4 -> 3; matrix products, arithmetic and copies ran while one was open for 0% -> 0% of each run, Pallas kernels for 7% -> 11%
where the time goes in v2:
time: 61 us; the launch traced here: 60.4 us
  blocking collectives  16.7 us (27%)
  Pallas kernels  15.9 us (26%)
  waiting for transfers between devices  13.8 us (23%)
  starting transfers between devices  9.29 us (15%)
  local copies, waits for them, and re-layouts  3.72 us (6%)
  between operations  0.78 us (1%)
    all_to_all x1, blocking collectives, shards(): whole = [lax.all_to_all(back[c], GROUP, 0, 0, tiled=True) for c in chunks]  16.7 us
    all_to_all x1, waiting for transfers between devices, shards(): held = [lax.all_to_all(chip[c], GROUP, 0, 0, tiled=True) for c in chunks]  9.47 us
    all_to_all x1, starting transfers between devices, shards(): held = [lax.all_to_all(chip[c], GROUP, 0, 0, tiled=True) for c in chunks]  6.12 us
    pallas_call x2, Pallas kernels, outputs(): pl.pallas_call(functools.partial(outputs_kernel, scale, len(prior)), grid...  6.09 us
    ppermute x4, waiting for transfers between devices, swap(): return lax.ppermute(value, axis, [(0, 1), (1, 0)])  4.33 us
    unnamed x16, local copies, waits for them, and re-layouts  3.72 us
    ppermute x4, starting transfers between devices, swap(): return lax.ppermute(value, axis, [(0, 1), (1, 0)])  3.18 us
    pallas_call x1, Pallas kernels, local_scores(): pl.pallas_call(local_kernel, grid=(heads // per,), in_specs=[wide] * 4 +...  2.38 us
  transfers between devices with their start and end apart: 5, of which 3 were waited for; matrix products, arithmetic and copies ran while one was open for 0% of the time, Pallas kernels for 11%

profile of v2, /device:TPU:0, one launch (start us, length us, event | category | flops | bytes accessed | tf_op | source)
XLA Modules:
  0.0 60.4 jit_solution(18206256657173885242)
XLA Ops:
  0.6 0.6 %copy-done.7 = s32[128]{0:T(128)S(1)} copy-done((s32[128]{0:T(128)S(1)}, s32[128]{0:T(128)}, u32[]{:S(2)}) %copy-start.7) | copy-done | bytes 536
  1.3 1.8 %block_states.2 = (f32[128,128]{1,0:T(8,128)S(1)}, f32[128,128]{1,0:T(8,128)S(1)}, f32[8,2,128,128]{3,2,1,0:T(8,128)S(1)}) custom-call(s32[1]{0:T(128)} %bitcast.refs_0_, s32[1,128]{1,0:T(1,128)S(1)} %bitcast.5, bf16[128,2048]{1,0:T(8,128)(2,1)} %q_ref.1, bf16[128,2048]{1,0:T(8,128)(2,1)} %k_ref.1, bf16[128,2048]{1,0:T(8,128)(2,1)} %v_ref.5, ...), custom_call_target="tpu_custom_call" | custom-call | flops 67108864 | bytes 2097152 | tf_op jit(solution)/shard_map/block_states/pallas_call | solution.py:108
  3.1 0.5 collective-permute-start
  3.6 1.8 %block_states.3.a_ref = f32[8,2,128,128]{3,2,1,0:T(8,128)S(1)} custom-call(s32[1]{0:T(128)} %bitcast.2.refs_0_.core, f32[128,128]{1,0:T(8,128)S(1)} %get-tuple-element.33.refs_1_.cos_ref, f32[128,128]{1,0:T(8,128)S(1)} %get-tuple-element.34.refs_2_.sin_ref, bf16[128,2048]{1,0:T(8,128)(2,1)} %q_ref.1, bf16[128,2048]{1,0:T(8,128)(2,1)} %k_ref.1, ...), custom_call_target="tpu_custom_call" | custom-call | flops 67108864 | bytes 2097152 | tf_op jit(solution)/shard_map/block_states/pallas_call | solution.py:111
  5.4 0.0 copy-start
  5.4 0.0 copy-start.1
  5.4 0.5 collective-permute-done.b_ref
  5.9 1.4 %chip_sum.1 = (f32[8,2,128,128]{3,2,1,0:T(8,128)}, f32[8,128,128]{2,1,0:T(8,128)}, f32[8,128,128]{2,1,0:T(8,128)}) custom-call(s32[1]{0:T(128)} %bitcast.2.refs_0_.core, f32[8,2,128,128]{3,2,1,0:T(8,128)S(1)} %block_states.3.a_ref, f32[8,2,128,128]{3,2,1,0:T(8,128)S(1)} %collective-permute-done.b_ref), custom_call_target="tpu_custom_call" | custom-call | flops 262144 | bytes 3145728 | tf_op jit(solution)/shard_map/chip_sum/pallas_call | solution.py:136
  7.3 6.1 %all-to-all-start = ((f32[8,2,128,128]{3,2,1,0:T(8,128)}), f32[8,2,128,128]{3,2,1,0:T(8,128)}, u32[]{:S(2)}, u32[]{:S(2)}) async-start(f32[8,2,128,128]{3,2,1,0:T(8,128)} %get-tuple-element.31), calls=%async_computation | async-start | bytes 2097152 | tf_op jit(solution)/shard_map/all_to_all | solution.py:328
  13.5 1.0 %copy-done.2 = bf16[128,2048]{1,0:T(8,128)(2,1)S(1)} copy-done((bf16[128,2048]{1,0:T(8,128)(2,1)S(1)}, bf16[128,2048]{1,0:T(8,128)(2,1)}, u32[]{:S(2)}) %copy-start.2) | copy-done | bytes 524312
  14.5 1.0 %copy-done.3 = bf16[128,2048]{1,0:T(8,128)(2,1)S(1)} copy-done((bf16[128,2048]{1,0:T(8,128)(2,1)S(1)}, bf16[128,2048]{1,0:T(8,128)(2,1)}, u32[]{:S(2)}) %copy-start.3) | copy-done | bytes 524312
  15.5 2.4 %local_scores.1 = (bf16[16,2,128,128]{3,2,1,0:T(8,128)(2,1)S(1)}, bf16[16,4,128,128]{3,2,1,0:T(8,128)(2,1)S(1)}) custom-call(bf16[128,2048]{1,0:T(8,128)(2,1)S(1)} %copy-done.2, bf16[128,2048]{1,0:T(8,128)(2,1)S(1)} %copy-done.3, bf16[128,2048]{1,0:T(8,128)(2,1)S(1)} %copy-done, bf16[128,2048]{1,0:T(8,128)(2,1)S(1)} %copy-done.1, ...), custom_call_target="tpu_custom_call" | custom-call | flops 268435456 | bytes 5242880 | tf_op jit(solution)/shard_map/local_scores/pallas_call | solution.py:214
  17.9 1.0 %copy-done.4 = bf16[16,2,128,128]{3,2,1,0:T(8,128)(2,1)} copy-done((bf16[16,2,128,128]{3,2,1,0:T(8,128)(2,1)}, bf16[16,2,128,128]{3,2,1,0:T(8,128)(2,1)S(1)}, u32[]{:S(2)}) %copy-start.4) | copy-done | bytes 1048600
  18.9 9.5 %all-to-all-done.held_ref = f32[8,2,128,128]{3,2,1,0:T(8,128)} async-done(((f32[8,2,128,128]{3,2,1,0:T(8,128)}), f32[8,2,128,128]{3,2,1,0:T(8,128)}, u32[]{:S(2)}, u32[]{:S(2)}) %all-to-all-start) | async-done | bytes 1048608 | tf_op jit(solution)/shard_map/all_to_all | solution.py:328
  28.4 1.4 %chip_scan.1 = (f32[8,2,128,128]{3,2,1,0:T(8,128)S(1)}, f32[1,128,128]{2,1,0:T(8,128)S(1)}) custom-call(s32[1]{0:T(128)} %bitcast.1.group, f32[8,2,128,128]{3,2,1,0:T(8,128)} %all-to-all-done.held_ref), custom_call_target="tpu_custom_call" | custom-call | flops 262144 | bytes 2097152 | tf_op jit(solution)/shard_map/chip_scan/pallas_call | solution.py:166
  29.8 2.7 %collective-permute-start.2 = (f32[1,128,128]{2,1,0:T(8,128)S(1)}, f32[1,128,128]{2,1,0:T(8,128)S(1)}, u32[]{:S(2)}, u32[]{:S(2)}) collective-permute-start(f32[1,128,128]{2,1,0:T(8,128)S(1)} %get-tuple-element.39), channel_id=1, source_target_pairs={{0,4},{4,0},{1,5},{5,1},{2,6},{6,2},{3,7},{7,3},{8,12},{12,8},{9,1... | collective-permute-start | bytes 196616 | tf_op jit(solution)/shard_map/ppermute | solution.py:299
  32.5 3.8 %collective-permute-done.2 = f32[1,128,128]{2,1,0:T(8,128)S(1)} collective-permute-done((f32[1,128,128]{2,1,0:T(8,128)S(1)}, f32[1,128,128]{2,1,0:T(8,128)S(1)}, u32[]{:S(2)}, u32[]{:S(2)}) %collective-permute-start.2) | collective-permute-done | bytes 65568 | tf_op jit(solution)/shard_map/ppermute | solution.py:299
  36.3 0.1 broadcast_select_fusion.passed_ref
  36.4 1.1 %group_sum.1 = f32[8,2,128,128]{3,2,1,0:T(8,128)} custom-call(f32[8,2,128,128]{3,2,1,0:T(8,128)S(1)} %get-tuple-element.38.sums_ref, f32[2,128,128]{2,1,0:T(8,128)S(1)} %broadcast_select_fusion.passed_ref), custom_call_target="tpu_custom_call" | custom-call | flops 262144 | bytes 2097152 | tf_op jit(solution)/shard_map/group_sum/pallas_call | solution.py:185
  37.5 16.7 %all_to_all.10.st_ref = f32[8,2,128,128]{3,2,1,0:T(8,128)S(1)} all-to-all(f32[8,2,128,128]{3,2,1,0:T(8,128)} %group_sum.1), channel_id=1, replica_groups=mesh['x'=2,'core'=2,'zh'=2,'zl'=2,'y'=2] {'zl','y','x'}, dimensions={0} | all-to-all | bytes 2097152 | tf_op jit(solution)/shard_map/all_to_all | solution.py:345
  54.2 0.1 pad_add_fusion.where
  54.2 0.1 pad_add_fusion.1.where
  54.3 2.6 %block_outputs.2 = (bf16[128,2048]{1,0:T(8,128)(2,1)}, bf16[128,2048]{1,0:T(8,128)(2,1)}, bf16[128,2048]{1,0:T(8,128)(2,1)}, bf16[128,2048]{1,0:T(8,128)(2,1)}) custom-call(s32[2]{0:T(128)S(1)} %pad_add_fusion.1.where, f32[8,2,128,128]{3,2,1,0:T(8,128)S(1)} %all_to_all.10.st_ref, f32[8,128,128]{2,1,0:T(8,128)S(1)} %copy-done.6, ...), custom_call_target="tpu_custom_call" | custom-call | flops 268435456 | bytes 3145728 | tf_op jit(solution)/shard_map/block_outputs/pallas_call | solution.py:270
  57.0 3.5 %block_outputs.3 = (bf16[128,2048]{1,0:T(8,128)(2,1)}, bf16[128,2048]{1,0:T(8,128)(2,1)}, bf16[128,2048]{1,0:T(8,128)(2,1)}, bf16[128,2048]{1,0:T(8,128)(2,1)}) custom-call(s32[2]{0:T(128)S(1)} %pad_add_fusion.where, ...), custom_call_target="tpu_custom_call", output_to_operand_aliasing={{0}: (9, {}), {1}: (10, {}), {2}: (11, {}), {3}: (12, {})} | custom-call | flops 268435456 | bytes 3145728 | tf_op jit(solution)/shard_map/block_outputs/pallas_call | solution.py:270
  (15 shorter events, 0.0 us)
Async XLA Ops:
  0.6 0.7 %copy-start.7 = (s32[128]{0:T(128)S(1)}, s32[128]{0:T(128)}, u32[]{:S(2)}) copy-start(s32[128]{0:T(128)} %param.9) | copy-start | bytes 1540
  3.1 2.8 %collective-permute-start = (f32[8,2,128,128]{3,2,1,0:T(8,128)S(1)}, f32[8,2,128,128]{3,2,1,0:T(8,128)S(1)}, u32[]{:S(2)}, u32[]{:S(2)}) collective-permute-start(f32[8,2,128,128]{3,2,1,0:T(8,128)S(1)} %get-tuple-element.28), channel_id=1, source_target_pairs={{0,8},{8,0},{1,9},{9,1},{2,10},{10,2},{3,11},{11,3},{4,12},{12,4},... | collective-permute-start | bytes 3145736 | tf_op jit(solution)/shard_map/ppermute | solution.py:299
  5.4 8.1 %copy-start = (bf16[128,2048]{1,0:T(8,128)(2,1)S(1)}, bf16[128,2048]{1,0:T(8,128)(2,1)}, u32[]{:S(2)}) copy-start(bf16[128,2048]{1,0:T(8,128)(2,1)} %v_ref.5) | copy-start | bytes 1572868
  5.4 8.1 %copy-start.1 = (bf16[128,2048]{1,0:T(8,128)(2,1)S(1)}, bf16[128,2048]{1,0:T(8,128)(2,1)}, u32[]{:S(2)}) copy-start(bf16[128,2048]{1,0:T(8,128)(2,1)} %g_ref.5) | copy-start | bytes 1572868
  7.3 21.1 %all-to-all-start = ((f32[8,2,128,128]{3,2,1,0:T(8,128)}), f32[8,2,128,128]{3,2,1,0:T(8,128)}, u32[]{:S(2)}, u32[]{:S(2)}) async-start(f32[8,2,128,128]{3,2,1,0:T(8,128)} %get-tuple-element.31), calls=%async_computation | async-start | bytes 2097152 | tf_op jit(solution)/shard_map/all_to_all | solution.py:328
  13.4 5.5 %collective-permute-start.1 = (f32[8,128,128]{2,1,0:T(8,128)}, f32[8,128,128]{2,1,0:T(8,128)}, u32[]{:S(2)}, u32[]{:S(2)}) collective-permute-start(f32[8,128,128]{2,1,0:T(8,128)} %get-tuple-element.32), channel_id=1, source_target_pairs={{0,8},{8,0},{1,9},{9,1},{2,10},{10,2},{3,11},{11,3},{4,12},{12,4},... | collective-permute-start | bytes 1572872 | tf_op jit(solution)/shard_map/ppermute | solution.py:299
  13.5 1.0 %copy-start.2 = (bf16[128,2048]{1,0:T(8,128)(2,1)S(1)}, bf16[128,2048]{1,0:T(8,128)(2,1)}, u32[]{:S(2)}) copy-start(bf16[128,2048]{1,0:T(8,128)(2,1)} %q_ref.1) | copy-start | bytes 1572868
  14.5 1.0 %copy-start.3 = (bf16[128,2048]{1,0:T(8,128)(2,1)S(1)}, bf16[128,2048]{1,0:T(8,128)(2,1)}, u32[]{:S(2)}) copy-start(bf16[128,2048]{1,0:T(8,128)(2,1)} %k_ref.1) | copy-start | bytes 1572868
  17.9 1.0 %copy-start.4 = (bf16[16,2,128,128]{3,2,1,0:T(8,128)(2,1)}, bf16[16,2,128,128]{3,2,1,0:T(8,128)(2,1)S(1)}, u32[]{:S(2)}) copy-start(bf16[16,2,128,128]{3,2,1,0:T(8,128)(2,1)S(1)} %get-tuple-element.41.rot_ref) | copy-start | bytes 3145732
  29.8 6.5 %collective-permute-start.2 = (f32[1,128,128]{2,1,0:T(8,128)S(1)}, f32[1,128,128]{2,1,0:T(8,128)S(1)}, u32[]{:S(2)}, u32[]{:S(2)}) collective-permute-start(f32[1,128,128]{2,1,0:T(8,128)S(1)} %get-tuple-element.39), channel_id=1, source_target_pairs={{0,4},{4,0},{1,5},{5,1},{2,6},{6,2},{3,7},{7,3},{8,12},{12,8},{9,1... | collective-permute-start | bytes 196616 | tf_op jit(solution)/shard_map/ppermute | solution.py:299
  36.4 18.0 %copy-start.5 = (bf16[16,2,128,128]{3,2,1,0:T(8,128)(2,1)S(1)}, bf16[16,2,128,128]{3,2,1,0:T(8,128)(2,1)}, u32[]{:S(2)}) copy-start(bf16[16,2,128,128]{3,2,1,0:T(8,128)(2,1)} %copy-done.4) | copy-start | bytes 3145732
  36.4 17.9 %copy-start.6 = (f32[8,128,128]{2,1,0:T(8,128)S(1)}, f32[8,128,128]{2,1,0:T(8,128)}, u32[]{:S(2)}) copy-start(f32[8,128,128]{2,1,0:T(8,128)} %get-tuple-element.43.ex_ref) | copy-start | bytes 1572868
  54.2 2.8 %collective-permute-start.3 = (f32[8,2,128,128]{3,2,1,0:T(8,128)S(1)}, f32[8,2,128,128]{3,2,1,0:T(8,128)S(1)}, u32[]{:S(2)}, u32[]{:S(2)}) collective-permute-start(f32[8,2,128,128]{3,2,1,0:T(8,128)S(1)} %all_to_all.10.st_ref), channel_id=1, source_target_pairs={{0,8},{8,0},{1,9},{9,1},{2,10},{10,2},{3,11},{11,3},{4,12},{12,4},... | collective-permute-start | bytes 3145736 | tf_op jit(solution)/shard_map/ppermute | solution.py:299

commit v3 on v2

v3 whole, which is shorter than its diff:
```python
import functools
import itertools
import math

import jax
import jax.numpy as jnp
from jax import lax
from jax.experimental import pallas as pl
from jax.experimental.pallas import tpu as pltpu
from jax.sharding import Mesh, PartitionSpec as P

D = 128
F32 = jnp.float32
BF16 = jnp.bfloat16
VMEM_LIMIT = 20 * 1024 * 1024
HBM = pl.BlockSpec(memory_space=pltpu.HBM)
VMEM = pl.BlockSpec(memory_space=pltpu.VMEM)
SMEM = pl.BlockSpec(memory_space=pltpu.SMEM)


def in_vmem(shape, dtype=F32):
    return pltpu.VMEM(shape, dtype)


def call(body, out_shape, in_specs, out_specs, scratch, flops, moved, name, aliases=None):
    return pl.pallas_call(
        body,
        out_shape=out_shape,
        in_specs=in_specs,
        out_specs=out_specs,
        scratch_shapes=scratch,
        input_output_aliases=aliases or {},
        compiler_params=pltpu.CompilerParams(vmem_limit_bytes=VMEM_LIMIT),
        cost_estimate=pl.CostEstimate(flops=flops, bytes_accessed=moved, transcendentals=0),
        name=name,
    )


def rotate(rows, cosine, sine):
    wide = rows.astype(F32)
    return wide * cosine + pltpu.roll(wide, D // 2, 1) * sine


def unrotate(rows, cosine, sine):
    return rows * cosine - pltpu.roll(rows, D // 2, 1) * sine


def dot(a, b, ca, cb):
    return lax.dot_general(a, b, (((ca,), (cb,)), ((), ())), preferred_element_type=F32)


def rotary_tables(positions):
    rows = positions.shape[1]
    half = D // 2
    lane = lax.broadcasted_iota(jnp.int32, (rows, D), 1)
    index = jnp.where(lane < half, lane, lane - half).astype(F32)
    frequency = jnp.exp(index * (-2.0 * math.log(500000.0) / D))
    place = jnp.broadcast_to(positions.astype(F32), (D, rows)).T
    angle = place * frequency
    sine = jnp.sin(angle)
    return jnp.cos(angle), jnp.where(lane < half, -sine, sine)


def states_body(first, far, heads, *refs):
    if first:
        core, _, _, pos, q, k, v, g, cos_ref, sin_ref, out_ref, ps, qs, ks, vs, gs, sems = refs
        pos_copy = pltpu.make_async_copy(pos, ps, sems.at[4])
        pos_copy.start()
    else:
        core, _, _, cos_ref, sin_ref, q, k, v, g, out_ref, qs, ks, vs, gs, sems = refs
    start = pl.multiple_of((1 - core[0] if far else core[0]) * (heads * D), heads * D)
    copies = []
    for i, (src, dst) in enumerate(((k, ks), (v, vs), (q, qs), (g, gs))):
        copies.append(pltpu.make_async_copy(src.at[:, pl.ds(start, heads * D)], dst, sems.at[i]))
    for copy in copies:
        copy.start()
    if first:
        pos_copy.wait()
        cosine, sine = rotary_tables(ps[...])
        cos_ref[...] = cosine
        sin_ref[...] = sine
    else:
        cosine, sine = cos_ref[...], sin_ref[...]
    per, cut = out_ref.shape[0] // heads, out_ref.shape[2]
    for side, (rows, others) in enumerate(((ks, vs), (qs, gs))):
        copies[2 * side].wait()
        copies[2 * side + 1].wait()
        for h in range(heads):
            cols = slice(h * D, (h + 1) * D)
            turned = rotate(rows[:, cols], cosine, sine).astype(BF16)
            state = dot(turned, others[:, cols], 0, 0)
            for i in range(per):
                out_ref[h * per + i, side] = state[i * cut : (i + 1) * cut]


def states(who, far, heads, members, q, k, v, g, tables, pos):
    rows = q.shape[0]
    first = tables is None
    table = in_vmem((rows, D))
    result = in_vmem((members, 2, heads * D // members, D))
    body = functools.partial(states_body, first, far, heads)
    scratch = [pltpu.VMEM((rows, heads * D), BF16)] * 4 + [pltpu.SemaphoreType.DMA((5,))]
    work = (4 * heads * rows * D * D, heads * D * (8 * rows + 8 * D))
    if first:
        return call(
            body, [table, table, result], [SMEM] * 3 + [HBM] * 5, [VMEM] * 3,
            [pltpu.VMEM((1, rows), jnp.int32)] + scratch, *work, "block_states",
        )(*who, pos, q, k, v, g)
    return call(body, result, [SMEM] * 3 + [VMEM, VMEM] + [HBM] * 4, VMEM, scratch, *work, "block_states")(
        *who, *tables, q, k, v, g
    )


def add_body(_, me, __, a_ref, b_ref, *pieces):
    me = me[0]
    for m, piece in enumerate(pieces):
        piece[...] = a_ref[me ^ m] + b_ref[me ^ m]


def add(who, a, b):
    members, _, cut, _ = a.shape
    return call(
        add_body, [in_vmem((2, cut, D))] * members, [SMEM] * 3 + [VMEM, VMEM],
        [VMEM] * members, [], a.size, a.size * 12, "chip_sum",
    )(*who, a, b)


def total_body(_, __, group, *refs):
    group = group[0]
    out_ref = refs[-1]
    for side in range(2):
        total = refs[0][side]
        for ref in refs[1:-1]:
            total = total + ref[side]
        if out_ref.shape[0] == 2:
            out_ref[side] = total
        elif side == 0:
            keys = total
        else:
            out_ref[0] = jnp.where(group == 0, keys, total)


def total(who, pieces, kinds):
    _, cut, _ = pieces[0].shape
    size = len(pieces) * pieces[0].size
    return call(
        total_body, in_vmem((kinds, cut, D)), [SMEM] * 3 + [VMEM] * len(pieces), VMEM, [], size, size * 4, "block_total",
    )(*who, *pieces)


def offset_body(members, _, __, group, passed_ref, *refs):
    group = group[0]
    for side in range(2):
        if passed_ref.shape[0] == 1:
            extra = jnp.where(group == 1 - side, passed_ref[0], 0.0)
        else:
            extra = passed_ref[side]
        for m in range(members):
            refs[members + m][side] = refs[m][side] + extra


def offset(who, sums, passed):
    members = len(sums)
    size = members * sums[0].size
    return call(
        functools.partial(offset_body, members), [in_vmem(sums[0].shape)] * members,
        [SMEM] * 3 + [VMEM] * (members + 1), [VMEM] * members, [], size, size * 8, "group_sum",
    )(*who, passed, *sums)


def scan_body(members, _, me, __, *refs):
    pieces, sums, (held, ran) = refs[:members], refs[members : 2 * members], refs[2 * members :]
    me = me[0]
    for m in range(members):
        held[me ^ m] = pieces[m][...]
    for side, order in enumerate((range(members), reversed(range(members)))):
        total = jnp.zeros(held.shape[2:], F32)
        for j in order:
            ran[j, side] = total
            total = total + held[j, side]
    for m in range(members):
        sums[m][...] = ran[me ^ m]


def scan(who, pieces):
    members, (_, cut, _) = len(pieces), pieces[0].shape
    shape = (members, 2, cut, D)
    size = math.prod(shape)
    return call(
        functools.partial(scan_body, members), [in_vmem((2, cut, D))] * members,
        [SMEM] * 3 + [VMEM] * members, [VMEM] * members, [pltpu.VMEM(shape, F32)] * 2, size, size * 8, "chip_scan",
    )(*who, *pieces)


def local_kernel(q_ref, k_ref, v_ref, g_ref, cos_ref, sin_ref, rot_ref, sc_ref):
    cosine, sine = cos_ref[...], sin_ref[...]
    rows = q_ref.shape[0]
    row = lax.broadcasted_iota(jnp.int32, (rows, rows), 0)
    col = lax.broadcasted_iota(jnp.int32, (rows, rows), 1)
    for h in range(rot_ref.shape[0]):
        cols = slice(h * D, (h + 1) * D)
        krot = rotate(k_ref[:, cols], cosine, sine).astype(BF16)
        qrot = rotate(q_ref[:, cols], cosine, sine).astype(BF16)
        v, g = v_ref[:, cols], g_ref[:, cols]
        rot_ref[h, 0] = qrot
        rot_ref[h, 1] = krot
        rot_ref[h, 2] = v
        rot_ref[h, 3] = g
        sc_ref[h, 0] = jnp.where(row >= col, dot(qrot, krot, 1, 1), 0.0).astype(BF16)
        sc_ref[h, 1] = jnp.where(row >= col, dot(g, v, 1, 1), 0.0).astype(BF16)
        sc_ref[h, 2] = jnp.where(row <= col, dot(krot, qrot, 1, 1), 0.0).astype(BF16)
        sc_ref[h, 3] = jnp.where(row <= col, dot(v, g, 1, 1), 0.0).astype(BF16)


def local_scores(q, k, v, g, cosine, sine, heads):
    rows = q.shape[0]
    return call(
        local_kernel,
        [in_vmem((heads, 4, rows, D), BF16), in_vmem((heads, 4, rows, rows), BF16)],
        [VMEM] * 6, [VMEM] * 2, [], 8 * heads * rows * D * D, 10 * rows * heads * D * 2, "local_scores",
    )(q, k, v, g, cosine, sine)


def outputs_body(scale, per, heads, far, core, me, _, rot_ref, sc_ref, cos_ref, sin_ref, *refs):
    core, me = core[0], me[0]
    count = heads * per
    if far:
        pieces, refs = refs[:1], refs[5:]
    else:
        extra_ref, pieces, refs = refs[0], refs[1 : 1 + count], refs[1 + count :]
    outs, (state_ref, held, sems) = refs[:4], refs[4:]
    cosine, sine = cos_ref[...], sin_ref[...]
    copies = []
    for n in range(heads):
        low = me % per
        head = (me // per) ^ n
        for i in range(per):
            cut = pieces[0].shape[-2]
            at = pl.ds(pl.multiple_of((low ^ i) * cut, cut), cut)
            for side in range(2):
                if far:
                    state = pieces[0][n * per + i, side]
                else:
                    extra = extra_ref[head * per + (low ^ i), side]
                    state = pieces[n * per + i][side] + jnp.where(core == 1 - side, extra, 0.0)
                state_ref[n, side, at] = state.astype(BF16)
        before, after = state_ref[n, 0], state_ref[n, 1]
        at = (1 - core if far else core) * heads + head
        qrot, krot, v, g = (rot_ref[at, i] for i in range(4))
        att = dot(sc_ref[at, 0], v, 1, 0) + dot(qrot, before, 1, 0)
        rqg = dot(sc_ref[at, 1], krot, 1, 0) + dot(g, before, 1, 1)
        rkg = dot(sc_ref[at, 3], qrot, 1, 0) + dot(v, after, 1, 1)
        vg = dot(sc_ref[at, 2], g, 1, 0) + dot(krot, after, 1, 0)
        held[n, 0] = (scale * att).astype(BF16)
        held[n, 1] = unrotate(scale * rqg, cosine, sine).astype(BF16)
        held[n, 2] = unrotate(scale * rkg, cosine, sine).astype(BF16)
        held[n, 3] = (scale * vg).astype(BF16)
        for i in range(4):
            cols = pl.ds(pl.multiple_of(at * D, D), D)
            copies.append(pltpu.make_async_copy(held.at[n, i], outs[i].at[:, cols], sems.at[n, i]))
            copies[-1].start()
    for copy in copies:
        copy.wait()


def outputs(scale, per, count, who, rot, sc, tables, extra, pieces, prior):
    heads, _, rows, _ = rot.shape
    far = extra is None
    pieces = list(pieces) if far else [extra, *pieces]
    return call(
        functools.partial(outputs_body, scale, per, count, far),
        [pltpu.HBM((rows, heads * D), BF16)] * 4,
        [SMEM] * 3 + [VMEM] * (4 + len(pieces)) + [HBM] * len(prior),
        [HBM] * 4,
        [
            pltpu.VMEM((count, 2, D, D), BF16),
            pltpu.VMEM((count, 4, rows, D), BF16),
            pltpu.SemaphoreType.DMA((count, 4)),
        ],
        16 * count * rows * D * D,
        12 * rows * count * D * 2,
        "block_outputs",
        {7 + len(pieces) + i: i for i in range(len(prior))},
    )(*who, rot, sc, *tables, *pieces, *prior)


def relay_body(masks, core, me, _, near_ref, *refs):
    core, me = core[0], me[0]
    out_ref = refs[-1]
    for n, mask in enumerate(masks):
        for side in range(2):
            own = jnp.where(core == side, near_ref[me ^ mask, side], 0.0)
            out_ref[n, side] = refs[n][side] + own


def relay(masks, who, near, pieces):
    size = len(pieces) * pieces[0].size
    return call(
        functools.partial(relay_body, masks), in_vmem((len(pieces),) + pieces[0].shape),
        [SMEM] * 3 + [VMEM] * (1 + len(pieces)), VMEM, [], size, size * 8, "sibling_state",
    )(*who, near, *pieces)


def swap(value, axis):
    return lax.ppermute(value, axis, [(0, 1), (1, 0)])


AXES = ("x", "zl", "y")


def send_to(value, mask):
    x, zl, y = (lax.axis_size(axis) for axis in AXES)
    mx, my, mz = mask % x, mask // x % y, mask // (x * y)
    place = lambda a, b, c: (a * zl + b) * y + c
    pairs = [
        (place(a, b, c), place(a ^ mx, b ^ mz, c ^ my))
        for a, b, c in itertools.product(range(x), range(zl), range(y))
    ]
    return lax.ppermute(value, AXES, pairs)


def barrier(*values):
    return lax.optimization_barrier(values)


def exchange(pieces, order):
    arrived = {m: send_to(pieces[m], m) for m in order}
    arrived[0] = pieces[0]
    return arrived


def shards(q, k, v, g, positions):
    rows, width = q.shape
    heads = width // D
    part = heads // 2
    tokens = rows
    for axis in ("x", "core", "zh", "zl", "y"):
        tokens = tokens * lax.axis_size(axis)
    scale = (D * tokens) ** (-0.5)
    core, group = lax.axis_index("core"), lax.axis_index("zh")
    members, groups = lax.axis_size(("zl", "y", "x")), lax.axis_size("zh")
    me = lax.axis_index(("zl", "y", "x"))
    who = [scalar.reshape(1) for scalar in (core, me, group)]
    per = members // part
    pos = positions.reshape(1, rows)

    hq, hk, hv, hg, pos = (pltpu.with_memory_space_constraint(a, pltpu.HBM) for a in (q, k, v, g, pos))
    *tables, far = states(who, True, part, members, hq, hk, hv, hg, None, pos)
    near_other = swap(far, "core")
    near = states(who, False, part, members, hq, hk, hv, hg, tables, pos)
    pieces = add(who, near, near_other)
    pieces, tables = barrier(pieces, tables)

    order = sorted(range(1, members), key=lambda m: (bin(m).count("1"), m))
    arrived = exchange(pieces, order)
    rot, sc = local_scores(q, k, v, g, *tables, heads)
    listed, rot, sc = barrier([arrived[m] for m in order], rot, sc)
    arrived = [pieces[0]] + [listed[order.index(m)] for m in range(1, members)]

    send = total(who, arrived, 1 if groups == 2 else 2)
    if groups == 2:
        passed = swap(send, "zh")
    else:
        every = lax.all_gather(send, "zh")
        place = jnp.arange(groups)[:, None, None, None]
        wanted = jnp.where(jnp.arange(2)[:, None, None] == 0, place < group, place > group)
        passed = jnp.sum(jnp.where(wanted, every, 0.0), axis=0)
    pieces = offset(who, scan(who, arrived), passed)
    whole = exchange(pieces, order)

    whole = barrier(*(whole[m] for m in range(members)))
    other = swap(relay(range(members), who, near, whole), "core")
    made = outputs(scale, per, part, who, rot, sc, tables, near_other, whole, ())
    made = outputs(scale, per, part, who, rot, sc, tables, None, [other], tuple(made))
    return tuple(made)


def solution(mesh):
    inner, outer = mesh.shape["inner"], mesh.shape["outer"]
    x = inner // 2
    y = x if outer % x == 0 else 1
    z = outer // y
    zl = 2 if z % 2 == 0 else 1
    whole = Mesh(mesh.devices.reshape(x, 2, z // zl, zl, y), ("x", "core", "zh", "zl", "y"))
    rows = ("zh", "zl", "y", "x", "core")
    return jax.shard_map(
        shards,
        mesh=whole,
        in_specs=(P(rows, None),) * 4 + (P(rows),),
        out_specs=(P(rows, None),) * 4,
        check_vma=False,
    )
```

time: 61 us -> 52.3 us (0.86)
  blocking collectives: 16.7 us -> 0 us
  starting transfers between devices: 9.29 us -> 23.3 us
  Pallas kernels: 15.9 us -> 9.77 us
  waiting for transfers between devices: 13.8 us -> 18.4 us
  local copies, waits for them, and re-layouts: 3.72 us -> 0.01 us
    ppermute x0 -> x14, starting transfers between devices: none -> 20.1 us  [send_to(): return lax.ppermute(value, AXES, pairs)]
    all_to_all x1 -> x0, blocking collectives: 16.7 us -> none  [shards(): whole = [lax.all_to_all(back[c], GROUP, 0, 0, tiled=True) for c in chunks]]
    ppermute x0 -> x14, waiting for transfers between devices: none -> 14.3 us  [send_to(): return lax.ppermute(value, AXES, pairs)]
    all_to_all x1 -> x0, waiting for transfers between devices: 9.47 us -> none  [shards(): held = [lax.all_to_all(chip[c], GROUP, 0, 0, tiled=True) for c in chunks]]
    pallas_call x8 -> x10, Pallas kernels: 15.9 us -> 9.77 us  [the longest x2 3.88 us: outputs(): call(functools.partial(outputs_body, scale, per, count, far), [pltpu.HBM(...]
    all_to_all x1 -> x0, starting transfers between devices: 6.12 us -> none  [shards(): held = [lax.all_to_all(chip[c], GROUP, 0, 0, tiled=True) for c in chunks]]
    unnamed x16 -> x8, local copies, waits for them, and re-layouts: 3.72 us -> 0.01 us
    ppermute x4 -> x3, waiting for transfers between devices: 4.33 us -> 4.1 us  [swap(): return lax.ppermute(value, axis, [(0, 1), (1, 0)])]
  transfers between devices with their start and end apart: 5 -> 17, of which waited for: 3 -> 10; matrix products, arithmetic and copies ran while one was open for 0% -> 0% of each run, Pallas kernels for 11% -> 11%
where the time goes in v3:
time: 52.3 us; the launch traced here: 52.2 us
  starting transfers between devices  23.3 us (45%)
  waiting for transfers between devices  18.4 us (35%)
  Pallas kernels  9.77 us (19%)
  between operations  0.73 us (1%)
    ppermute x14, starting transfers between devices, send_to(): return lax.ppermute(value, AXES, pairs)  20.1 us
    ppermute x14, waiting for transfers between devices, send_to(): return lax.ppermute(value, AXES, pairs)  14.3 us
    ppermute x3, waiting for transfers between devices, swap(): return lax.ppermute(value, axis, [(0, 1), (1, 0)])  4.1 us
    pallas_call x2, Pallas kernels, outputs(): call(functools.partial(outputs_body, scale, per, count, far), [pltpu.HBM(...  3.88 us
    ppermute x3, starting transfers between devices, swap(): return lax.ppermute(value, axis, [(0, 1), (1, 0)])  3.24 us
    pallas_call x1, Pallas kernels, states(): call(body, result, [SMEM] * 3 + [VMEM, VMEM] + [HBM] * 4, VMEM, scratch,...  1.92 us
    pallas_call x1, Pallas kernels, states(): call(body, [table, table, result], [SMEM] * 3 + [HBM] * 5, [VMEM] * 3, [p...  1.79 us
    pallas_call x1, Pallas kernels, local_scores(): call(local_kernel, [in_vmem((heads, 4, rows, D), BF16), in_vmem((heads, 4...  1.59 us
  transfers between devices with their start and end apart: 17, of which 10 were waited for; matrix products, arithmetic and copies ran while one was open for 0% of the time, Pallas kernels for 11%

profile of v3, /device:TPU:0, one launch (start us, length us, event | category | flops | bytes accessed | tf_op | source)
XLA Modules:
  0.0 52.2 jit_solution(18174770689604021750)
XLA Ops:
  0.6 1.8 %block_states.2 = (f32[128,128]{1,0:T(8,128)S(1)}, f32[128,128]{1,0:T(8,128)S(1)}, f32[8,2,128,128]{3,2,1,0:T(8,128)S(1)}) custom-call(s32[1]{0:T(128)} %bitcast.refs_0_._.core, s32[1]{0:T(128)} %bitcast.1.refs_1_.me.__, s32[1]{0:T(128)} %bitcast.2.refs_2_.__.group._, s32[1,128]{1,0:T(1,128)} %bitcast.4, bf16[128,2048]{1,0:T(8,128)(2,1)} %q_ref.1, ...), custom_call_target="tpu_custom_call" | custom-call | flops 67108864 | bytes 2097152 | tf_op jit(solution)/shard_map/block_states/pallas_call | solution.py:105
  3.0 1.9 %block_states.3.a_ref.near_ref = f32[8,2,128,128]{3,2,1,0:T(8,128)S(1)} custom-call(s32[1]{0:T(128)} %bitcast.refs_0_._.core, s32[1]{0:T(128)} %bitcast.1.refs_1_.me.__, s32[1]{0:T(128)} %bitcast.2.refs_2_.__.group._, f32[128,128]{1,0:T(8,128)S(1)} %get-tuple-element.82.refs_3_.cos_ref, f32[128,128]{1,0:T(8,128)S(1)} %get-tuple-element.83.refs_4_.sin_ref, ...), custom_call_target="tpu_custom_call" | custom-call | flops 67108864 | bytes 2097152 | tf_op jit(solution)/shard_map/block_states/pallas_call | solution.py:109
  5.4 2.9 %collective-permute-start.1 = (f32[2,128,128]{2,1,0:T(8,128)S(1)}, f32[2,128,128]{2,1,0:T(8,128)S(1)}, u32[]{:S(2)}, u32[]{:S(2)}) collective-permute-start(f32[2,128,128]{2,1,0:T(8,128)S(1)} %get-tuple-element.75), channel_id=1, source_target_pairs={{0,16},{1,17},{2,18},{3,19},{16,0},{17,1},{18,2},{19,3},{4,20},{5,... | collective-permute-start | bytes 393224 | tf_op jit(solution)/shard_map/ppermute | solution.py:319
  8.3 1.5 %collective-permute-start.2 = (f32[2,128,128]{2,1,0:T(8,128)S(1)}, f32[2,128,128]{2,1,0:T(8,128)S(1)}, u32[]{:S(2)}, u32[]{:S(2)}) collective-permute-start(f32[2,128,128]{2,1,0:T(8,128)S(1)} %get-tuple-element.76), channel_id=1, source_target_pairs={{0,1},{1,0},{2,3},{3,2},{16,17},{17,16},{18,19},{19,18},{4,5},{5,4... | collective-permute-start | bytes 393224 | tf_op jit(solution)/shard_map/ppermute | solution.py:319
  9.8 1.6 %collective-permute-start.3 = (f32[2,128,128]{2,1,0:T(8,128)S(1)}, f32[2,128,128]{2,1,0:T(8,128)S(1)}, u32[]{:S(2)}, u32[]{:S(2)}) collective-permute-start(f32[2,128,128]{2,1,0:T(8,128)S(1)} %get-tuple-element.77), channel_id=1, source_target_pairs={{0,2},{1,3},{2,0},{3,1},{16,18},{17,19},{18,16},{19,17},{4,6},{5,7... | collective-permute-start | bytes 393224 | tf_op jit(solution)/shard_map/ppermute | solution.py:319
  11.9 1.4 %collective-permute-start.5 = (f32[2,128,128]{2,1,0:T(8,128)S(1)}, f32[2,128,128]{2,1,0:T(8,128)S(1)}, u32[]{:S(2)}, u32[]{:S(2)}) collective-permute-start(f32[2,128,128]{2,1,0:T(8,128)S(1)} %get-tuple-element.79), channel_id=1, source_target_pairs={{0,18},{1,19},{2,16},{3,17},{16,2},{17,3},{18,0},{19,1},{4,22},{5,... | collective-permute-start | bytes 393224 | tf_op jit(solution)/shard_map/ppermute | solution.py:319
  13.2 2.5 %collective-permute-start.6 = (f32[2,128,128]{2,1,0:T(8,128)S(1)}, f32[2,128,128]{2,1,0:T(8,128)S(1)}, u32[]{:S(2)}, u32[]{:S(2)}) collective-permute-start(f32[2,128,128]{2,1,0:T(8,128)S(1)} %get-tuple-element.80), channel_id=1, source_target_pairs={{0,3},{1,2},{2,1},{3,0},{16,19},{17,18},{18,17},{19,16},{4,7},{5,6... | collective-permute-start | bytes 393224 | tf_op jit(solution)/shard_map/ppermute | solution.py:319
  15.8 1.5 %collective-permute-start.7 = (f32[2,128,128]{2,1,0:T(8,128)S(1)}, f32[2,128,128]{2,1,0:T(8,128)S(1)}, u32[]{:S(2)}, u32[]{:S(2)}) collective-permute-start(f32[2,128,128]{2,1,0:T(8,128)S(1)} %get-tuple-element.81), channel_id=1, source_target_pairs={{0,19},{1,18},{2,17},{3,16},{16,3},{17,2},{18,1},{19,0},{4,23},{5,... | collective-permute-start | bytes 393224 | tf_op jit(solution)/shard_map/ppermute | solution.py:319
  17.3 1.6 %local_scores.1 = (bf16[16,4,128,128]{3,2,1,0:T(8,128)(2,1)S(1)}, bf16[16,4,128,128]{3,2,1,0:T(8,128)(2,1)S(1)}) custom-call(bf16[128,2048]{1,0:T(8,128)(2,1)S(1)} %copy-done, bf16[128,2048]{1,0:T(8,128)(2,1)S(1)} %copy-done.1, bf16[128,2048]{1,0:T(8,128)(2,1)S(1)} %copy-done.2, bf16[128,2048]{1,0:T(8,128)(2,1)S(1)} %copy-done.3, ...), custom_call_target="tpu_custom_call" | custom-call | flops 268435456 | bytes 5242880 | tf_op jit(solution)/shard_map/local_scores/pallas_call | solution.py:217
  18.9 1.7 %collective-permute-done.4.refs_3_ = f32[2,128,128]{2,1,0:T(8,128)S(1)} collective-permute-done((f32[2,128,128]{2,1,0:T(8,128)S(1)}, f32[2,128,128]{2,1,0:T(8,128)S(1)}, u32[]{:S(2)}, u32[]{:S(2)}) %collective-permute-start.4) | collective-permute-done | bytes 131104 | tf_op jit(solution)/shard_map/ppermute | solution.py:319
  20.7 1.9 %collective-permute-done.6.refs_6_ = f32[2,128,128]{2,1,0:T(8,128)S(1)} collective-permute-done((f32[2,128,128]{2,1,0:T(8,128)S(1)}, f32[2,128,128]{2,1,0:T(8,128)S(1)}, u32[]{:S(2)}, u32[]{:S(2)}) %collective-permute-start.6) | collective-permute-done | bytes 131104 | tf_op jit(solution)/shard_map/ppermute | solution.py:319
  22.6 1.4 %collective-permute-done.7.refs_7_ = f32[2,128,128]{2,1,0:T(8,128)S(1)} collective-permute-done((f32[2,128,128]{2,1,0:T(8,128)S(1)}, f32[2,128,128]{2,1,0:T(8,128)S(1)}, u32[]{:S(2)}, u32[]{:S(2)}) %collective-permute-start.7) | collective-permute-done | bytes 131104 | tf_op jit(solution)/shard_map/ppermute | solution.py:319
  24.0 2.7 %collective-permute-start.8 = (f32[1,128,128]{2,1,0:T(8,128)S(1)}, f32[1,128,128]{2,1,0:T(8,128)S(1)}, u32[]{:S(2)}, u32[]{:S(2)}) collective-permute-start(f32[1,128,128]{2,1,0:T(8,128)S(1)} %block_total.1), channel_id=1, source_target_pairs={{0,4},{4,0},{1,5},{5,1},{2,6},{6,2},{3,7},{7,3},{8,12},{12,8},{9,1... | collective-permute-start | bytes 196616 | tf_op jit(solution)/shard_map/ppermute | solution.py:305
  26.9 3.1 %collective-permute-done.8.passed_ref = f32[1,128,128]{2,1,0:T(8,128)S(1)} collective-permute-done((f32[1,128,128]{2,1,0:T(8,128)S(1)}, f32[1,128,128]{2,1,0:T(8,128)S(1)}, u32[]{:S(2)}, u32[]{:S(2)}) %collective-permute-start.8) | collective-permute-done | bytes 65568 | tf_op jit(solution)/shard_map/ppermute | solution.py:305
  30.0 1.4 %collective-permute-start.9 = (f32[2,128,128]{2,1,0:T(8,128)S(1)}, f32[2,128,128]{2,1,0:T(8,128)S(1)}, u32[]{:S(2)}, u32[]{:S(2)}) collective-permute-start(f32[2,128,128]{2,1,0:T(8,128)S(1)} %get-tuple-element.105), channel_id=1, source_target_pairs={{0,16},{1,17},{2,18},{3,19},{16,0},{17,1},{18,2},{19,3},{4,20},{5,... | collective-permute-start | bytes 393224 | tf_op jit(solution)/shard_map/ppermute | solution.py:319
  31.6 2.0 %collective-permute-start.11 = (f32[2,128,128]{2,1,0:T(8,128)S(1)}, f32[2,128,128]{2,1,0:T(8,128)S(1)}, u32[]{:S(2)}, u32[]{:S(2)}) collective-permute-start(f32[2,128,128]{2,1,0:T(8,128)S(1)} %get-tuple-element.107), channel_id=1, source_target_pairs={{0,17},{1,16},{2,19},{3,18},{16,1},{17,0},{18,3},{19,2},{4,21},{5,... | collective-permute-start | bytes 393224 | tf_op jit(solution)/shard_map/ppermute | solution.py:319
  33.8 2.6 %collective-permute-start.13 = (f32[2,128,128]{2,1,0:T(8,128)S(1)}, f32[2,128,128]{2,1,0:T(8,128)S(1)}, u32[]{:S(2)}, u32[]{:S(2)}) collective-permute-start(f32[2,128,128]{2,1,0:T(8,128)S(1)} %get-tuple-element.109), channel_id=1, source_target_pairs={{0,18},{1,19},{2,16},{3,17},{16,2},{17,3},{18,0},{19,1},{4,22},{5,... | collective-permute-start | bytes 393224 | tf_op jit(solution)/shard_map/ppermute | solution.py:319
  36.4 1.1 %collective-permute-start.14 = (f32[2,128,128]{2,1,0:T(8,128)S(1)}, f32[2,128,128]{2,1,0:T(8,128)S(1)}, u32[]{:S(2)}, u32[]{:S(2)}) collective-permute-start(f32[2,128,128]{2,1,0:T(8,128)S(1)} %get-tuple-element.110), channel_id=1, source_target_pairs={{0,3},{1,2},{2,1},{3,0},{16,19},{17,18},{18,17},{19,16},{4,7},{5,6... | collective-permute-start | bytes 393224 | tf_op jit(solution)/shard_map/ppermute | solution.py:319
  37.5 3.1 %collective-permute-done.10.refs_2_.refs_3_ = f32[2,128,128]{2,1,0:T(8,128)S(1)} collective-permute-done((f32[2,128,128]{2,1,0:T(8,128)S(1)}, f32[2,128,128]{2,1,0:T(8,128)S(1)}, u32[]{:S(2)}, u32[]{:S(2)}) %collective-permute-start.10) | collective-permute-done | bytes 131104 | tf_op jit(solution)/shard_map/ppermute | solution.py:319
  41.3 1.4 %collective-permute-done.14.refs_6_.refs_7_ = f32[2,128,128]{2,1,0:T(8,128)S(1)} collective-permute-done((f32[2,128,128]{2,1,0:T(8,128)S(1)}, f32[2,128,128]{2,1,0:T(8,128)S(1)}, u32[]{:S(2)}, u32[]{:S(2)}) %collective-permute-start.14) | collective-permute-done | bytes 131104 | tf_op jit(solution)/shard_map/ppermute | solution.py:319
  42.7 4.6 %collective-permute-done.15.refs_7_.refs_8_ = f32[2,128,128]{2,1,0:T(8,128)S(1)} collective-permute-done((f32[2,128,128]{2,1,0:T(8,128)S(1)}, f32[2,128,128]{2,1,0:T(8,128)S(1)}, u32[]{:S(2)}, u32[]{:S(2)}) %collective-permute-start.15) | collective-permute-done | bytes 131104 | tf_op jit(solution)/shard_map/ppermute | solution.py:319
  47.6 2.0 %block_outputs.2 = (bf16[128,2048]{1,0:T(8,128)(2,1)}, bf16[128,2048]{1,0:T(8,128)(2,1)}, bf16[128,2048]{1,0:T(8,128)(2,1)}, bf16[128,2048]{1,0:T(8,128)(2,1)}) custom-call(s32[1]{0:T(128)} %bitcast.refs_0_._.core, s32[1]{0:T(128)} %bitcast.1.refs_1_.me.__, s32[1]{0:T(128)} %bitcast.2.refs_2_.__.group._, ...), custom_call_target="tpu_custom_call" | custom-call | flops 268435456 | bytes 3145728 | tf_op jit(solution)/shard_map/block_outputs/pallas_call | solution.py:270
  49.5 0.7 %collective-permute-done.16.refs_0_ = f32[8,2,128,128]{3,2,1,0:T(8,128)S(1)} collective-permute-done((f32[8,2,128,128]{3,2,1,0:T(8,128)S(1)}, f32[8,2,128,128]{3,2,1,0:T(8,128)S(1)}, u32[]{:S(2)}, u32[]{:S(2)}) %collective-permute-start.16) | collective-permute-done | bytes 1048608 | tf_op jit(solution)/shard_map/ppermute | solution.py:305
  50.2 1.9 %block_outputs.3 = (bf16[128,2048]{1,0:T(8,128)(2,1)}, bf16[128,2048]{1,0:T(8,128)(2,1)}, bf16[128,2048]{1,0:T(8,128)(2,1)}, bf16[128,2048]{1,0:T(8,128)(2,1)}) custom-call(s32[1]{0:T(128)} %bitcast.refs_0_._.core, s32[1]{0:T(128)} %bitcast.1.refs_1_.me.__, ...), custom_call_target="tpu_custom_call", output_to_operand_aliasing={{0}: (8, {}), {1}: (9, {}), {2}: (10, {}), {3}: (11, {})} | custom-call | flops 268435456 | bytes 3145728 | tf_op jit(solution)/shard_map/block_outputs/pallas_call | solution.py:270
  (28 shorter events, 3.1 us)
Async XLA Ops:
  2.4 2.8 %collective-permute-start = (f32[8,2,128,128]{3,2,1,0:T(8,128)S(1)}, f32[8,2,128,128]{3,2,1,0:T(8,128)S(1)}, u32[]{:S(2)}, u32[]{:S(2)}) collective-permute-start(f32[8,2,128,128]{3,2,1,0:T(8,128)S(1)} %get-tuple-element.66), channel_id=1, source_target_pairs={{0,8},{8,0},{1,9},{9,1},{2,10},{10,2},{3,11},{11,3},{4,12},{12,4},... | collective-permute-start | bytes 3145736 | tf_op jit(solution)/shard_map/ppermute | solution.py:305
  3.0 14.4 %copy-start = (bf16[128,2048]{1,0:T(8,128)(2,1)S(1)}, bf16[128,2048]{1,0:T(8,128)(2,1)}, u32[]{:S(2)}) copy-start(bf16[128,2048]{1,0:T(8,128)(2,1)} %q_ref.1) | copy-start | bytes 1572868
  3.0 14.4 %copy-start.1 = (bf16[128,2048]{1,0:T(8,128)(2,1)S(1)}, bf16[128,2048]{1,0:T(8,128)(2,1)}, u32[]{:S(2)}) copy-start(bf16[128,2048]{1,0:T(8,128)(2,1)} %k_ref.1) | copy-start | bytes 1572868
  3.0 14.4 %copy-start.2 = (bf16[128,2048]{1,0:T(8,128)(2,1)S(1)}, bf16[128,2048]{1,0:T(8,128)(2,1)}, u32[]{:S(2)}) copy-start(bf16[128,2048]{1,0:T(8,128)(2,1)} %v_ref.1) | copy-start | bytes 1572868
  3.0 14.4 %copy-start.3 = (bf16[128,2048]{1,0:T(8,128)(2,1)S(1)}, bf16[128,2048]{1,0:T(8,128)(2,1)}, u32[]{:S(2)}) copy-start(bf16[128,2048]{1,0:T(8,128)(2,1)} %g_ref.1) | copy-start | bytes 1572868
  5.4 7.9 %collective-permute-start.1 = (f32[2,128,128]{2,1,0:T(8,128)S(1)}, f32[2,128,128]{2,1,0:T(8,128)S(1)}, u32[]{:S(2)}, u32[]{:S(2)}) collective-permute-start(f32[2,128,128]{2,1,0:T(8,128)S(1)} %get-tuple-element.75), channel_id=1, source_target_pairs={{0,16},{1,17},{2,18},{3,19},{16,0},{17,1},{18,2},{19,3},{4,20},{5,... | collective-permute-start | bytes 393224 | tf_op jit(solution)/shard_map/ppermute | solution.py:319
  8.3 7.5 %collective-permute-start.2 = (f32[2,128,128]{2,1,0:T(8,128)S(1)}, f32[2,128,128]{2,1,0:T(8,128)S(1)}, u32[]{:S(2)}, u32[]{:S(2)}) collective-permute-start(f32[2,128,128]{2,1,0:T(8,128)S(1)} %get-tuple-element.76), channel_id=1, source_target_pairs={{0,1},{1,0},{2,3},{3,2},{16,17},{17,16},{18,19},{19,18},{4,5},{5,4... | collective-permute-start | bytes 393224 | tf_op jit(solution)/shard_map/ppermute | solution.py:319
  9.8 9.1 %collective-permute-start.3 = (f32[2,128,128]{2,1,0:T(8,128)S(1)}, f32[2,128,128]{2,1,0:T(8,128)S(1)}, u32[]{:S(2)}, u32[]{:S(2)}) collective-permute-start(f32[2,128,128]{2,1,0:T(8,128)S(1)} %get-tuple-element.77), channel_id=1, source_target_pairs={{0,2},{1,3},{2,0},{3,1},{16,18},{17,19},{18,16},{19,17},{4,6},{5,7... | collective-permute-start | bytes 393224 | tf_op jit(solution)/shard_map/ppermute | solution.py:319
  11.4 9.3 %collective-permute-start.4 = (f32[2,128,128]{2,1,0:T(8,128)S(1)}, f32[2,128,128]{2,1,0:T(8,128)S(1)}, u32[]{:S(2)}, u32[]{:S(2)}) collective-permute-start(f32[2,128,128]{2,1,0:T(8,128)S(1)} %get-tuple-element.78), channel_id=1, source_target_pairs={{0,17},{1,16},{2,19},{3,18},{16,1},{17,0},{18,3},{19,2},{4,21},{5,... | collective-permute-start | bytes 393224 | tf_op jit(solution)/shard_map/ppermute | solution.py:319
  11.9 8.8 %collective-permute-start.5 = (f32[2,128,128]{2,1,0:T(8,128)S(1)}, f32[2,128,128]{2,1,0:T(8,128)S(1)}, u32[]{:S(2)}, u32[]{:S(2)}) collective-permute-start(f32[2,128,128]{2,1,0:T(8,128)S(1)} %get-tuple-element.79), channel_id=1, source_target_pairs={{0,18},{1,19},{2,16},{3,17},{16,2},{17,3},{18,0},{19,1},{4,22},{5,... | collective-permute-start | bytes 393224 | tf_op jit(solution)/shard_map/ppermute | solution.py:319
  13.2 9.3 %collective-permute-start.6 = (f32[2,128,128]{2,1,0:T(8,128)S(1)}, f32[2,128,128]{2,1,0:T(8,128)S(1)}, u32[]{:S(2)}, u32[]{:S(2)}) collective-permute-start(f32[2,128,128]{2,1,0:T(8,128)S(1)} %get-tuple-element.80), channel_id=1, source_target_pairs={{0,3},{1,2},{2,1},{3,0},{16,19},{17,18},{18,17},{19,16},{4,7},{5,6... | collective-permute-start | bytes 393224 | tf_op jit(solution)/shard_map/ppermute | solution.py:319
  15.8 8.2 %collective-permute-start.7 = (f32[2,128,128]{2,1,0:T(8,128)S(1)}, f32[2,128,128]{2,1,0:T(8,128)S(1)}, u32[]{:S(2)}, u32[]{:S(2)}) collective-permute-start(f32[2,128,128]{2,1,0:T(8,128)S(1)} %get-tuple-element.81), channel_id=1, source_target_pairs={{0,19},{1,18},{2,17},{3,16},{16,3},{17,2},{18,1},{19,0},{4,23},{5,... | collective-permute-start | bytes 393224 | tf_op jit(solution)/shard_map/ppermute | solution.py:319
  24.0 5.9 %collective-permute-start.8 = (f32[1,128,128]{2,1,0:T(8,128)S(1)}, f32[1,128,128]{2,1,0:T(8,128)S(1)}, u32[]{:S(2)}, u32[]{:S(2)}) collective-permute-start(f32[1,128,128]{2,1,0:T(8,128)S(1)} %block_total.1), channel_id=1, source_target_pairs={{0,4},{4,0},{1,5},{5,1},{2,6},{6,2},{3,7},{7,3},{8,12},{12,8},{9,1... | collective-permute-start | bytes 196616 | tf_op jit(solution)/shard_map/ppermute | solution.py:305
  30.0 6.4 %collective-permute-start.9 = (f32[2,128,128]{2,1,0:T(8,128)S(1)}, f32[2,128,128]{2,1,0:T(8,128)S(1)}, u32[]{:S(2)}, u32[]{:S(2)}) collective-permute-start(f32[2,128,128]{2,1,0:T(8,128)S(1)} %get-tuple-element.105), channel_id=1, source_target_pairs={{0,16},{1,17},{2,18},{3,19},{16,0},{17,1},{18,2},{19,3},{4,20},{5,... | collective-permute-start | bytes 393224 | tf_op jit(solution)/shard_map/ppermute | solution.py:319
  31.4 9.2 %collective-permute-start.10 = (f32[2,128,128]{2,1,0:T(8,128)S(1)}, f32[2,128,128]{2,1,0:T(8,128)S(1)}, u32[]{:S(2)}, u32[]{:S(2)}) collective-permute-start(f32[2,128,128]{2,1,0:T(8,128)S(1)} %get-tuple-element.106), channel_id=1, source_target_pairs={{0,1},{1,0},{2,3},{3,2},{16,17},{17,16},{18,19},{19,18},{4,5},{5,4... | collective-permute-start | bytes 393224 | tf_op jit(solution)/shard_map/ppermute | solution.py:319
  31.6 9.7 %collective-permute-start.11 = (f32[2,128,128]{2,1,0:T(8,128)S(1)}, f32[2,128,128]{2,1,0:T(8,128)S(1)}, u32[]{:S(2)}, u32[]{:S(2)}) collective-permute-start(f32[2,128,128]{2,1,0:T(8,128)S(1)} %get-tuple-element.107), channel_id=1, source_target_pairs={{0,17},{1,16},{2,19},{3,18},{16,1},{17,0},{18,3},{19,2},{4,21},{5,... | collective-permute-start | bytes 393224 | tf_op jit(solution)/shard_map/ppermute | solution.py:319
  33.6 7.7 %collective-permute-start.12 = (f32[2,128,128]{2,1,0:T(8,128)S(1)}, f32[2,128,128]{2,1,0:T(8,128)S(1)}, u32[]{:S(2)}, u32[]{:S(2)}) collective-permute-start(f32[2,128,128]{2,1,0:T(8,128)S(1)} %get-tuple-element.108), channel_id=1, source_target_pairs={{0,2},{1,3},{2,0},{3,1},{16,18},{17,19},{18,16},{19,17},{4,6},{5,7... | collective-permute-start | bytes 393224 | tf_op jit(solution)/shard_map/ppermute | solution.py:319
  33.8 7.5 %collective-permute-start.13 = (f32[2,128,128]{2,1,0:T(8,128)S(1)}, f32[2,128,128]{2,1,0:T(8,128)S(1)}, u32[]{:S(2)}, u32[]{:S(2)}) collective-permute-start(f32[2,128,128]{2,1,0:T(8,128)S(1)} %get-tuple-element.109), channel_id=1, source_target_pairs={{0,18},{1,19},{2,16},{3,17},{16,2},{17,3},{18,0},{19,1},{4,22},{5,... | collective-permute-start | bytes 393224 | tf_op jit(solution)/shard_map/ppermute | solution.py:319
  36.4 6.3 %collective-permute-start.14 = (f32[2,128,128]{2,1,0:T(8,128)S(1)}, f32[2,128,128]{2,1,0:T(8,128)S(1)}, u32[]{:S(2)}, u32[]{:S(2)}) collective-permute-start(f32[2,128,128]{2,1,0:T(8,128)S(1)} %get-tuple-element.110), channel_id=1, source_target_pairs={{0,3},{1,2},{2,1},{3,0},{16,19},{17,18},{18,17},{19,16},{4,7},{5,6... | collective-permute-start | bytes 393224 | tf_op jit(solution)/shard_map/ppermute | solution.py:319
  40.6 6.8 %collective-permute-start.15 = (f32[2,128,128]{2,1,0:T(8,128)S(1)}, f32[2,128,128]{2,1,0:T(8,128)S(1)}, u32[]{:S(2)}, u32[]{:S(2)}) collective-permute-start(f32[2,128,128]{2,1,0:T(8,128)S(1)} %get-tuple-element.111), channel_id=1, source_target_pairs={{0,19},{1,18},{2,17},{3,16},{16,3},{17,2},{18,1},{19,0},{4,23},{5,... | collective-permute-start | bytes 393224 | tf_op jit(solution)/shard_map/ppermute | solution.py:319
  47.5 2.7 %collective-permute-start.16 = (f32[8,2,128,128]{3,2,1,0:T(8,128)S(1)}, f32[8,2,128,128]{3,2,1,0:T(8,128)S(1)}, u32[]{:S(2)}, u32[]{:S(2)}) collective-permute-start(f32[8,2,128,128]{3,2,1,0:T(8,128)S(1)} %sibling_state.1), channel_id=1, source_target_pairs={{0,8},{8,0},{1,9},{9,1},{2,10},{10,2},{3,11},{11,3},{4,12},{12,4},... | collective-permute-start | bytes 3145736 | tf_op jit(solution)/shard_map/ppermute | solution.py:305

commit v4 on v3

--- a/solution.py
+++ b/solution.py
@@ -351,7 +351,10 @@
     pieces = add(who, near, near_other)
     pieces, tables = barrier(pieces, tables)
 
-    order = sorted(range(1, members), key=lambda m: (bin(m).count("1"), m))
+    order = []
+    for m in sorted(range(1, members - 1), key=lambda m: (bin(m).count("1"), m))[: members // 2 - 1]:
+        order += [m, members - 1 - m]
+    order.append(members - 1)
     arrived = exchange(pieces, order)
     rot, sc = local_scores(q, k, v, g, *tables, heads)
     listed, rot, sc = barrier([arrived[m] for m in order], rot, sc)
@@ -368,7 +371,8 @@
     pieces = offset(who, scan(who, arrived), passed)
     whole = exchange(pieces, order)
 
-    whole = barrier(*(whole[m] for m in range(members)))
+    whole = dict(zip([0] + order, barrier(*(whole[m] for m in [0] + order))))
+    whole = [whole[m] for m in range(members)]
     other = swap(relay(range(members), who, near, whole), "core")
     made = outputs(scale, per, part, who, rot, sc, tables, near_other, whole, ())
     made = outputs(scale, per, part, who, rot, sc, tables, None, [other], tuple(made))

time: 52.3 us -> 49.4 us (0.945)
  waiting for transfers between devices: 18.4 us -> 14.7 us
  starting transfers between devices: 23.3 us -> 24 us
    ppermute x14, waiting for transfers between devices: 14.3 us -> 10.6 us  [send_to(): return lax.ppermute(value, AXES, pairs)]
    ppermute x14, starting transfers between devices: 20.1 us -> 20.8 us  [send_to(): return lax.ppermute(value, AXES, pairs)]
  transfers between devices with their start and end apart: 17 -> 17, of which waited for: 10 -> 12; matrix products, arithmetic and copies ran while one was open for 0% -> 0% of each run, Pallas kernels for 11% -> 12%
where the time goes in v4:
time: 49.4 us; the launch traced here: 49.2 us
  starting transfers between devices  24 us (49%)
  waiting for transfers between devices  14.7 us (30%)
  Pallas kernels  9.77 us (20%)
  between operations  0.74 us (1%)
    ppermute x14, starting transfers between devices, send_to(): return lax.ppermute(value, AXES, pairs)  20.8 us
    ppermute x14, waiting for transfers between devices, send_to(): return lax.ppermute(value, AXES, pairs)  10.6 us
    ppermute x3, waiting for transfers between devices, swap(): return lax.ppermute(value, axis, [(0, 1), (1, 0)])  4.1 us
    pallas_call x2, Pallas kernels, outputs(): call(functools.partial(outputs_body, scale, per, count, far), [pltpu.HBM(...  3.88 us
    ppermute x3, starting transfers between devices, swap(): return lax.ppermute(value, axis, [(0, 1), (1, 0)])  3.24 us
    pallas_call x1, Pallas kernels, states(): call(body, result, [SMEM] * 3 + [VMEM, VMEM] + [HBM] * 4, VMEM, scratch,...  1.92 us
    pallas_call x1, Pallas kernels, states(): call(body, [table, table, result], [SMEM] * 3 + [HBM] * 5, [VMEM] * 3, [p...  1.79 us
    pallas_call x1, Pallas kernels, local_scores(): call(local_kernel, [in_vmem((heads, 4, rows, D), BF16), in_vmem((heads, 4...  1.59 us
  transfers between devices with their start and end apart: 17, of which 12 were waited for; matrix products, arithmetic and copies ran while one was open for 0% of the time, Pallas kernels for 12%

profile of v4, /device:TPU:0, one launch (start us, length us, event | category | flops | bytes accessed | tf_op | source)
XLA Modules:
  0.0 49.2 jit_solution(3543247857838066021)
XLA Ops:
  0.6 1.8 %block_states.2 = (f32[128,128]{1,0:T(8,128)S(1)}, f32[128,128]{1,0:T(8,128)S(1)}, f32[8,2,128,128]{3,2,1,0:T(8,128)S(1)}) custom-call(s32[1]{0:T(128)} %bitcast.refs_0_._.core, s32[1]{0:T(128)} %bitcast.1.refs_1_.me.__, s32[1]{0:T(128)} %bitcast.2.refs_2_.__.group._, s32[1,128]{1,0:T(1,128)} %bitcast.4, bf16[128,2048]{1,0:T(8,128)(2,1)} %q_ref.1, ...), custom_call_target="tpu_custom_call" | custom-call | flops 67108864 | bytes 2097152 | tf_op jit(solution)/shard_map/block_states/pallas_call | solution.py:105
  3.0 1.9 %block_states.3.a_ref.near_ref = f32[8,2,128,128]{3,2,1,0:T(8,128)S(1)} custom-call(s32[1]{0:T(128)} %bitcast.refs_0_._.core, s32[1]{0:T(128)} %bitcast.1.refs_1_.me.__, s32[1]{0:T(128)} %bitcast.2.refs_2_.__.group._, f32[128,128]{1,0:T(8,128)S(1)} %get-tuple-element.82.refs_3_.cos_ref, f32[128,128]{1,0:T(8,128)S(1)} %get-tuple-element.83.refs_4_.sin_ref, ...), custom_call_target="tpu_custom_call" | custom-call | flops 67108864 | bytes 2097152 | tf_op jit(solution)/shard_map/block_states/pallas_call | solution.py:109
  5.4 2.9 %collective-permute-start.1 = (f32[2,128,128]{2,1,0:T(8,128)S(1)}, f32[2,128,128]{2,1,0:T(8,128)S(1)}, u32[]{:S(2)}, u32[]{:S(2)}) collective-permute-start(f32[2,128,128]{2,1,0:T(8,128)S(1)} %get-tuple-element.75), channel_id=1, source_target_pairs={{0,16},{1,17},{2,18},{3,19},{16,0},{17,1},{18,2},{19,3},{4,20},{5,... | collective-permute-start | bytes 393224 | tf_op jit(solution)/shard_map/ppermute | solution.py:319
  8.3 2.5 %collective-permute-start.2 = (f32[2,128,128]{2,1,0:T(8,128)S(1)}, f32[2,128,128]{2,1,0:T(8,128)S(1)}, u32[]{:S(2)}, u32[]{:S(2)}) collective-permute-start(f32[2,128,128]{2,1,0:T(8,128)S(1)} %get-tuple-element.76), channel_id=1, source_target_pairs={{0,3},{1,2},{2,1},{3,0},{16,19},{17,18},{18,17},{19,16},{4,7},{5,6... | collective-permute-start | bytes 393224 | tf_op jit(solution)/shard_map/ppermute | solution.py:319
  11.4 2.0 %collective-permute-start.5 = (f32[2,128,128]{2,1,0:T(8,128)S(1)}, f32[2,128,128]{2,1,0:T(8,128)S(1)}, u32[]{:S(2)}, u32[]{:S(2)}) collective-permute-start(f32[2,128,128]{2,1,0:T(8,128)S(1)} %get-tuple-element.79), channel_id=1, source_target_pairs={{0,2},{1,3},{2,0},{3,1},{16,18},{17,19},{18,16},{19,17},{4,6},{5,7... | collective-permute-start | bytes 393224 | tf_op jit(solution)/shard_map/ppermute | solution.py:319
  13.3 2.4 %collective-permute-start.6 = (f32[2,128,128]{2,1,0:T(8,128)S(1)}, f32[2,128,128]{2,1,0:T(8,128)S(1)}, u32[]{:S(2)}, u32[]{:S(2)}) collective-permute-start(f32[2,128,128]{2,1,0:T(8,128)S(1)} %get-tuple-element.80), channel_id=1, source_target_pairs={{0,17},{1,16},{2,19},{3,18},{16,1},{17,0},{18,3},{19,2},{4,21},{5,... | collective-permute-start | bytes 393224 | tf_op jit(solution)/shard_map/ppermute | solution.py:319
  15.8 2.3 %collective-permute-start.7 = (f32[2,128,128]{2,1,0:T(8,128)S(1)}, f32[2,128,128]{2,1,0:T(8,128)S(1)}, u32[]{:S(2)}, u32[]{:S(2)}) collective-permute-start(f32[2,128,128]{2,1,0:T(8,128)S(1)} %get-tuple-element.81), channel_id=1, source_target_pairs={{0,19},{1,18},{2,17},{3,16},{16,3},{17,2},{18,1},{19,0},{4,23},{5,... | collective-permute-start | bytes 393224 | tf_op jit(solution)/shard_map/ppermute | solution.py:319
  18.1 1.6 %local_scores.1 = (bf16[16,4,128,128]{3,2,1,0:T(8,128)(2,1)S(1)}, bf16[16,4,128,128]{3,2,1,0:T(8,128)(2,1)S(1)}) custom-call(bf16[128,2048]{1,0:T(8,128)(2,1)S(1)} %copy-done, bf16[128,2048]{1,0:T(8,128)(2,1)S(1)} %copy-done.1, bf16[128,2048]{1,0:T(8,128)(2,1)S(1)} %copy-done.2, bf16[128,2048]{1,0:T(8,128)(2,1)S(1)} %copy-done.3, ...), custom_call_target="tpu_custom_call" | custom-call | flops 268435456 | bytes 5242880 | tf_op jit(solution)/shard_map/local_scores/pallas_call | solution.py:217
  19.7 1.5 %collective-permute-done.5.refs_4_ = f32[2,128,128]{2,1,0:T(8,128)S(1)} collective-permute-done((f32[2,128,128]{2,1,0:T(8,128)S(1)}, f32[2,128,128]{2,1,0:T(8,128)S(1)}, u32[]{:S(2)}, u32[]{:S(2)}) %collective-permute-start.5) | collective-permute-done | bytes 131104 | tf_op jit(solution)/shard_map/ppermute | solution.py:319
  21.2 0.8 %collective-permute-done.6.refs_3_ = f32[2,128,128]{2,1,0:T(8,128)S(1)} collective-permute-done((f32[2,128,128]{2,1,0:T(8,128)S(1)}, f32[2,128,128]{2,1,0:T(8,128)S(1)}, u32[]{:S(2)}, u32[]{:S(2)}) %collective-permute-start.6) | collective-permute-done | bytes 131104 | tf_op jit(solution)/shard_map/ppermute | solution.py:319
  22.1 1.4 %collective-permute-done.7.refs_7_ = f32[2,128,128]{2,1,0:T(8,128)S(1)} collective-permute-done((f32[2,128,128]{2,1,0:T(8,128)S(1)}, f32[2,128,128]{2,1,0:T(8,128)S(1)}, u32[]{:S(2)}, u32[]{:S(2)}) %collective-permute-start.7) | collective-permute-done | bytes 131104 | tf_op jit(solution)/shard_map/ppermute | solution.py:319
  23.5 2.7 %collective-permute-start.8 = (f32[1,128,128]{2,1,0:T(8,128)S(1)}, f32[1,128,128]{2,1,0:T(8,128)S(1)}, u32[]{:S(2)}, u32[]{:S(2)}) collective-permute-start(f32[1,128,128]{2,1,0:T(8,128)S(1)} %block_total.1), channel_id=1, source_target_pairs={{0,4},{4,0},{1,5},{5,1},{2,6},{6,2},{3,7},{7,3},{8,12},{12,8},{9,1... | collective-permute-start | bytes 196616 | tf_op jit(solution)/shard_map/ppermute | solution.py:305
  26.4 3.1 %collective-permute-done.8.passed_ref = f32[1,128,128]{2,1,0:T(8,128)S(1)} collective-permute-done((f32[1,128,128]{2,1,0:T(8,128)S(1)}, f32[1,128,128]{2,1,0:T(8,128)S(1)}, u32[]{:S(2)}, u32[]{:S(2)}) %collective-permute-start.8) | collective-permute-done | bytes 65568 | tf_op jit(solution)/shard_map/ppermute | solution.py:305
  29.8 2.6 %collective-permute-start.10 = (f32[2,128,128]{2,1,0:T(8,128)S(1)}, f32[2,128,128]{2,1,0:T(8,128)S(1)}, u32[]{:S(2)}, u32[]{:S(2)}) collective-permute-start(f32[2,128,128]{2,1,0:T(8,128)S(1)} %get-tuple-element.106), channel_id=1, source_target_pairs={{0,3},{1,2},{2,1},{3,0},{16,19},{17,18},{18,17},{19,16},{4,7},{5,6... | collective-permute-start | bytes 393224 | tf_op jit(solution)/shard_map/ppermute | solution.py:319
  32.8 1.8 %collective-permute-start.12 = (f32[2,128,128]{2,1,0:T(8,128)S(1)}, f32[2,128,128]{2,1,0:T(8,128)S(1)}, u32[]{:S(2)}, u32[]{:S(2)}) collective-permute-start(f32[2,128,128]{2,1,0:T(8,128)S(1)} %get-tuple-element.108), channel_id=1, source_target_pairs={{0,18},{1,19},{2,16},{3,17},{16,2},{17,3},{18,0},{19,1},{4,22},{5,... | collective-permute-start | bytes 393224 | tf_op jit(solution)/shard_map/ppermute | solution.py:319
  34.9 2.0 %collective-permute-done.9.refs_1_.refs_2_ = f32[2,128,128]{2,1,0:T(8,128)S(1)} collective-permute-done((f32[2,128,128]{2,1,0:T(8,128)S(1)}, f32[2,128,128]{2,1,0:T(8,128)S(1)}, u32[]{:S(2)}, u32[]{:S(2)}) %collective-permute-start.9) | collective-permute-done | bytes 131104 | tf_op jit(solution)/shard_map/ppermute | solution.py:319
  36.9 0.6 %collective-permute-start.14 = (f32[2,128,128]{2,1,0:T(8,128)S(1)}, f32[2,128,128]{2,1,0:T(8,128)S(1)}, u32[]{:S(2)}, u32[]{:S(2)}) collective-permute-start(f32[2,128,128]{2,1,0:T(8,128)S(1)} %get-tuple-element.110), channel_id=1, source_target_pairs={{0,17},{1,16},{2,19},{3,18},{16,1},{17,0},{18,3},{19,2},{4,21},{5,... | collective-permute-start | bytes 393224 | tf_op jit(solution)/shard_map/ppermute | solution.py:319
  37.6 2.0 %collective-permute-start.15 = (f32[2,128,128]{2,1,0:T(8,128)S(1)}, f32[2,128,128]{2,1,0:T(8,128)S(1)}, u32[]{:S(2)}, u32[]{:S(2)}) collective-permute-start(f32[2,128,128]{2,1,0:T(8,128)S(1)} %get-tuple-element.111), channel_id=1, source_target_pairs={{0,19},{1,18},{2,17},{3,16},{16,3},{17,2},{18,1},{19,0},{4,23},{5,... | collective-permute-start | bytes 393224 | tf_op jit(solution)/shard_map/ppermute | solution.py:319
  40.2 0.6 %collective-permute-done.13.refs_4_.refs_5_ = f32[2,128,128]{2,1,0:T(8,128)S(1)} collective-permute-done((f32[2,128,128]{2,1,0:T(8,128)S(1)}, f32[2,128,128]{2,1,0:T(8,128)S(1)}, u32[]{:S(2)}, u32[]{:S(2)}) %collective-permute-start.13) | collective-permute-done | bytes 131104 | tf_op jit(solution)/shard_map/ppermute | solution.py:319
  40.8 2.1 %collective-permute-done.14.refs_3_.refs_4_ = f32[2,128,128]{2,1,0:T(8,128)S(1)} collective-permute-done((f32[2,128,128]{2,1,0:T(8,128)S(1)}, f32[2,128,128]{2,1,0:T(8,128)S(1)}, u32[]{:S(2)}, u32[]{:S(2)}) %collective-permute-start.14) | collective-permute-done | bytes 131104 | tf_op jit(solution)/shard_map/ppermute | solution.py:319
  42.9 1.5 %collective-permute-done.15.refs_7_.refs_8_ = f32[2,128,128]{2,1,0:T(8,128)S(1)} collective-permute-done((f32[2,128,128]{2,1,0:T(8,128)S(1)}, f32[2,128,128]{2,1,0:T(8,128)S(1)}, u32[]{:S(2)}, u32[]{:S(2)}) %collective-permute-start.15) | collective-permute-done | bytes 131104 | tf_op jit(solution)/shard_map/ppermute | solution.py:319
  44.6 2.0 %block_outputs.2 = (bf16[128,2048]{1,0:T(8,128)(2,1)}, bf16[128,2048]{1,0:T(8,128)(2,1)}, bf16[128,2048]{1,0:T(8,128)(2,1)}, bf16[128,2048]{1,0:T(8,128)(2,1)}) custom-call(s32[1]{0:T(128)} %bitcast.refs_0_._.core, s32[1]{0:T(128)} %bitcast.1.refs_1_.me.__, s32[1]{0:T(128)} %bitcast.2.refs_2_.__.group._, ...), custom_call_target="tpu_custom_call" | custom-call | flops 268435456 | bytes 3145728 | tf_op jit(solution)/shard_map/block_outputs/pallas_call | solution.py:270
  46.6 0.7 %collective-permute-done.16.refs_0_ = f32[8,2,128,128]{3,2,1,0:T(8,128)S(1)} collective-permute-done((f32[8,2,128,128]{3,2,1,0:T(8,128)S(1)}, f32[8,2,128,128]{3,2,1,0:T(8,128)S(1)}, u32[]{:S(2)}, u32[]{:S(2)}) %collective-permute-start.16) | collective-permute-done | bytes 1048608 | tf_op jit(solution)/shard_map/ppermute | solution.py:305
  47.3 1.9 %block_outputs.3 = (bf16[128,2048]{1,0:T(8,128)(2,1)}, bf16[128,2048]{1,0:T(8,128)(2,1)}, bf16[128,2048]{1,0:T(8,128)(2,1)}, bf16[128,2048]{1,0:T(8,128)(2,1)}) custom-call(s32[1]{0:T(128)} %bitcast.refs_0_._.core, s32[1]{0:T(128)} %bitcast.1.refs_1_.me.__, ...), custom_call_target="tpu_custom_call", output_to_operand_aliasing={{0}: (8, {}), {1}: (9, {}), {2}: (10, {}), {3}: (11, {})} | custom-call | flops 268435456 | bytes 3145728 | tf_op jit(solution)/shard_map/block_outputs/pallas_call | solution.py:270
  (28 shorter events, 3.7 us)
Async XLA Ops:
  2.4 2.8 %collective-permute-start = (f32[8,2,128,128]{3,2,1,0:T(8,128)S(1)}, f32[8,2,128,128]{3,2,1,0:T(8,128)S(1)}, u32[]{:S(2)}, u32[]{:S(2)}) collective-permute-start(f32[8,2,128,128]{3,2,1,0:T(8,128)S(1)} %get-tuple-element.66), channel_id=1, source_target_pairs={{0,8},{8,0},{1,9},{9,1},{2,10},{10,2},{3,11},{11,3},{4,12},{12,4},... | collective-permute-start | bytes 3145736 | tf_op jit(solution)/shard_map/ppermute | solution.py:305
  3.0 15.1 %copy-start = (bf16[128,2048]{1,0:T(8,128)(2,1)S(1)}, bf16[128,2048]{1,0:T(8,128)(2,1)}, u32[]{:S(2)}) copy-start(bf16[128,2048]{1,0:T(8,128)(2,1)} %q_ref.1) | copy-start | bytes 1572868
  3.0 15.1 %copy-start.1 = (bf16[128,2048]{1,0:T(8,128)(2,1)S(1)}, bf16[128,2048]{1,0:T(8,128)(2,1)}, u32[]{:S(2)}) copy-start(bf16[128,2048]{1,0:T(8,128)(2,1)} %k_ref.1) | copy-start | bytes 1572868
  3.0 15.1 %copy-start.2 = (bf16[128,2048]{1,0:T(8,128)(2,1)S(1)}, bf16[128,2048]{1,0:T(8,128)(2,1)}, u32[]{:S(2)}) copy-start(bf16[128,2048]{1,0:T(8,128)(2,1)} %v_ref.1) | copy-start | bytes 1572868
  3.0 15.1 %copy-start.3 = (bf16[128,2048]{1,0:T(8,128)(2,1)S(1)}, bf16[128,2048]{1,0:T(8,128)(2,1)}, u32[]{:S(2)}) copy-start(bf16[128,2048]{1,0:T(8,128)(2,1)} %g_ref.1) | copy-start | bytes 1572868
  5.4 8.0 %collective-permute-start.1 = (f32[2,128,128]{2,1,0:T(8,128)S(1)}, f32[2,128,128]{2,1,0:T(8,128)S(1)}, u32[]{:S(2)}, u32[]{:S(2)}) collective-permute-start(f32[2,128,128]{2,1,0:T(8,128)S(1)} %get-tuple-element.75), channel_id=1, source_target_pairs={{0,16},{1,17},{2,18},{3,19},{16,0},{17,1},{18,2},{19,3},{4,20},{5,... | collective-permute-start | bytes 393224 | tf_op jit(solution)/shard_map/ppermute | solution.py:319
  8.3 7.5 %collective-permute-start.2 = (f32[2,128,128]{2,1,0:T(8,128)S(1)}, f32[2,128,128]{2,1,0:T(8,128)S(1)}, u32[]{:S(2)}, u32[]{:S(2)}) collective-permute-start(f32[2,128,128]{2,1,0:T(8,128)S(1)} %get-tuple-element.76), channel_id=1, source_target_pairs={{0,3},{1,2},{2,1},{3,0},{16,19},{17,18},{18,17},{19,16},{4,7},{5,6... | collective-permute-start | bytes 393224 | tf_op jit(solution)/shard_map/ppermute | solution.py:319
  10.8 8.9 %collective-permute-start.3 = (f32[2,128,128]{2,1,0:T(8,128)S(1)}, f32[2,128,128]{2,1,0:T(8,128)S(1)}, u32[]{:S(2)}, u32[]{:S(2)}) collective-permute-start(f32[2,128,128]{2,1,0:T(8,128)S(1)} %get-tuple-element.77), channel_id=1, source_target_pairs={{0,1},{1,0},{2,3},{3,2},{16,17},{17,16},{18,19},{19,18},{4,5},{5,4... | collective-permute-start | bytes 393224 | tf_op jit(solution)/shard_map/ppermute | solution.py:319
  11.3 8.4 %collective-permute-start.4 = (f32[2,128,128]{2,1,0:T(8,128)S(1)}, f32[2,128,128]{2,1,0:T(8,128)S(1)}, u32[]{:S(2)}, u32[]{:S(2)}) collective-permute-start(f32[2,128,128]{2,1,0:T(8,128)S(1)} %get-tuple-element.78), channel_id=1, source_target_pairs={{0,18},{1,19},{2,16},{3,17},{16,2},{17,3},{18,0},{19,1},{4,22},{5,... | collective-permute-start | bytes 393224 | tf_op jit(solution)/shard_map/ppermute | solution.py:319
  11.4 9.9 %collective-permute-start.5 = (f32[2,128,128]{2,1,0:T(8,128)S(1)}, f32[2,128,128]{2,1,0:T(8,128)S(1)}, u32[]{:S(2)}, u32[]{:S(2)}) collective-permute-start(f32[2,128,128]{2,1,0:T(8,128)S(1)} %get-tuple-element.79), channel_id=1, source_target_pairs={{0,2},{1,3},{2,0},{3,1},{16,18},{17,19},{18,16},{19,17},{4,6},{5,7... | collective-permute-start | bytes 393224 | tf_op jit(solution)/shard_map/ppermute | solution.py:319
  13.3 8.8 %collective-permute-start.6 = (f32[2,128,128]{2,1,0:T(8,128)S(1)}, f32[2,128,128]{2,1,0:T(8,128)S(1)}, u32[]{:S(2)}, u32[]{:S(2)}) collective-permute-start(f32[2,128,128]{2,1,0:T(8,128)S(1)} %get-tuple-element.80), channel_id=1, source_target_pairs={{0,17},{1,16},{2,19},{3,18},{16,1},{17,0},{18,3},{19,2},{4,21},{5,... | collective-permute-start | bytes 393224 | tf_op jit(solution)/shard_map/ppermute | solution.py:319
  15.8 7.7 %collective-permute-start.7 = (f32[2,128,128]{2,1,0:T(8,128)S(1)}, f32[2,128,128]{2,1,0:T(8,128)S(1)}, u32[]{:S(2)}, u32[]{:S(2)}) collective-permute-start(f32[2,128,128]{2,1,0:T(8,128)S(1)} %get-tuple-element.81), channel_id=1, source_target_pairs={{0,19},{1,18},{2,17},{3,16},{16,3},{17,2},{18,1},{19,0},{4,23},{5,... | collective-permute-start | bytes 393224 | tf_op jit(solution)/shard_map/ppermute | solution.py:319
  23.5 5.9 %collective-permute-start.8 = (f32[1,128,128]{2,1,0:T(8,128)S(1)}, f32[1,128,128]{2,1,0:T(8,128)S(1)}, u32[]{:S(2)}, u32[]{:S(2)}) collective-permute-start(f32[1,128,128]{2,1,0:T(8,128)S(1)} %block_total.1), channel_id=1, source_target_pairs={{0,4},{4,0},{1,5},{5,1},{2,6},{6,2},{3,7},{7,3},{8,12},{12,8},{9,1... | collective-permute-start | bytes 196616 | tf_op jit(solution)/shard_map/ppermute | solution.py:305
  29.6 7.3 %collective-permute-start.9 = (f32[2,128,128]{2,1,0:T(8,128)S(1)}, f32[2,128,128]{2,1,0:T(8,128)S(1)}, u32[]{:S(2)}, u32[]{:S(2)}) collective-permute-start(f32[2,128,128]{2,1,0:T(8,128)S(1)} %get-tuple-element.105), channel_id=1, source_target_pairs={{0,16},{1,17},{2,18},{3,19},{16,0},{17,1},{18,2},{19,3},{4,20},{5,... | collective-permute-start | bytes 393224 | tf_op jit(solution)/shard_map/ppermute | solution.py:319
  29.8 7.9 %collective-permute-start.10 = (f32[2,128,128]{2,1,0:T(8,128)S(1)}, f32[2,128,128]{2,1,0:T(8,128)S(1)}, u32[]{:S(2)}, u32[]{:S(2)}) collective-permute-start(f32[2,128,128]{2,1,0:T(8,128)S(1)} %get-tuple-element.106), channel_id=1, source_target_pairs={{0,3},{1,2},{2,1},{3,0},{16,19},{17,18},{18,17},{19,16},{4,7},{5,6... | collective-permute-start | bytes 393224 | tf_op jit(solution)/shard_map/ppermute | solution.py:319
  32.3 7.3 %collective-permute-start.11 = (f32[2,128,128]{2,1,0:T(8,128)S(1)}, f32[2,128,128]{2,1,0:T(8,128)S(1)}, u32[]{:S(2)}, u32[]{:S(2)}) collective-permute-start(f32[2,128,128]{2,1,0:T(8,128)S(1)} %get-tuple-element.107), channel_id=1, source_target_pairs={{0,1},{1,0},{2,3},{3,2},{16,17},{17,16},{18,19},{19,18},{4,5},{5,4... | collective-permute-start | bytes 393224 | tf_op jit(solution)/shard_map/ppermute | solution.py:319
  32.8 7.4 %collective-permute-start.12 = (f32[2,128,128]{2,1,0:T(8,128)S(1)}, f32[2,128,128]{2,1,0:T(8,128)S(1)}, u32[]{:S(2)}, u32[]{:S(2)}) collective-permute-start(f32[2,128,128]{2,1,0:T(8,128)S(1)} %get-tuple-element.108), channel_id=1, source_target_pairs={{0,18},{1,19},{2,16},{3,17},{16,2},{17,3},{18,0},{19,1},{4,22},{5,... | collective-permute-start | bytes 393224 | tf_op jit(solution)/shard_map/ppermute | solution.py:319
  34.6 6.2 %collective-permute-start.13 = (f32[2,128,128]{2,1,0:T(8,128)S(1)}, f32[2,128,128]{2,1,0:T(8,128)S(1)}, u32[]{:S(2)}, u32[]{:S(2)}) collective-permute-start(f32[2,128,128]{2,1,0:T(8,128)S(1)} %get-tuple-element.109), channel_id=1, source_target_pairs={{0,2},{1,3},{2,0},{3,1},{16,18},{17,19},{18,16},{19,17},{4,6},{5,7... | collective-permute-start | bytes 393224 | tf_op jit(solution)/shard_map/ppermute | solution.py:319
  36.9 6.0 %collective-permute-start.14 = (f32[2,128,128]{2,1,0:T(8,128)S(1)}, f32[2,128,128]{2,1,0:T(8,128)S(1)}, u32[]{:S(2)}, u32[]{:S(2)}) collective-permute-start(f32[2,128,128]{2,1,0:T(8,128)S(1)} %get-tuple-element.110), channel_id=1, source_target_pairs={{0,17},{1,16},{2,19},{3,18},{16,1},{17,0},{18,3},{19,2},{4,21},{5,... | collective-permute-start | bytes 393224 | tf_op jit(solution)/shard_map/ppermute | solution.py:319
  37.6 6.8 %collective-permute-start.15 = (f32[2,128,128]{2,1,0:T(8,128)S(1)}, f32[2,128,128]{2,1,0:T(8,128)S(1)}, u32[]{:S(2)}, u32[]{:S(2)}) collective-permute-start(f32[2,128,128]{2,1,0:T(8,128)S(1)} %get-tuple-element.111), channel_id=1, source_target_pairs={{0,19},{1,18},{2,17},{3,16},{16,3},{17,2},{18,1},{19,0},{4,23},{5,... | collective-permute-start | bytes 393224 | tf_op jit(solution)/shard_map/ppermute | solution.py:319
  44.5 2.7 %collective-permute-start.16 = (f32[8,2,128,128]{3,2,1,0:T(8,128)S(1)}, f32[8,2,128,128]{3,2,1,0:T(8,128)S(1)}, u32[]{:S(2)}, u32[]{:S(2)}) collective-permute-start(f32[8,2,128,128]{3,2,1,0:T(8,128)S(1)} %sibling_state.1), channel_id=1, source_target_pairs={{0,8},{8,0},{1,9},{9,1},{2,10},{10,2},{3,11},{11,3},{4,12},{12,4},... | collective-permute-start | bytes 3145736 | tf_op jit(solution)/shard_map/ppermute | solution.py:305

commit v5 on v4

v5 whole, which is shorter than its diff:
```python
import functools
import itertools
import math

import jax
import jax.numpy as jnp
from jax import lax
from jax.experimental import pallas as pl
from jax.experimental.pallas import tpu as pltpu
from jax.sharding import Mesh, PartitionSpec as P

D = 128
F32 = jnp.float32
BF16 = jnp.bfloat16
VMEM_LIMIT = 20 * 1024 * 1024
HBM = pl.BlockSpec(memory_space=pltpu.HBM)
VMEM = pl.BlockSpec(memory_space=pltpu.VMEM)
SMEM = pl.BlockSpec(memory_space=pltpu.SMEM)


def in_vmem(shape, dtype=F32):
    return pltpu.VMEM(shape, dtype)


def call(body, out_shape, in_specs, out_specs, scratch, flops, moved, name, aliases=None):
    return pl.pallas_call(
        body,
        out_shape=out_shape,
        in_specs=in_specs,
        out_specs=out_specs,
        scratch_shapes=scratch,
        input_output_aliases=aliases or {},
        compiler_params=pltpu.CompilerParams(vmem_limit_bytes=VMEM_LIMIT),
        cost_estimate=pl.CostEstimate(flops=flops, bytes_accessed=moved, transcendentals=0),
        name=name,
    )


def rotate(rows, cosine, sine):
    wide = rows.astype(F32)
    return wide * cosine + pltpu.roll(wide, D // 2, 1) * sine


def unrotate(rows, cosine, sine):
    return rows * cosine - pltpu.roll(rows, D // 2, 1) * sine


def dot(a, b, ca, cb):
    return lax.dot_general(a, b, (((ca,), (cb,)), ((), ())), preferred_element_type=F32)


def rotary_tables(positions):
    rows = positions.shape[1]
    half = D // 2
    lane = lax.broadcasted_iota(jnp.int32, (rows, D), 1)
    index = jnp.where(lane < half, lane, lane - half).astype(F32)
    frequency = jnp.exp(index * (-2.0 * math.log(500000.0) / D))
    place = jnp.broadcast_to(positions.astype(F32), (D, rows)).T
    angle = place * frequency
    sine = jnp.sin(angle)
    return jnp.cos(angle), jnp.where(lane < half, -sine, sine)


def states_body(first, per, sets, _, me, __, core, *refs):
    half, me = core[0], me[0]
    if first:
        pos, *sources = refs[:5]
        cos_ref, sin_ref, *nearby = refs[5:11]
        outs, (place, *inputs), sems = refs[11:13], refs[13:18], refs[18]
        width = inputs[0].shape[1]
        pos_copy = pltpu.make_async_copy(pos, place, sems.at[8])
        pos_copy.start()
        copies = []
        for n, (at, targets) in enumerate(((1 - half, inputs), (half, nearby))):
            start = pl.multiple_of(at * width, width)
            for i, (source, target) in enumerate(zip(sources, targets)):
                copies.append(pltpu.make_async_copy(source.at[:, pl.ds(start, width)], target, sems.at[4 * n + i]))
                copies[-1].start()
        pos_copy.wait()
        cosine, sine = rotary_tables(place[...])
        cos_ref[...] = cosine
        sin_ref[...] = sine
    else:
        cos_ref, sin_ref, *inputs = refs[:6]
        outs = refs[6:]
        cosine, sine = cos_ref[...], sin_ref[...]
    low = me % per
    for side in range(2):
        rows, others = inputs[2 * side : 2 * side + 2]
        if first:
            copies[2 * side].wait()
            copies[2 * side + 1].wait()
        for group, out in zip(sets, outs):
            cut = out.shape[2]
            for n, mask in enumerate(group):
                cols = pl.ds(pl.multiple_of(((me // per) ^ mask) * D, D), D)
                turned = rotate(rows[:, cols], cosine, sine).astype(BF16)
                state = dot(turned, others[:, cols], 0, 0)
                for i in range(per):
                    out[n * per + (low ^ i), side] = state[i * cut : (i + 1) * cut]
    if first:
        for copy in copies[4:]:
            copy.wait()


def states(who, first, per, sets, sources, tables_or_pos):
    rows, width = sources[0].shape
    heads = sum(map(len, sets))
    table = in_vmem((rows, D))
    results = [in_vmem((len(group) * per, 2, D // per, D)) for group in sets]
    body = functools.partial(states_body, first, per, sets)
    work = (4 * heads * rows * D * D, heads * D * (8 * rows + 8 * D))
    if first:
        piece = (rows, heads * D)
        scratch = [pltpu.VMEM((1, rows), jnp.int32)] + [pltpu.VMEM(piece, BF16)] * 4 + [pltpu.SemaphoreType.DMA((9,))]
        out = call(
            body, [table] * 2 + [in_vmem(piece, BF16)] * 4 + results, [SMEM] * 4 + [HBM] * 5, [VMEM] * 8,
            scratch, *work, "block_states",
        )(*who, tables_or_pos, *sources)
        return out[:2], out[2:6], out[6:]
    return call(body, results, [SMEM] * 4 + [VMEM] * 6, [VMEM] * 2, [], *work, "block_states")(
        *who, *tables_or_pos, *sources
    )


def add_body(a_ref, b_ref, *pieces):
    for n, piece in enumerate(pieces):
        piece[...] = a_ref[n] + b_ref[n]


def add(a, b):
    count, _, cut, _ = a.shape
    return call(
        add_body, [in_vmem((2, cut, D))] * count, [VMEM] * 2, [VMEM] * count, [], a.size, a.size * 12, "chip_sum",
    )(a, b)


def total_body(_, __, group, ___, *refs):
    group = group[0]
    out_ref = refs[-1]
    for side in range(2):
        total = refs[0][side]
        for ref in refs[1:-1]:
            total = total + ref[side]
        if out_ref.shape[0] == 2:
            out_ref[side] = total
        elif side == 0:
            keys = total
        else:
            out_ref[0] = jnp.where(group == 0, keys, total)


def total(who, pieces, kinds):
    _, cut, _ = pieces[0].shape
    size = len(pieces) * pieces[0].size
    return call(
        total_body, in_vmem((kinds, cut, D)), [SMEM] * 4 + [VMEM] * len(pieces), VMEM, [], size, size * 4, "block_total",
    )(*who, *pieces)


def offset_body(members, _, __, group, ___, passed_ref, *refs):
    group = group[0]
    for side in range(2):
        if passed_ref.shape[0] == 1:
            extra = jnp.where(group == 1 - side, passed_ref[0], 0.0)
        else:
            extra = passed_ref[side]
        for m in range(members):
            refs[members + m][side] = refs[m][side] + extra


def offset(who, sums, passed):
    members = len(sums)
    size = members * sums[0].size
    return call(
        functools.partial(offset_body, members), [in_vmem(sums[0].shape)] * members,
        [SMEM] * 4 + [VMEM] * (members + 1), [VMEM] * members, [], size, size * 8, "group_sum",
    )(*who, passed, *sums)


def scan_body(members, _, me, __, ___, *refs):
    pieces, sums, (held, ran) = refs[:members], refs[members : 2 * members], refs[2 * members :]
    me = me[0]
    for m in range(members):
        held[me ^ m] = pieces[m][...]
    for side, order in enumerate((range(members), reversed(range(members)))):
        total = jnp.zeros(held.shape[2:], F32)
        for j in order:
            ran[j, side] = total
            total = total + held[j, side]
    for m in range(members):
        sums[m][...] = ran[me ^ m]


def scan(who, pieces):
    members, (_, cut, _) = len(pieces), pieces[0].shape
    shape = (members, 2, cut, D)
    size = math.prod(shape)
    return call(
        functools.partial(scan_body, members), [in_vmem((2, cut, D))] * members,
        [SMEM] * 4 + [VMEM] * members, [VMEM] * members, [pltpu.VMEM(shape, F32)] * 2, size, size * 8, "chip_scan",
    )(*who, *pieces)


def local_body(q_ref, k_ref, v_ref, g_ref, cos_ref, sin_ref, rot_ref, part_ref, sc_ref):
    cosine, sine = cos_ref[...], sin_ref[...]
    rows = q_ref.shape[0]
    row = lax.broadcasted_iota(jnp.int32, (rows, rows), 0)
    col = lax.broadcasted_iota(jnp.int32, (rows, rows), 1)

    def scores(a, b, kept):
        return jnp.where(kept, dot(a, b, 1, 1), 0.0).astype(BF16)

    for h in range(rot_ref.shape[0]):
        cols = slice(h * D, (h + 1) * D)
        krot = rotate(k_ref[:, cols], cosine, sine).astype(BF16)
        qrot = rotate(q_ref[:, cols], cosine, sine).astype(BF16)
        v, g = v_ref[:, cols], g_ref[:, cols]
        for i, value in enumerate((qrot, g, v, krot)):
            rot_ref[h, i] = value
        sc_ref[h, 0] = scores(qrot, krot, row >= col)
        sc_ref[h, 1] = scores(g, v, row >= col)
        sc_ref[h, 2] = scores(v, g, row <= col)
        sc_ref[h, 3] = scores(krot, qrot, row <= col)
    for h in range(rot_ref.shape[0]):
        for i, other in enumerate((2, 3, 0, 1)):
            part_ref[h, i] = dot(sc_ref[h, i], rot_ref[h, other], 1, 0)


def local_parts(q, k, v, g, cosine, sine, heads):
    rows = q.shape[0]
    return call(
        local_body,
        [in_vmem((heads, 4, rows, D), BF16), in_vmem((heads, 4, rows, D))],
        [VMEM] * 6, [VMEM] * 2, [pltpu.VMEM((heads, 4, rows, rows), BF16)], 16 * heads * rows * D * D, 16 * rows * heads * D * 2, "local_parts",
    )(q, k, v, g, cosine, sine)


def outputs_body(scale, per, heads, far, spots, core, me, _, __, rot_ref, part_ref, cos_ref, sin_ref, *refs):
    core, me = core[0], me[0]
    count = heads * per
    if far:
        pieces, refs = refs[:1], refs[5:]
    else:
        extras, pieces, refs = refs[:2], refs[2 : 2 + count], refs[2 + count :]
    outs, (state_ref, held, sems) = refs[:4], refs[4:]
    cosine, sine = cos_ref[...], sin_ref[...]
    copies = []
    for n in range(heads):
        low = me % per
        head = (me // per) ^ n
        for i in range(per):
            cut = pieces[0].shape[-2]
            at = pl.ds(pl.multiple_of((low ^ i) * cut, cut), cut)
            for side in range(2):
                if far:
                    state = pieces[0][n * per + i, side]
                else:
                    which, spot = spots[n]
                    extra = extras[which][spot * per + i, side]
                    state = pieces[n * per + i][side] + jnp.where(core == 1 - side, extra, 0.0)
                state_ref[n, side, at] = state.astype(BF16)
        before, after = state_ref[n, 0], state_ref[n, 1]
        at = (1 - core if far else core) * heads + head
        att = part_ref[at, 0] + dot(rot_ref[at, 0], before, 1, 0)
        rqg = part_ref[at, 1] + dot(rot_ref[at, 1], before, 1, 1)
        rkg = part_ref[at, 2] + dot(rot_ref[at, 2], after, 1, 1)
        vg = part_ref[at, 3] + dot(rot_ref[at, 3], after, 1, 0)
        held[n, 0] = (scale * att).astype(BF16)
        held[n, 1] = unrotate(scale * rqg, cosine, sine).astype(BF16)
        held[n, 2] = unrotate(scale * rkg, cosine, sine).astype(BF16)
        held[n, 3] = (scale * vg).astype(BF16)
        for i in range(4):
            cols = pl.ds(pl.multiple_of(at * D, D), D)
            copies.append(pltpu.make_async_copy(held.at[n, i], outs[i].at[:, cols], sems.at[n, i]))
            copies[-1].start()
    for copy in copies:
        copy.wait()


def outputs(scale, per, count, spots, who, rot, local, tables, extra, pieces, prior):
    heads, _, rows, _ = rot.shape
    far = extra is None
    pieces = list(pieces) if far else [*extra, *pieces]
    return call(
        functools.partial(outputs_body, scale, per, count, far, spots),
        [pltpu.HBM((rows, heads * D), BF16)] * 4,
        [SMEM] * 4 + [VMEM] * (4 + len(pieces)) + [HBM] * len(prior),
        [HBM] * 4,
        [
            pltpu.VMEM((count, 2, D, D), BF16),
            pltpu.VMEM((count, 4, rows, D), BF16),
            pltpu.SemaphoreType.DMA((count, 4)),
        ],
        8 * count * rows * D * D,
        16 * rows * count * D * 2,
        "block_outputs",
        {8 + len(pieces) + i: i for i in range(len(prior))},
    )(*who, rot, local, *tables, *pieces, *prior)


def relay_body(per, spots, core, _, __, ___, near_1, near_2, *refs):
    core = core[0]
    out_ref = refs[-1]
    for m in range(out_ref.shape[0]):
        which, spot = spots[m // per]
        near = (near_1, near_2)[which]
        for side in range(2):
            out_ref[m, side] = refs[m][side] + jnp.where(core == side, near[spot * per + m % per, side], 0.0)


def relay(per, spots, who, near, pieces):
    size = len(pieces) * pieces[0].size
    return call(
        functools.partial(relay_body, per, spots), in_vmem((len(pieces),) + pieces[0].shape),
        [SMEM] * 4 + [VMEM] * (2 + len(pieces)), VMEM, [], size, size * 8, "sibling_state",
    )(*who, *near, *pieces)


def swap(value, axis):
    return lax.ppermute(value, axis, [(0, 1), (1, 0)])


AXES = ("x", "zl", "y")


def send_to(value, mask):
    x, zl, y = (lax.axis_size(axis) for axis in AXES)
    mx, my, mz = mask % x, mask // x % y, mask // (x * y)
    place = lambda a, b, c: (a * zl + b) * y + c
    pairs = [
        (place(a, b, c), place(a ^ mx, b ^ mz, c ^ my))
        for a, b, c in itertools.product(range(x), range(zl), range(y))
    ]
    return lax.ppermute(value, AXES, pairs)


def barrier(*values):
    return lax.optimization_barrier(values)


def exchange(pieces, order):
    arrived = {m: send_to(pieces[m], m) for m in order}
    arrived[0] = pieces[0]
    return arrived


def shards(q, k, v, g, positions):
    rows, width = q.shape
    heads = width // D
    part = heads // 2
    tokens = rows
    for axis in ("x", "core", "zh", "zl", "y"):
        tokens = tokens * lax.axis_size(axis)
    scale = (D * tokens) ** (-0.5)
    core, group = lax.axis_index("core"), lax.axis_index("zh")
    members, groups = lax.axis_size(("zl", "y", "x")), lax.axis_size("zh")
    me = lax.axis_index(("zl", "y", "x"))
    who = [scalar.reshape(1) for scalar in (core, me, group, core)]
    per = members // part
    pos = positions.reshape(1, rows)

    order = []
    for m in sorted(range(1, members - 1), key=lambda m: (bin(m).count("1"), m))[: members // 2 - 1]:
        order += [m, members - 1 - m]
    order.append(members - 1)
    masks = list(dict.fromkeys([m // per for m in order] + [0]))
    sets = masks[: part // 2], masks[part // 2 :]
    spots = {mask: (which, group.index(mask)) for which, group in enumerate(sets) for mask in group}

    sources = [pltpu.with_memory_space_constraint(a, pltpu.HBM) for a in (k, v, q, g)]
    tables, nearby, far = states(who, True, per, sets, sources, pltpu.with_memory_space_constraint(pos, pltpu.HBM))
    near_other = [swap(value, "core") for value in far]
    near = states(who, False, per, sets, nearby, tables)
    summed = [add(*pair) for pair in zip(near, near_other)]
    pieces = {mask * per + i: summed[which][n * per + i] for mask, (which, n) in spots.items() for i in range(per)}
    pieces = [pieces[m] for m in range(members)]
    pieces[order[0]], tables = barrier(pieces[order[0]], tables)
    arrived = exchange(pieces, order)
    rot, local = local_parts(q, k, v, g, *tables, heads)
    listed, rot, local = barrier([arrived[m] for m in order], rot, local)
    arrived = [pieces[0]] + [listed[order.index(m)] for m in range(1, members)]

    send = total(who, arrived, 1 if groups == 2 else 2)
    if groups == 2:
        passed = swap(send, "zh")
    else:
        every = lax.all_gather(send, "zh")
        place = jnp.arange(groups)[:, None, None, None]
        wanted = jnp.where(jnp.arange(2)[:, None, None] == 0, place < group, place > group)
        passed = jnp.sum(jnp.where(wanted, every, 0.0), axis=0)
    pieces = offset(who, scan(who, arrived), passed)
    whole = exchange(pieces, order)

    whole = dict(zip([0] + order, barrier(*(whole[m] for m in [0] + order))))
    whole = [whole[m] for m in range(members)]
    other = swap(relay(per, spots, who, near, whole), "core")
    made = outputs(scale, per, part, spots, who, rot, local, tables, near_other, whole, ())
    made = outputs(scale, per, part, spots, who, rot, local, tables, None, [other], tuple(made))
    return tuple(made)


def solution(mesh):
    inner, outer = mesh.shape["inner"], mesh.shape["outer"]
    x = inner // 2
    y = x if outer % x == 0 else 1
    z = outer // y
    zl = 2 if z % 2 == 0 else 1
    whole = Mesh(mesh.devices.reshape(x, 2, z // zl, zl, y), ("x", "core", "zh", "zl", "y"))
    rows = ("zh", "zl", "y", "x", "core")
    return jax.shard_map(
        shards,
        mesh=whole,
        in_specs=(P(rows, None),) * 4 + (P(rows),),
        out_specs=(P(rows, None),) * 4,
        check_vma=False,
    )
```

time: 49.4 us -> 48.5 us (0.982)
  Pallas kernels: 9.77 us -> 8.78 us
    pallas_call x8 -> x9, Pallas kernels: 9.48 us -> 8.49 us  [the longest x2 3.38 us: outputs(): call(functools.partial(outputs_body, scale, per, count, far, spots), [plt...]
    ppermute x3 -> x4, waiting for transfers between devices: 4.1 us -> 4.8 us  [swap(): return lax.ppermute(value, axis, [(0, 1), (1, 0)])]
    ppermute x14, waiting for transfers between devices: 10.6 us -> 9.96 us  [send_to(): return lax.ppermute(value, AXES, pairs)]
    ppermute x3 -> x4, starting transfers between devices: 3.24 us -> 3.32 us  [swap(): return lax.ppermute(value, axis, [(0, 1), (1, 0)])]
  transfers between devices with their start and end apart: 17 -> 18, of which waited for: 12 -> 12; matrix products, arithmetic and copies ran while one was open for 0% -> 0% of each run, Pallas kernels for 12% -> 10%
where the time goes in v5:
time: 48.5 us; the launch traced here: 48.4 us
  starting transfers between devices  24.1 us (50%)
  waiting for transfers between devices  14.8 us (31%)
  Pallas kernels  8.78 us (18%)
  between operations  0.76 us (2%)
    ppermute x14, starting transfers between devices, send_to(): return lax.ppermute(value, AXES, pairs)  20.7 us
    ppermute x14, waiting for transfers between devices, send_to(): return lax.ppermute(value, AXES, pairs)  9.96 us
    ppermute x4, waiting for transfers between devices, swap(): return lax.ppermute(value, axis, [(0, 1), (1, 0)])  4.8 us
    pallas_call x2, Pallas kernels, outputs(): call(functools.partial(outputs_body, scale, per, count, far, spots), [plt...  3.38 us
    ppermute x4, starting transfers between devices, swap(): return lax.ppermute(value, axis, [(0, 1), (1, 0)])  3.32 us
    pallas_call x1, Pallas kernels, local_parts(): call(local_body, [in_vmem((heads, 4, rows, D), BF16), in_vmem((heads, 4,...  2.17 us
    pallas_call x1, Pallas kernels, states(): call(body, [table] * 2 + [in_vmem(piece, BF16)] * 4 + results, [SMEM] * 4...  1.99 us
  transfers between devices with their start and end apart: 18, of which 12 were waited for; matrix products, arithmetic and copies ran while one was open for 0% of the time, Pallas kernels for 10%

profile of v5, /device:TPU:0, one launch (start us, length us, event | category | flops | bytes accessed | tf_op | source)
XLA Modules:
  0.0 48.4 jit_solution(8148819236358811299)
XLA Ops:
  0.7 2.0 %block_states.2 = (f32[128,128]{1,0:T(8,128)S(1)}, f32[128,128]{1,0:T(8,128)S(1)}, bf16[128,1024]{1,0:T(8,128)(2,1)S(1)}, bf16[128,1024]{1,0:T(8,128)(2,1)S(1)},...) custom-call(s32[1]{0:T(128)} %bitcast._.core.___.__, ...), custom_call_target="tpu_custom_call" | custom-call | flops 67108864 | bytes 2097152 | tf_op jit(solution)/shard_map/block_states/pallas_call | solution.py:116
  3.3 0.7 %block_states.3 = (f32[4,2,128,128]{3,2,1,0:T(8,128)S(1)}, f32[4,2,128,128]{3,2,1,0:T(8,128)S(1)}) custom-call(s32[1]{0:T(128)} %bitcast._.core.___.__, s32[1]{0:T(128)} %bitcast.1.me.__._, s32[1]{0:T(128)} %bitcast.2.__.group._, s32[1]{0:T(128)} %bitcast._.core.___.__, f32[128,128]{1,0:T(8,128)S(1)} %get-tuple-element.82.refs_0_.cos_ref, ...), custom_call_target="tpu_custom_call" | custom-call | flops 67108864 | bytes 2097152 | tf_op jit(solution)/shard_map/block_states/pallas_call | solution.py:121
  3.9 0.8 %collective-permute-done.b_ref.refs_0_ = f32[4,2,128,128]{3,2,1,0:T(8,128)S(1)} collective-permute-done((f32[4,2,128,128]{3,2,1,0:T(8,128)S(1)}, f32[4,2,128,128]{3,2,1,0:T(8,128)S(1)}, u32[]{:S(2)}, u32[]{:S(2)}) %collective-permute-start) | collective-permute-done | bytes 524320 | tf_op jit(solution)/shard_map/ppermute | solution.py:321
  4.8 2.9 %collective-permute-start.1 = (f32[2,128,128]{2,1,0:T(8,128)S(1)}, f32[2,128,128]{2,1,0:T(8,128)S(1)}, u32[]{:S(2)}, u32[]{:S(2)}) collective-permute-start(f32[2,128,128]{2,1,0:T(8,128)S(1)} %get-tuple-element.73), channel_id=1, source_target_pairs={{0,16},{1,17},{2,18},{3,19},{16,0},{17,1},{18,2},{19,3},{4,20},{5,... | collective-permute-start | bytes 393224 | tf_op jit(solution)/shard_map/ppermute | solution.py:335
  7.7 2.5 %collective-permute-start.2 = (f32[2,128,128]{2,1,0:T(8,128)S(1)}, f32[2,128,128]{2,1,0:T(8,128)S(1)}, u32[]{:S(2)}, u32[]{:S(2)}) collective-permute-start(f32[2,128,128]{2,1,0:T(8,128)S(1)} %get-tuple-element.74), channel_id=1, source_target_pairs={{0,3},{1,2},{2,1},{3,0},{16,19},{17,18},{18,17},{19,16},{4,7},{5,6... | collective-permute-start | bytes 393224 | tf_op jit(solution)/shard_map/ppermute | solution.py:335
  10.9 2.0 %collective-permute-start.6 = (f32[2,128,128]{2,1,0:T(8,128)S(1)}, f32[2,128,128]{2,1,0:T(8,128)S(1)}, u32[]{:S(2)}, u32[]{:S(2)}) collective-permute-start(f32[2,128,128]{2,1,0:T(8,128)S(1)} %get-tuple-element.79), channel_id=1, source_target_pairs={{0,2},{1,3},{2,0},{3,1},{16,18},{17,19},{18,16},{19,17},{4,6},{5,7... | collective-permute-start | bytes 393224 | tf_op jit(solution)/shard_map/ppermute | solution.py:335
  12.9 2.4 %collective-permute-start.7 = (f32[2,128,128]{2,1,0:T(8,128)S(1)}, f32[2,128,128]{2,1,0:T(8,128)S(1)}, u32[]{:S(2)}, u32[]{:S(2)}) collective-permute-start(f32[2,128,128]{2,1,0:T(8,128)S(1)} %get-tuple-element.80), channel_id=1, source_target_pairs={{0,17},{1,16},{2,19},{3,18},{16,1},{17,0},{18,3},{19,2},{4,21},{5,... | collective-permute-start | bytes 393224 | tf_op jit(solution)/shard_map/ppermute | solution.py:335
  15.3 2.2 %collective-permute-start.8 = (f32[2,128,128]{2,1,0:T(8,128)S(1)}, f32[2,128,128]{2,1,0:T(8,128)S(1)}, u32[]{:S(2)}, u32[]{:S(2)}) collective-permute-start(f32[2,128,128]{2,1,0:T(8,128)S(1)} %get-tuple-element.81), channel_id=1, source_target_pairs={{0,19},{1,18},{2,17},{3,16},{16,3},{17,2},{18,1},{19,0},{4,23},{5,... | collective-permute-start | bytes 393224 | tf_op jit(solution)/shard_map/ppermute | solution.py:335
  17.5 2.2 %local_parts.1 = (bf16[16,4,128,128]{3,2,1,0:T(8,128)(2,1)S(1)}, f32[16,4,128,128]{3,2,1,0:T(8,128)S(1)}) custom-call(bf16[128,2048]{1,0:T(8,128)(2,1)S(1)} %copy-done, bf16[128,2048]{1,0:T(8,128)(2,1)S(1)} %copy-done.1, bf16[128,2048]{1,0:T(8,128)(2,1)S(1)} %copy-done.2, bf16[128,2048]{1,0:T(8,128)(2,1)S(1)} %copy-done.3, ...), custom_call_target="tpu_custom_call" | custom-call | flops 536870912 | bytes 8388608 | tf_op jit(solution)/shard_map/local_parts/pallas_call | solution.py:232
  19.7 1.0 %collective-permute-done.6.refs_4_ = f32[2,128,128]{2,1,0:T(8,128)S(1)} collective-permute-done((f32[2,128,128]{2,1,0:T(8,128)S(1)}, f32[2,128,128]{2,1,0:T(8,128)S(1)}, u32[]{:S(2)}, u32[]{:S(2)}) %collective-permute-start.6) | collective-permute-done | bytes 131104 | tf_op jit(solution)/shard_map/ppermute | solution.py:335
  20.7 0.8 %collective-permute-done.7.refs_3_ = f32[2,128,128]{2,1,0:T(8,128)S(1)} collective-permute-done((f32[2,128,128]{2,1,0:T(8,128)S(1)}, f32[2,128,128]{2,1,0:T(8,128)S(1)}, u32[]{:S(2)}, u32[]{:S(2)}) %collective-permute-start.7) | collective-permute-done | bytes 131104 | tf_op jit(solution)/shard_map/ppermute | solution.py:335
  21.5 1.4 %collective-permute-done.8.refs_7_ = f32[2,128,128]{2,1,0:T(8,128)S(1)} collective-permute-done((f32[2,128,128]{2,1,0:T(8,128)S(1)}, f32[2,128,128]{2,1,0:T(8,128)S(1)}, u32[]{:S(2)}, u32[]{:S(2)}) %collective-permute-start.8) | collective-permute-done | bytes 131104 | tf_op jit(solution)/shard_map/ppermute | solution.py:335
  23.0 2.7 %collective-permute-start.9 = (f32[1,128,128]{2,1,0:T(8,128)S(1)}, f32[1,128,128]{2,1,0:T(8,128)S(1)}, u32[]{:S(2)}, u32[]{:S(2)}) collective-permute-start(f32[1,128,128]{2,1,0:T(8,128)S(1)} %block_total.1), channel_id=1, source_target_pairs={{0,4},{4,0},{1,5},{5,1},{2,6},{6,2},{3,7},{7,3},{8,12},{12,8},{9,1... | collective-permute-start | bytes 196616 | tf_op jit(solution)/shard_map/ppermute | solution.py:321
  25.9 3.1 %collective-permute-done.9.passed_ref = f32[1,128,128]{2,1,0:T(8,128)S(1)} collective-permute-done((f32[1,128,128]{2,1,0:T(8,128)S(1)}, f32[1,128,128]{2,1,0:T(8,128)S(1)}, u32[]{:S(2)}, u32[]{:S(2)}) %collective-permute-start.9) | collective-permute-done | bytes 65568 | tf_op jit(solution)/shard_map/ppermute | solution.py:321
  29.2 2.6 %collective-permute-start.11 = (f32[2,128,128]{2,1,0:T(8,128)S(1)}, f32[2,128,128]{2,1,0:T(8,128)S(1)}, u32[]{:S(2)}, u32[]{:S(2)}) collective-permute-start(f32[2,128,128]{2,1,0:T(8,128)S(1)} %get-tuple-element.106), channel_id=1, source_target_pairs={{0,3},{1,2},{2,1},{3,0},{16,19},{17,18},{18,17},{19,16},{4,7},{5,6... | collective-permute-start | bytes 393224 | tf_op jit(solution)/shard_map/ppermute | solution.py:335
  32.2 1.8 %collective-permute-start.13 = (f32[2,128,128]{2,1,0:T(8,128)S(1)}, f32[2,128,128]{2,1,0:T(8,128)S(1)}, u32[]{:S(2)}, u32[]{:S(2)}) collective-permute-start(f32[2,128,128]{2,1,0:T(8,128)S(1)} %get-tuple-element.108), channel_id=1, source_target_pairs={{0,18},{1,19},{2,16},{3,17},{16,2},{17,3},{18,0},{19,1},{4,22},{5,... | collective-permute-start | bytes 393224 | tf_op jit(solution)/shard_map/ppermute | solution.py:335
  34.4 2.0 %collective-permute-done.10.refs_1_.refs_3_ = f32[2,128,128]{2,1,0:T(8,128)S(1)} collective-permute-done((f32[2,128,128]{2,1,0:T(8,128)S(1)}, f32[2,128,128]{2,1,0:T(8,128)S(1)}, u32[]{:S(2)}, u32[]{:S(2)}) %collective-permute-start.10) | collective-permute-done | bytes 131104 | tf_op jit(solution)/shard_map/ppermute | solution.py:335
  36.3 0.7 %collective-permute-start.15 = (f32[2,128,128]{2,1,0:T(8,128)S(1)}, f32[2,128,128]{2,1,0:T(8,128)S(1)}, u32[]{:S(2)}, u32[]{:S(2)}) collective-permute-start(f32[2,128,128]{2,1,0:T(8,128)S(1)} %get-tuple-element.110), channel_id=1, source_target_pairs={{0,17},{1,16},{2,19},{3,18},{16,1},{17,0},{18,3},{19,2},{4,21},{5,... | collective-permute-start | bytes 393224 | tf_op jit(solution)/shard_map/ppermute | solution.py:335
  37.1 2.0 %collective-permute-start.16 = (f32[2,128,128]{2,1,0:T(8,128)S(1)}, f32[2,128,128]{2,1,0:T(8,128)S(1)}, u32[]{:S(2)}, u32[]{:S(2)}) collective-permute-start(f32[2,128,128]{2,1,0:T(8,128)S(1)} %get-tuple-element.111), channel_id=1, source_target_pairs={{0,19},{1,18},{2,17},{3,16},{16,3},{17,2},{18,1},{19,0},{4,23},{5,... | collective-permute-start | bytes 393224 | tf_op jit(solution)/shard_map/ppermute | solution.py:335
  40.2 2.1 %collective-permute-done.15.refs_3_.refs_5_ = f32[2,128,128]{2,1,0:T(8,128)S(1)} collective-permute-done((f32[2,128,128]{2,1,0:T(8,128)S(1)}, f32[2,128,128]{2,1,0:T(8,128)S(1)}, u32[]{:S(2)}, u32[]{:S(2)}) %collective-permute-start.15) | collective-permute-done | bytes 131104 | tf_op jit(solution)/shard_map/ppermute | solution.py:335
  42.3 1.5 %collective-permute-done.16.refs_7_.refs_9_ = f32[2,128,128]{2,1,0:T(8,128)S(1)} collective-permute-done((f32[2,128,128]{2,1,0:T(8,128)S(1)}, f32[2,128,128]{2,1,0:T(8,128)S(1)}, u32[]{:S(2)}, u32[]{:S(2)}) %collective-permute-start.16) | collective-permute-done | bytes 131104 | tf_op jit(solution)/shard_map/ppermute | solution.py:335
  44.1 1.7 %block_outputs.2 = (bf16[128,2048]{1,0:T(8,128)(2,1)}, bf16[128,2048]{1,0:T(8,128)(2,1)}, bf16[128,2048]{1,0:T(8,128)(2,1)}, bf16[128,2048]{1,0:T(8,128)(2,1)}) custom-call(s32[1]{0:T(128)} %bitcast._.core.___.__, s32[1]{0:T(128)} %bitcast.1.me.__._, s32[1]{0:T(128)} %bitcast.2.__.group._, s32[1]{0:T(128)} %bitcast._.core.___.__, ...), custom_call_target="tpu_custom_call" | custom-call | flops 134217728 | bytes 4194304 | tf_op jit(solution)/shard_map/block_outputs/pallas_call | solution.py:285
  45.8 0.9 %collective-permute-done.17.refs_0_ = f32[8,2,128,128]{3,2,1,0:T(8,128)S(1)} collective-permute-done((f32[8,2,128,128]{3,2,1,0:T(8,128)S(1)}, f32[8,2,128,128]{3,2,1,0:T(8,128)S(1)}, u32[]{:S(2)}, u32[]{:S(2)}) %collective-permute-start.17) | collective-permute-done | bytes 1048608 | tf_op jit(solution)/shard_map/ppermute | solution.py:321
  46.7 1.7 %block_outputs.3 = (bf16[128,2048]{1,0:T(8,128)(2,1)}, bf16[128,2048]{1,0:T(8,128)(2,1)}, bf16[128,2048]{1,0:T(8,128)(2,1)}, bf16[128,2048]{1,0:T(8,128)(2,1)}) custom-call(s32[1]{0:T(128)} %bitcast._.core.___.__, s32[1]{0:T(128)} %bitcast.1.me.__._, ...), custom_call_target="tpu_custom_call", output_to_operand_aliasing={{0}: (9, {}), {1}: (10, {}), {2}: (11, {}), {3}: (12, {})} | custom-call | flops 134217728 | bytes 4194304 | tf_op jit(solution)/shard_map/block_outputs/pallas_call | solution.py:285
  (31 shorter events, 4.0 us)
Async XLA Ops:
  0.6 16.9 %copy-start.3 = (bf16[128,2048]{1,0:T(8,128)(2,1)S(1)}, bf16[128,2048]{1,0:T(8,128)(2,1)}, u32[]{:S(2)}) copy-start(bf16[128,2048]{1,0:T(8,128)(2,1)} %g_ref.1) | copy-start | bytes 1572868
  0.6 16.9 %copy-start.2 = (bf16[128,2048]{1,0:T(8,128)(2,1)S(1)}, bf16[128,2048]{1,0:T(8,128)(2,1)}, u32[]{:S(2)}) copy-start(bf16[128,2048]{1,0:T(8,128)(2,1)} %v_ref.1) | copy-start | bytes 1572868
  0.7 16.9 %copy-start.1 = (bf16[128,2048]{1,0:T(8,128)(2,1)S(1)}, bf16[128,2048]{1,0:T(8,128)(2,1)}, u32[]{:S(2)}) copy-start(bf16[128,2048]{1,0:T(8,128)(2,1)} %k_ref.1) | copy-start | bytes 1572868
  0.7 16.9 %copy-start = (bf16[128,2048]{1,0:T(8,128)(2,1)S(1)}, bf16[128,2048]{1,0:T(8,128)(2,1)}, u32[]{:S(2)}) copy-start(bf16[128,2048]{1,0:T(8,128)(2,1)} %q_ref.1) | copy-start | bytes 1572868
  2.7 2.1 %collective-permute-start = (f32[4,2,128,128]{3,2,1,0:T(8,128)S(1)}, f32[4,2,128,128]{3,2,1,0:T(8,128)S(1)}, u32[]{:S(2)}, u32[]{:S(2)}) collective-permute-start(f32[4,2,128,128]{3,2,1,0:T(8,128)S(1)} %get-tuple-element.71), channel_id=1, source_target_pairs={{0,8},{8,0},{1,9},{9,1},{2,10},{10,2},{3,11},{11,3},{4,12},{12,4},... | collective-permute-start | bytes 1572872 | tf_op jit(solution)/shard_map/ppermute | solution.py:321
  3.2 7.6 %collective-permute-start.5 = (f32[4,2,128,128]{3,2,1,0:T(8,128)S(1)}, f32[4,2,128,128]{3,2,1,0:T(8,128)S(1)}, u32[]{:S(2)}, u32[]{:S(2)}) collective-permute-start(f32[4,2,128,128]{3,2,1,0:T(8,128)S(1)} %get-tuple-element.78), channel_id=1, source_target_pairs={{0,8},{8,0},{1,9},{9,1},{2,10},{10,2},{3,11},{11,3},{4,12},{12,4},... | collective-permute-start | bytes 1572872 | tf_op jit(solution)/shard_map/ppermute | solution.py:321
  4.8 8.1 %collective-permute-start.1 = (f32[2,128,128]{2,1,0:T(8,128)S(1)}, f32[2,128,128]{2,1,0:T(8,128)S(1)}, u32[]{:S(2)}, u32[]{:S(2)}) collective-permute-start(f32[2,128,128]{2,1,0:T(8,128)S(1)} %get-tuple-element.73), channel_id=1, source_target_pairs={{0,16},{1,17},{2,18},{3,19},{16,0},{17,1},{18,2},{19,3},{4,20},{5,... | collective-permute-start | bytes 393224 | tf_op jit(solution)/shard_map/ppermute | solution.py:335
  7.7 7.6 %collective-permute-start.2 = (f32[2,128,128]{2,1,0:T(8,128)S(1)}, f32[2,128,128]{2,1,0:T(8,128)S(1)}, u32[]{:S(2)}, u32[]{:S(2)}) collective-permute-start(f32[2,128,128]{2,1,0:T(8,128)S(1)} %get-tuple-element.74), channel_id=1, source_target_pairs={{0,3},{1,2},{2,1},{3,0},{16,19},{17,18},{18,17},{19,16},{4,7},{5,6... | collective-permute-start | bytes 393224 | tf_op jit(solution)/shard_map/ppermute | solution.py:335
  10.3 9.4 %collective-permute-start.3 = (f32[2,128,128]{2,1,0:T(8,128)S(1)}, f32[2,128,128]{2,1,0:T(8,128)S(1)}, u32[]{:S(2)}, u32[]{:S(2)}) collective-permute-start(f32[2,128,128]{2,1,0:T(8,128)S(1)} %get-tuple-element.75), channel_id=1, source_target_pairs={{0,1},{1,0},{2,3},{3,2},{16,17},{17,16},{18,19},{19,18},{4,5},{5,4... | collective-permute-start | bytes 393224 | tf_op jit(solution)/shard_map/ppermute | solution.py:335
  10.8 8.9 %collective-permute-start.4 = (f32[2,128,128]{2,1,0:T(8,128)S(1)}, f32[2,128,128]{2,1,0:T(8,128)S(1)}, u32[]{:S(2)}, u32[]{:S(2)}) collective-permute-start(f32[2,128,128]{2,1,0:T(8,128)S(1)} %get-tuple-element.76), channel_id=1, source_target_pairs={{0,18},{1,19},{2,16},{3,17},{16,2},{17,3},{18,0},{19,1},{4,22},{5,... | collective-permute-start | bytes 393224 | tf_op jit(solution)/shard_map/ppermute | solution.py:335
  10.9 9.8 %collective-permute-start.6 = (f32[2,128,128]{2,1,0:T(8,128)S(1)}, f32[2,128,128]{2,1,0:T(8,128)S(1)}, u32[]{:S(2)}, u32[]{:S(2)}) collective-permute-start(f32[2,128,128]{2,1,0:T(8,128)S(1)} %get-tuple-element.79), channel_id=1, source_target_pairs={{0,2},{1,3},{2,0},{3,1},{16,18},{17,19},{18,16},{19,17},{4,6},{5,7... | collective-permute-start | bytes 393224 | tf_op jit(solution)/shard_map/ppermute | solution.py:335
  12.9 8.6 %collective-permute-start.7 = (f32[2,128,128]{2,1,0:T(8,128)S(1)}, f32[2,128,128]{2,1,0:T(8,128)S(1)}, u32[]{:S(2)}, u32[]{:S(2)}) collective-permute-start(f32[2,128,128]{2,1,0:T(8,128)S(1)} %get-tuple-element.80), channel_id=1, source_target_pairs={{0,17},{1,16},{2,19},{3,18},{16,1},{17,0},{18,3},{19,2},{4,21},{5,... | collective-permute-start | bytes 393224 | tf_op jit(solution)/shard_map/ppermute | solution.py:335
  15.3 7.6 %collective-permute-start.8 = (f32[2,128,128]{2,1,0:T(8,128)S(1)}, f32[2,128,128]{2,1,0:T(8,128)S(1)}, u32[]{:S(2)}, u32[]{:S(2)}) collective-permute-start(f32[2,128,128]{2,1,0:T(8,128)S(1)} %get-tuple-element.81), channel_id=1, source_target_pairs={{0,19},{1,18},{2,17},{3,16},{16,3},{17,2},{18,1},{19,0},{4,23},{5,... | collective-permute-start | bytes 393224 | tf_op jit(solution)/shard_map/ppermute | solution.py:335
  23.0 5.9 %collective-permute-start.9 = (f32[1,128,128]{2,1,0:T(8,128)S(1)}, f32[1,128,128]{2,1,0:T(8,128)S(1)}, u32[]{:S(2)}, u32[]{:S(2)}) collective-permute-start(f32[1,128,128]{2,1,0:T(8,128)S(1)} %block_total.1), channel_id=1, source_target_pairs={{0,4},{4,0},{1,5},{5,1},{2,6},{6,2},{3,7},{7,3},{8,12},{12,8},{9,1... | collective-permute-start | bytes 196616 | tf_op jit(solution)/shard_map/ppermute | solution.py:321
  29.0 7.3 %collective-permute-start.10 = (f32[2,128,128]{2,1,0:T(8,128)S(1)}, f32[2,128,128]{2,1,0:T(8,128)S(1)}, u32[]{:S(2)}, u32[]{:S(2)}) collective-permute-start(f32[2,128,128]{2,1,0:T(8,128)S(1)} %get-tuple-element.105), channel_id=1, source_target_pairs={{0,16},{1,17},{2,18},{3,19},{16,0},{17,1},{18,2},{19,3},{4,20},{5,... | collective-permute-start | bytes 393224 | tf_op jit(solution)/shard_map/ppermute | solution.py:335
  29.2 7.9 %collective-permute-start.11 = (f32[2,128,128]{2,1,0:T(8,128)S(1)}, f32[2,128,128]{2,1,0:T(8,128)S(1)}, u32[]{:S(2)}, u32[]{:S(2)}) collective-permute-start(f32[2,128,128]{2,1,0:T(8,128)S(1)} %get-tuple-element.106), channel_id=1, source_target_pairs={{0,3},{1,2},{2,1},{3,0},{16,19},{17,18},{18,17},{19,16},{4,7},{5,6... | collective-permute-start | bytes 393224 | tf_op jit(solution)/shard_map/ppermute | solution.py:335
  31.8 7.3 %collective-permute-start.12 = (f32[2,128,128]{2,1,0:T(8,128)S(1)}, f32[2,128,128]{2,1,0:T(8,128)S(1)}, u32[]{:S(2)}, u32[]{:S(2)}) collective-permute-start(f32[2,128,128]{2,1,0:T(8,128)S(1)} %get-tuple-element.107), channel_id=1, source_target_pairs={{0,1},{1,0},{2,3},{3,2},{16,17},{17,16},{18,19},{19,18},{4,5},{5,4... | collective-permute-start | bytes 393224 | tf_op jit(solution)/shard_map/ppermute | solution.py:335
  32.2 7.4 %collective-permute-start.13 = (f32[2,128,128]{2,1,0:T(8,128)S(1)}, f32[2,128,128]{2,1,0:T(8,128)S(1)}, u32[]{:S(2)}, u32[]{:S(2)}) collective-permute-start(f32[2,128,128]{2,1,0:T(8,128)S(1)} %get-tuple-element.108), channel_id=1, source_target_pairs={{0,18},{1,19},{2,16},{3,17},{16,2},{17,3},{18,0},{19,1},{4,22},{5,... | collective-permute-start | bytes 393224 | tf_op jit(solution)/shard_map/ppermute | solution.py:335
  34.0 6.2 %collective-permute-start.14 = (f32[2,128,128]{2,1,0:T(8,128)S(1)}, f32[2,128,128]{2,1,0:T(8,128)S(1)}, u32[]{:S(2)}, u32[]{:S(2)}) collective-permute-start(f32[2,128,128]{2,1,0:T(8,128)S(1)} %get-tuple-element.109), channel_id=1, source_target_pairs={{0,2},{1,3},{2,0},{3,1},{16,18},{17,19},{18,16},{19,17},{4,6},{5,7... | collective-permute-start | bytes 393224 | tf_op jit(solution)/shard_map/ppermute | solution.py:335
  36.3 6.0 %collective-permute-start.15 = (f32[2,128,128]{2,1,0:T(8,128)S(1)}, f32[2,128,128]{2,1,0:T(8,128)S(1)}, u32[]{:S(2)}, u32[]{:S(2)}) collective-permute-start(f32[2,128,128]{2,1,0:T(8,128)S(1)} %get-tuple-element.110), channel_id=1, source_target_pairs={{0,17},{1,16},{2,19},{3,18},{16,1},{17,0},{18,3},{19,2},{4,21},{5,... | collective-permute-start | bytes 393224 | tf_op jit(solution)/shard_map/ppermute | solution.py:335
  37.1 6.8 %collective-permute-start.16 = (f32[2,128,128]{2,1,0:T(8,128)S(1)}, f32[2,128,128]{2,1,0:T(8,128)S(1)}, u32[]{:S(2)}, u32[]{:S(2)}) collective-permute-start(f32[2,128,128]{2,1,0:T(8,128)S(1)} %get-tuple-element.111), channel_id=1, source_target_pairs={{0,19},{1,18},{2,17},{3,16},{16,3},{17,2},{18,1},{19,0},{4,23},{5,... | collective-permute-start | bytes 393224 | tf_op jit(solution)/shard_map/ppermute | solution.py:335
  44.0 2.7 %collective-permute-start.17 = (f32[8,2,128,128]{3,2,1,0:T(8,128)S(1)}, f32[8,2,128,128]{3,2,1,0:T(8,128)S(1)}, u32[]{:S(2)}, u32[]{:S(2)}) collective-permute-start(f32[8,2,128,128]{3,2,1,0:T(8,128)S(1)} %sibling_state.1), channel_id=1, source_target_pairs={{0,8},{8,0},{1,9},{9,1},{2,10},{10,2},{3,11},{11,3},{4,12},{12,4},... | collective-permute-start | bytes 3145736 | tf_op jit(solution)/shard_map/ppermute | solution.py:321

commit v6 on v5

--- a/solution.py
+++ b/solution.py
@@ -236,32 +236,29 @@
     )(q, k, v, g, cosine, sine)
 
 
-def outputs_body(scale, per, heads, far, spots, core, me, _, __, rot_ref, part_ref, cos_ref, sin_ref, *refs):
+def outputs_body(scale, per, jobs, arrays, prior, spots, core, me, _, __, rot_ref, part_ref, cos_ref, sin_ref, *refs):
     core, me = core[0], me[0]
-    count = heads * per
-    if far:
-        pieces, refs = refs[:1], refs[5:]
-    else:
-        extras, pieces, refs = refs[:2], refs[2 : 2 + count], refs[2 + count :]
+    extras, pieces, refs = refs[:2], refs[2 : 2 + arrays], refs[2 + arrays + prior :]
     outs, (state_ref, held, sems) = refs[:4], refs[4:]
     cosine, sine = cos_ref[...], sin_ref[...]
+    half = rot_ref.shape[0] // 2
     copies = []
-    for n in range(heads):
+    for n, (mask, mine, first, spot) in enumerate(jobs):
         low = me % per
-        head = (me // per) ^ n
+        head = (me // per) ^ mask
         for i in range(per):
             cut = pieces[0].shape[-2]
             at = pl.ds(pl.multiple_of((low ^ i) * cut, cut), cut)
             for side in range(2):
-                if far:
-                    state = pieces[0][n * per + i, side]
+                if mine:
+                    which, kept = spots[mask]
+                    extra = extras[which][kept * per + i, side]
+                    state = pieces[first + i][side] + jnp.where(core == 1 - side, extra, 0.0)
                 else:
-                    which, spot = spots[n]
-                    extra = extras[which][spot * per + i, side]
-                    state = pieces[n * per + i][side] + jnp.where(core == 1 - side, extra, 0.0)
+                    state = pieces[first][spot * per + i, side]
                 state_ref[n, side, at] = state.astype(BF16)
         before, after = state_ref[n, 0], state_ref[n, 1]
-        at = (1 - core if far else core) * heads + head
+        at = (core if mine else 1 - core) * half + head
         att = part_ref[at, 0] + dot(rot_ref[at, 0], before, 1, 0)
         rqg = part_ref[at, 1] + dot(rot_ref[at, 1], before, 1, 1)
         rkg = part_ref[at, 2] + dot(rot_ref[at, 2], after, 1, 1)
@@ -278,14 +275,20 @@
         copy.wait()
 
 
-def outputs(scale, per, count, spots, who, rot, local, tables, extra, pieces, prior):
+def outputs(scale, per, spots, who, rot, local, tables, kept, own, far, prior):
     heads, _, rows, _ = rot.shape
-    far = extra is None
-    pieces = list(pieces) if far else [*extra, *pieces]
-    return call(
-        functools.partial(outputs_body, scale, per, count, far, spots),
+    jobs, pieces = [], []
+    for mask, values in own:
+        jobs.append((mask, True, len(pieces), 0))
+        pieces += values
+    for masks, value in far:
+        jobs += [(mask, False, len(pieces), spot) for spot, mask in enumerate(masks)]
+        pieces.append(value)
+    count = len(jobs)
+    return call(
+        functools.partial(outputs_body, scale, per, jobs, len(pieces), len(prior), spots),
         [pltpu.HBM((rows, heads * D), BF16)] * 4,
-        [SMEM] * 4 + [VMEM] * (4 + len(pieces)) + [HBM] * len(prior),
+        [SMEM] * 4 + [VMEM] * (6 + len(pieces)) + [HBM] * len(prior),
         [HBM] * 4,
         [
             pltpu.VMEM((count, 2, D, D), BF16),
@@ -295,24 +298,26 @@
         8 * count * rows * D * D,
         16 * rows * count * D * 2,
         "block_outputs",
-        {8 + len(pieces) + i: i for i in range(len(prior))},
-    )(*who, rot, local, *tables, *pieces, *prior)
-
-
-def relay_body(per, spots, core, _, __, ___, near_1, near_2, *refs):
+        {10 + len(pieces) + i: i for i in range(len(prior))},
+    )(*who, rot, local, *tables, *kept, *pieces, *prior)
+
+
+def relay_body(per, masks, spots, core, _, __, ___, near_1, near_2, *refs):
     core = core[0]
     out_ref = refs[-1]
-    for m in range(out_ref.shape[0]):
-        which, spot = spots[m // per]
+    for n, mask in enumerate(masks):
+        which, spot = spots[mask]
         near = (near_1, near_2)[which]
-        for side in range(2):
-            out_ref[m, side] = refs[m][side] + jnp.where(core == side, near[spot * per + m % per, side], 0.0)
-
-
-def relay(per, spots, who, near, pieces):
+        for i in range(per):
+            for side in range(2):
+                extra = jnp.where(core == side, near[spot * per + i, side], 0.0)
+                out_ref[n * per + i, side] = refs[n * per + i][side] + extra
+
+
+def relay(per, masks, spots, who, near, pieces):
     size = len(pieces) * pieces[0].size
     return call(
-        functools.partial(relay_body, per, spots), in_vmem((len(pieces),) + pieces[0].shape),
+        functools.partial(relay_body, per, masks, spots), in_vmem((len(pieces),) + pieces[0].shape),
         [SMEM] * 4 + [VMEM] * (2 + len(pieces)), VMEM, [], size, size * 8, "sibling_state",
     )(*who, *near, *pieces)
 
@@ -392,12 +397,24 @@
     pieces = offset(who, scan(who, arrived), passed)
     whole = exchange(pieces, order)
 
-    whole = dict(zip([0] + order, barrier(*(whole[m] for m in [0] + order))))
-    whole = [whole[m] for m in range(members)]
-    other = swap(relay(per, spots, who, near, whole), "core")
-    made = outputs(scale, per, part, spots, who, rot, local, tables, near_other, whole, ())
-    made = outputs(scale, per, part, spots, who, rot, local, tables, None, [other], tuple(made))
-    return tuple(made)
+    whole = {mask: [whole[mask * per + i] for i in range(per)] for mask in masks}
+
+    def pass_on(chosen):
+        listed = [piece for mask in chosen for piece in whole[mask]]
+        return chosen, swap(relay(per, chosen, spots, who, near, listed), "core")
+
+    early, late = masks[: part // 2], masks[part // 2 :]
+    soon = list(dict.fromkeys([0, *early]))
+    first = [pass_on([mask]) for mask in early]
+    finish = functools.partial(outputs, scale, per, spots, who, rot, local, tables, near_other)
+    made = finish([(mask, whole[mask]) for mask in soon], [], ())
+    held = [whole[mask] for mask in late]
+    held, first, made = barrier(held, [value for _, value in first], made)
+    whole.update(zip(late, held))
+    first = [([mask], value) for mask, value in zip(early, first)]
+    last = pass_on(late)
+    made = finish([(mask, whole[mask]) for mask in late if mask not in soon], first, tuple(made))
+    return tuple(finish([], [last], tuple(made)))
 
 
 def solution(mesh):

time: 48.5 us -> 47.4 us (0.977)
  waiting for transfers between devices: 14.8 us -> 12.1 us
  Pallas kernels: 8.78 us -> 9.58 us
  starting transfers between devices: 24.1 us -> 24.7 us
    ppermute x14, waiting for transfers between devices: 9.96 us -> 8.24 us  [send_to(): return lax.ppermute(value, AXES, pairs)]
    ppermute x4 -> x8, waiting for transfers between devices: 4.8 us -> 3.88 us  [swap(): return lax.ppermute(value, axis, [(0, 1), (1, 0)])]
    pallas_call x3 -> x8, Pallas kernels: 3.51 us -> 4.35 us  [the longest x3 4.19 us: outputs(): call(functools.partial(outputs_body, scale, per, jobs, len(pieces), len(p...]
    ppermute x4 -> x8, starting transfers between devices: 3.32 us -> 3.95 us  [swap(): return lax.ppermute(value, axis, [(0, 1), (1, 0)])]
  transfers between devices with their start and end apart: 18 -> 22, of which waited for: 12 -> 10; matrix products, arithmetic and copies ran while one was open for 0% -> 0% of each run, Pallas kernels for 10% -> 13%
where the time goes in v6:
time: 47.4 us; the launch traced here: 47.2 us
  starting transfers between devices  24.7 us (52%)
  waiting for transfers between devices  12.1 us (26%)
  Pallas kernels  9.58 us (20%)
  between operations  0.82 us (2%)
    ppermute x14, starting transfers between devices, send_to(): return lax.ppermute(value, AXES, pairs)  20.7 us
    ppermute x14, waiting for transfers between devices, send_to(): return lax.ppermute(value, AXES, pairs)  8.24 us
    pallas_call x3, Pallas kernels, outputs(): call(functools.partial(outputs_body, scale, per, jobs, len(pieces), len(p...  4.19 us
    ppermute x8, starting transfers between devices, swap(): return lax.ppermute(value, axis, [(0, 1), (1, 0)])  3.95 us
    ppermute x8, waiting for transfers between devices, swap(): return lax.ppermute(value, axis, [(0, 1), (1, 0)])  3.88 us
    pallas_call x1, Pallas kernels, local_parts(): call(local_body, [in_vmem((heads, 4, rows, D), BF16), in_vmem((heads, 4,...  2.13 us
    pallas_call x1, Pallas kernels, states(): call(body, [table] * 2 + [in_vmem(piece, BF16)] * 4 + results, [SMEM] * 4...  1.99 us
  transfers between devices with their start and end apart: 22, of which 10 were waited for; matrix products, arithmetic and copies ran while one was open for 0% of the time, Pallas kernels for 13%

profile of v6, /device:TPU:0, one launch (start us, length us, event | category | flops | bytes accessed | tf_op | source)
XLA Modules:
  0.0 47.2 jit_solution(16145032088723615114)
XLA Ops:
  0.7 2.0 %block_states.2 = (f32[128,128]{1,0:T(8,128)S(1)}, f32[128,128]{1,0:T(8,128)S(1)}, bf16[128,1024]{1,0:T(8,128)(2,1)S(1)}, bf16[128,1024]{1,0:T(8,128)(2,1)S(1)},...) custom-call(s32[1]{0:T(128)} %bitcast._.core.___.__, ...), custom_call_target="tpu_custom_call" | custom-call | flops 67108864 | bytes 2097152 | tf_op jit(solution)/shard_map/block_states/pallas_call | solution.py:116
  2.7 0.5 %collective-permute-start = (f32[4,2,128,128]{3,2,1,0:T(8,128)S(1)}, f32[4,2,128,128]{3,2,1,0:T(8,128)S(1)}, u32[]{:S(2)}, u32[]{:S(2)}) collective-permute-start(f32[4,2,128,128]{3,2,1,0:T(8,128)S(1)} %get-tuple-element.79), channel_id=1, source_target_pairs={{0,8},{8,0},{1,9},{9,1},{2,10},{10,2},{3,11},{11,3},{4,12},{12,4},... | collective-permute-start | bytes 1572872 | tf_op jit(solution)/shard_map/ppermute | solution.py:326
  3.3 0.7 %block_states.3 = (f32[4,2,128,128]{3,2,1,0:T(8,128)S(1)}, f32[4,2,128,128]{3,2,1,0:T(8,128)S(1)}) custom-call(s32[1]{0:T(128)} %bitcast._.core.___.__, s32[1]{0:T(128)} %bitcast.1.me.__._, s32[1]{0:T(128)} %bitcast.2.__.group._, s32[1]{0:T(128)} %bitcast._.core.___.__, f32[128,128]{1,0:T(8,128)S(1)} %get-tuple-element.90.refs_0_.cos_ref, ...), custom_call_target="tpu_custom_call" | custom-call | flops 67108864 | bytes 2097152 | tf_op jit(solution)/shard_map/block_states/pallas_call | solution.py:121
  3.9 0.8 %collective-permute-done.b_ref.refs_0_ = f32[4,2,128,128]{3,2,1,0:T(8,128)S(1)} collective-permute-done((f32[4,2,128,128]{3,2,1,0:T(8,128)S(1)}, f32[4,2,128,128]{3,2,1,0:T(8,128)S(1)}, u32[]{:S(2)}, u32[]{:S(2)}) %collective-permute-start) | collective-permute-done | bytes 524320 | tf_op jit(solution)/shard_map/ppermute | solution.py:326
  4.8 2.9 %collective-permute-start.1 = (f32[2,128,128]{2,1,0:T(8,128)S(1)}, f32[2,128,128]{2,1,0:T(8,128)S(1)}, u32[]{:S(2)}, u32[]{:S(2)}) collective-permute-start(f32[2,128,128]{2,1,0:T(8,128)S(1)} %get-tuple-element.81), channel_id=1, source_target_pairs={{0,16},{1,17},{2,18},{3,19},{16,0},{17,1},{18,2},{19,3},{4,20},{5,... | collective-permute-start | bytes 393224 | tf_op jit(solution)/shard_map/ppermute | solution.py:340
  7.7 2.5 %collective-permute-start.2 = (f32[2,128,128]{2,1,0:T(8,128)S(1)}, f32[2,128,128]{2,1,0:T(8,128)S(1)}, u32[]{:S(2)}, u32[]{:S(2)}) collective-permute-start(f32[2,128,128]{2,1,0:T(8,128)S(1)} %get-tuple-element.82), channel_id=1, source_target_pairs={{0,3},{1,2},{2,1},{3,0},{16,19},{17,18},{18,17},{19,16},{4,7},{5,6... | collective-permute-start | bytes 393224 | tf_op jit(solution)/shard_map/ppermute | solution.py:340
  10.9 2.0 %collective-permute-start.6 = (f32[2,128,128]{2,1,0:T(8,128)S(1)}, f32[2,128,128]{2,1,0:T(8,128)S(1)}, u32[]{:S(2)}, u32[]{:S(2)}) collective-permute-start(f32[2,128,128]{2,1,0:T(8,128)S(1)} %get-tuple-element.87), channel_id=1, source_target_pairs={{0,2},{1,3},{2,0},{3,1},{16,18},{17,19},{18,16},{19,17},{4,6},{5,7... | collective-permute-start | bytes 393224 | tf_op jit(solution)/shard_map/ppermute | solution.py:340
  12.9 2.4 %collective-permute-start.7 = (f32[2,128,128]{2,1,0:T(8,128)S(1)}, f32[2,128,128]{2,1,0:T(8,128)S(1)}, u32[]{:S(2)}, u32[]{:S(2)}) collective-permute-start(f32[2,128,128]{2,1,0:T(8,128)S(1)} %get-tuple-element.88), channel_id=1, source_target_pairs={{0,17},{1,16},{2,19},{3,18},{16,1},{17,0},{18,3},{19,2},{4,21},{5,... | collective-permute-start | bytes 393224 | tf_op jit(solution)/shard_map/ppermute | solution.py:340
  15.3 2.2 %collective-permute-start.8 = (f32[2,128,128]{2,1,0:T(8,128)S(1)}, f32[2,128,128]{2,1,0:T(8,128)S(1)}, u32[]{:S(2)}, u32[]{:S(2)}) collective-permute-start(f32[2,128,128]{2,1,0:T(8,128)S(1)} %get-tuple-element.89), channel_id=1, source_target_pairs={{0,19},{1,18},{2,17},{3,16},{16,3},{17,2},{18,1},{19,0},{4,23},{5,... | collective-permute-start | bytes 393224 | tf_op jit(solution)/shard_map/ppermute | solution.py:340
  17.5 2.1 %local_parts.1 = (bf16[16,4,128,128]{3,2,1,0:T(8,128)(2,1)S(1)}, f32[16,4,128,128]{3,2,1,0:T(8,128)S(1)}) custom-call(bf16[128,2048]{1,0:T(8,128)(2,1)S(1)} %copy-done, bf16[128,2048]{1,0:T(8,128)(2,1)S(1)} %copy-done.1, bf16[128,2048]{1,0:T(8,128)(2,1)S(1)} %copy-done.2, bf16[128,2048]{1,0:T(8,128)(2,1)S(1)} %copy-done.3, ...), custom_call_target="tpu_custom_call" | custom-call | flops 536870912 | bytes 8388608 | tf_op jit(solution)/shard_map/local_parts/pallas_call | solution.py:232
  19.7 1.0 %collective-permute-done.6.refs_4_ = f32[2,128,128]{2,1,0:T(8,128)S(1)} collective-permute-done((f32[2,128,128]{2,1,0:T(8,128)S(1)}, f32[2,128,128]{2,1,0:T(8,128)S(1)}, u32[]{:S(2)}, u32[]{:S(2)}) %collective-permute-start.6) | collective-permute-done | bytes 131104 | tf_op jit(solution)/shard_map/ppermute | solution.py:340
  20.7 0.8 %collective-permute-done.7.refs_3_ = f32[2,128,128]{2,1,0:T(8,128)S(1)} collective-permute-done((f32[2,128,128]{2,1,0:T(8,128)S(1)}, f32[2,128,128]{2,1,0:T(8,128)S(1)}, u32[]{:S(2)}, u32[]{:S(2)}) %collective-permute-start.7) | collective-permute-done | bytes 131104 | tf_op jit(solution)/shard_map/ppermute | solution.py:340
  21.5 1.4 %collective-permute-done.8.refs_7_ = f32[2,128,128]{2,1,0:T(8,128)S(1)} collective-permute-done((f32[2,128,128]{2,1,0:T(8,128)S(1)}, f32[2,128,128]{2,1,0:T(8,128)S(1)}, u32[]{:S(2)}, u32[]{:S(2)}) %collective-permute-start.8) | collective-permute-done | bytes 131104 | tf_op jit(solution)/shard_map/ppermute | solution.py:340
  23.0 2.7 %collective-permute-start.9 = (f32[1,128,128]{2,1,0:T(8,128)S(1)}, f32[1,128,128]{2,1,0:T(8,128)S(1)}, u32[]{:S(2)}, u32[]{:S(2)}) collective-permute-start(f32[1,128,128]{2,1,0:T(8,128)S(1)} %block_total.1), channel_id=1, source_target_pairs={{0,4},{4,0},{1,5},{5,1},{2,6},{6,2},{3,7},{7,3},{8,12},{12,8},{9,1... | collective-permute-start | bytes 196616 | tf_op jit(solution)/shard_map/ppermute | solution.py:326
  25.9 3.1 %collective-permute-done.9.passed_ref = f32[1,128,128]{2,1,0:T(8,128)S(1)} collective-permute-done((f32[1,128,128]{2,1,0:T(8,128)S(1)}, f32[1,128,128]{2,1,0:T(8,128)S(1)}, u32[]{:S(2)}, u32[]{:S(2)}) %collective-permute-start.9) | collective-permute-done | bytes 65568 | tf_op jit(solution)/shard_map/ppermute | solution.py:326
  29.2 2.6 %collective-permute-start.15 = (f32[2,128,128]{2,1,0:T(8,128)S(1)}, f32[2,128,128]{2,1,0:T(8,128)S(1)}, u32[]{:S(2)}, u32[]{:S(2)}) collective-permute-start(f32[2,128,128]{2,1,0:T(8,128)S(1)} %get-tuple-element.117), channel_id=1, source_target_pairs={{0,3},{1,2},{2,1},{3,0},{16,19},{17,18},{18,17},{19,16},{4,7},{5,6... | collective-permute-start | bytes 393224 | tf_op jit(solution)/shard_map/ppermute | solution.py:340
  32.2 1.8 %collective-permute-start.19 = (f32[2,128,128]{2,1,0:T(8,128)S(1)}, f32[2,128,128]{2,1,0:T(8,128)S(1)}, u32[]{:S(2)}, u32[]{:S(2)}) collective-permute-start(f32[2,128,128]{2,1,0:T(8,128)S(1)} %get-tuple-element.119), channel_id=1, source_target_pairs={{0,18},{1,19},{2,16},{3,17},{16,2},{17,3},{18,0},{19,1},{4,22},{5,... | collective-permute-start | bytes 393224 | tf_op jit(solution)/shard_map/ppermute | solution.py:340
  34.4 2.0 %collective-permute-done.13.refs_0_.refs_3_ = f32[2,128,128]{2,1,0:T(8,128)S(1)} collective-permute-done((f32[2,128,128]{2,1,0:T(8,128)S(1)}, f32[2,128,128]{2,1,0:T(8,128)S(1)}, u32[]{:S(2)}, u32[]{:S(2)}) %collective-permute-start.13) | collective-permute-done | bytes 131104 | tf_op jit(solution)/shard_map/ppermute | solution.py:340
  36.3 0.7 %collective-permute-start.11 = (f32[2,128,128]{2,1,0:T(8,128)S(1)}, f32[2,128,128]{2,1,0:T(8,128)S(1)}, u32[]{:S(2)}, u32[]{:S(2)}) collective-permute-start(f32[2,128,128]{2,1,0:T(8,128)S(1)} %get-tuple-element.113), channel_id=1, source_target_pairs={{0,17},{1,16},{2,19},{3,18},{16,1},{17,0},{18,3},{19,2},{4,21},{5,... | collective-permute-start | bytes 393224 | tf_op jit(solution)/shard_map/ppermute | solution.py:340
  37.1 2.0 %collective-permute-start.12 = (f32[2,128,128]{2,1,0:T(8,128)S(1)}, f32[2,128,128]{2,1,0:T(8,128)S(1)}, u32[]{:S(2)}, u32[]{:S(2)}) collective-permute-start(f32[2,128,128]{2,1,0:T(8,128)S(1)} %get-tuple-element.114), channel_id=1, source_target_pairs={{0,19},{1,18},{2,17},{3,16},{16,3},{17,2},{18,1},{19,0},{4,23},{5,... | collective-permute-start | bytes 393224 | tf_op jit(solution)/shard_map/ppermute | solution.py:340
  40.3 2.0 %collective-permute-done.11.refs_1_.refs_3_ = f32[2,128,128]{2,1,0:T(8,128)S(1)} collective-permute-done((f32[2,128,128]{2,1,0:T(8,128)S(1)}, f32[2,128,128]{2,1,0:T(8,128)S(1)}, u32[]{:S(2)}, u32[]{:S(2)}) %collective-permute-start.11) | collective-permute-done | bytes 131104 | tf_op jit(solution)/shard_map/ppermute | solution.py:340
  42.3 1.4 %block_outputs.3 = (bf16[128,2048]{1,0:T(8,128)(2,1)}, bf16[128,2048]{1,0:T(8,128)(2,1)}, bf16[128,2048]{1,0:T(8,128)(2,1)}, bf16[128,2048]{1,0:T(8,128)(2,1)}) custom-call(s32[1]{0:T(128)} %bitcast._.core.___.__, s32[1]{0:T(128)} %bitcast.1.me.__._, s32[1]{0:T(128)} %bitcast.2.__.group._, s32[1]{0:T(128)} %bitcast._.core.___.__, ...), custom_call_target="tpu_custom_call" | custom-call | flops 83886080 | bytes 2621440 | tf_op jit(solution)/shard_map/block_outputs/pallas_call | solution.py:288
  44.4 1.6 %block_outputs.4 = (bf16[128,2048]{1,0:T(8,128)(2,1)}, bf16[128,2048]{1,0:T(8,128)(2,1)}, bf16[128,2048]{1,0:T(8,128)(2,1)}, bf16[128,2048]{1,0:T(8,128)(2,1)}) custom-call(s32[1]{0:T(128)} %bitcast._.core.___.__, s32[1]{0:T(128)} %bitcast.1.me.__._, ...), custom_call_target="tpu_custom_call", output_to_operand_aliasing={{0}: (17, {}), {1}: (18, {}), {2}: (19, {}), {3}: (20, {})} | custom-call | flops 117440512 | bytes 3670016 | tf_op jit(solution)/shard_map/block_outputs/pallas_call | solution.py:288
  46.0 1.3 %block_outputs.5 = (bf16[128,2048]{1,0:T(8,128)(2,1)}, bf16[128,2048]{1,0:T(8,128)(2,1)}, bf16[128,2048]{1,0:T(8,128)(2,1)}, bf16[128,2048]{1,0:T(8,128)(2,1)}) custom-call(s32[1]{0:T(128)} %bitcast._.core.___.__, s32[1]{0:T(128)} %bitcast.1.me.__._, ...), custom_call_target="tpu_custom_call", output_to_operand_aliasing={{0}: (11, {}), {1}: (12, {}), {2}: (13, {}), {3}: (14, {})} | custom-call | flops 67108864 | bytes 2097152 | tf_op jit(solution)/shard_map/block_outputs/pallas_call | solution.py:288
  (44 shorter events, 4.0 us)
Async XLA Ops:
  0.6 16.9 %copy-start.3 = (bf16[128,2048]{1,0:T(8,128)(2,1)S(1)}, bf16[128,2048]{1,0:T(8,128)(2,1)}, u32[]{:S(2)}) copy-start(bf16[128,2048]{1,0:T(8,128)(2,1)} %g_ref.1) | copy-start | bytes 1572868
  0.6 16.9 %copy-start.2 = (bf16[128,2048]{1,0:T(8,128)(2,1)S(1)}, bf16[128,2048]{1,0:T(8,128)(2,1)}, u32[]{:S(2)}) copy-start(bf16[128,2048]{1,0:T(8,128)(2,1)} %v_ref.1) | copy-start | bytes 1572868
  2.7 2.1 %collective-permute-start = (f32[4,2,128,128]{3,2,1,0:T(8,128)S(1)}, f32[4,2,128,128]{3,2,1,0:T(8,128)S(1)}, u32[]{:S(2)}, u32[]{:S(2)}) collective-permute-start(f32[4,2,128,128]{3,2,1,0:T(8,128)S(1)} %get-tuple-element.79), channel_id=1, source_target_pairs={{0,8},{8,0},{1,9},{9,1},{2,10},{10,2},{3,11},{11,3},{4,12},{12,4},... | collective-permute-start | bytes 1572872 | tf_op jit(solution)/shard_map/ppermute | solution.py:326
  3.2 7.6 %collective-permute-start.5 = (f32[4,2,128,128]{3,2,1,0:T(8,128)S(1)}, f32[4,2,128,128]{3,2,1,0:T(8,128)S(1)}, u32[]{:S(2)}, u32[]{:S(2)}) collective-permute-start(f32[4,2,128,128]{3,2,1,0:T(8,128)S(1)} %get-tuple-element.86), channel_id=1, source_target_pairs={{0,8},{8,0},{1,9},{9,1},{2,10},{10,2},{3,11},{11,3},{4,12},{12,4},... | collective-permute-start | bytes 1572872 | tf_op jit(solution)/shard_map/ppermute | solution.py:326
  4.8 8.1 %collective-permute-start.1 = (f32[2,128,128]{2,1,0:T(8,128)S(1)}, f32[2,128,128]{2,1,0:T(8,128)S(1)}, u32[]{:S(2)}, u32[]{:S(2)}) collective-permute-start(f32[2,128,128]{2,1,0:T(8,128)S(1)} %get-tuple-element.81), channel_id=1, source_target_pairs={{0,16},{1,17},{2,18},{3,19},{16,0},{17,1},{18,2},{19,3},{4,20},{5,... | collective-permute-start | bytes 393224 | tf_op jit(solution)/shard_map/ppermute | solution.py:340
  7.7 7.6 %collective-permute-start.2 = (f32[2,128,128]{2,1,0:T(8,128)S(1)}, f32[2,128,128]{2,1,0:T(8,128)S(1)}, u32[]{:S(2)}, u32[]{:S(2)}) collective-permute-start(f32[2,128,128]{2,1,0:T(8,128)S(1)} %get-tuple-element.82), channel_id=1, source_target_pairs={{0,3},{1,2},{2,1},{3,0},{16,19},{17,18},{18,17},{19,16},{4,7},{5,6... | collective-permute-start | bytes 393224 | tf_op jit(solution)/shard_map/ppermute | solution.py:340
  10.3 9.4 %collective-permute-start.3 = (f32[2,128,128]{2,1,0:T(8,128)S(1)}, f32[2,128,128]{2,1,0:T(8,128)S(1)}, u32[]{:S(2)}, u32[]{:S(2)}) collective-permute-start(f32[2,128,128]{2,1,0:T(8,128)S(1)} %get-tuple-element.83), channel_id=1, source_target_pairs={{0,1},{1,0},{2,3},{3,2},{16,17},{17,16},{18,19},{19,18},{4,5},{5,4... | collective-permute-start | bytes 393224 | tf_op jit(solution)/shard_map/ppermute | solution.py:340
  10.8 8.9 %collective-permute-start.4 = (f32[2,128,128]{2,1,0:T(8,128)S(1)}, f32[2,128,128]{2,1,0:T(8,128)S(1)}, u32[]{:S(2)}, u32[]{:S(2)}) collective-permute-start(f32[2,128,128]{2,1,0:T(8,128)S(1)} %get-tuple-element.84), channel_id=1, source_target_pairs={{0,18},{1,19},{2,16},{3,17},{16,2},{17,3},{18,0},{19,1},{4,22},{5,... | collective-permute-start | bytes 393224 | tf_op jit(solution)/shard_map/ppermute | solution.py:340
  10.9 9.8 %collective-permute-start.6 = (f32[2,128,128]{2,1,0:T(8,128)S(1)}, f32[2,128,128]{2,1,0:T(8,128)S(1)}, u32[]{:S(2)}, u32[]{:S(2)}) collective-permute-start(f32[2,128,128]{2,1,0:T(8,128)S(1)} %get-tuple-element.87), channel_id=1, source_target_pairs={{0,2},{1,3},{2,0},{3,1},{16,18},{17,19},{18,16},{19,17},{4,6},{5,7... | collective-permute-start | bytes 393224 | tf_op jit(solution)/shard_map/ppermute | solution.py:340
  12.9 8.6 %collective-permute-start.7 = (f32[2,128,128]{2,1,0:T(8,128)S(1)}, f32[2,128,128]{2,1,0:T(8,128)S(1)}, u32[]{:S(2)}, u32[]{:S(2)}) collective-permute-start(f32[2,128,128]{2,1,0:T(8,128)S(1)} %get-tuple-element.88), channel_id=1, source_target_pairs={{0,17},{1,16},{2,19},{3,18},{16,1},{17,0},{18,3},{19,2},{4,21},{5,... | collective-permute-start | bytes 393224 | tf_op jit(solution)/shard_map/ppermute | solution.py:340
  15.3 7.6 %collective-permute-start.8 = (f32[2,128,128]{2,1,0:T(8,128)S(1)}, f32[2,128,128]{2,1,0:T(8,128)S(1)}, u32[]{:S(2)}, u32[]{:S(2)}) collective-permute-start(f32[2,128,128]{2,1,0:T(8,128)S(1)} %get-tuple-element.89), channel_id=1, source_target_pairs={{0,19},{1,18},{2,17},{3,16},{16,3},{17,2},{18,1},{19,0},{4,23},{5,... | collective-permute-start | bytes 393224 | tf_op jit(solution)/shard_map/ppermute | solution.py:340
  23.0 5.9 %collective-permute-start.9 = (f32[1,128,128]{2,1,0:T(8,128)S(1)}, f32[1,128,128]{2,1,0:T(8,128)S(1)}, u32[]{:S(2)}, u32[]{:S(2)}) collective-permute-start(f32[1,128,128]{2,1,0:T(8,128)S(1)} %block_total.1), channel_id=1, source_target_pairs={{0,4},{4,0},{1,5},{5,1},{2,6},{6,2},{3,7},{7,3},{8,12},{12,8},{9,1... | collective-permute-start | bytes 196616 | tf_op jit(solution)/shard_map/ppermute | solution.py:326
  29.0 7.3 %collective-permute-start.13 = (f32[2,128,128]{2,1,0:T(8,128)S(1)}, f32[2,128,128]{2,1,0:T(8,128)S(1)}, u32[]{:S(2)}, u32[]{:S(2)}) collective-permute-start(f32[2,128,128]{2,1,0:T(8,128)S(1)} %get-tuple-element.116), channel_id=1, source_target_pairs={{0,16},{1,17},{2,18},{3,19},{16,0},{17,1},{18,2},{19,3},{4,20},{5,... | collective-permute-start | bytes 393224 | tf_op jit(solution)/shard_map/ppermute | solution.py:340
  29.2 7.9 %collective-permute-start.15 = (f32[2,128,128]{2,1,0:T(8,128)S(1)}, f32[2,128,128]{2,1,0:T(8,128)S(1)}, u32[]{:S(2)}, u32[]{:S(2)}) collective-permute-start(f32[2,128,128]{2,1,0:T(8,128)S(1)} %get-tuple-element.117), channel_id=1, source_target_pairs={{0,3},{1,2},{2,1},{3,0},{16,19},{17,18},{18,17},{19,16},{4,7},{5,6... | collective-permute-start | bytes 393224 | tf_op jit(solution)/shard_map/ppermute | solution.py:340
  31.8 7.4 %collective-permute-start.17 = (f32[2,128,128]{2,1,0:T(8,128)S(1)}, f32[2,128,128]{2,1,0:T(8,128)S(1)}, u32[]{:S(2)}, u32[]{:S(2)}) collective-permute-start(f32[2,128,128]{2,1,0:T(8,128)S(1)} %get-tuple-element.118), channel_id=1, source_target_pairs={{0,1},{1,0},{2,3},{3,2},{16,17},{17,16},{18,19},{19,18},{4,5},{5,4... | collective-permute-start | bytes 393224 | tf_op jit(solution)/shard_map/ppermute | solution.py:340
  32.2 7.4 %collective-permute-start.19 = (f32[2,128,128]{2,1,0:T(8,128)S(1)}, f32[2,128,128]{2,1,0:T(8,128)S(1)}, u32[]{:S(2)}, u32[]{:S(2)}) collective-permute-start(f32[2,128,128]{2,1,0:T(8,128)S(1)} %get-tuple-element.119), channel_id=1, source_target_pairs={{0,18},{1,19},{2,16},{3,17},{16,2},{17,3},{18,0},{19,1},{4,22},{5,... | collective-permute-start | bytes 393224 | tf_op jit(solution)/shard_map/ppermute | solution.py:340
  34.0 6.2 %collective-permute-start.10 = (f32[2,128,128]{2,1,0:T(8,128)S(1)}, f32[2,128,128]{2,1,0:T(8,128)S(1)}, u32[]{:S(2)}, u32[]{:S(2)}) collective-permute-start(f32[2,128,128]{2,1,0:T(8,128)S(1)} %get-tuple-element.112), channel_id=1, source_target_pairs={{0,2},{1,3},{2,0},{3,1},{16,18},{17,19},{18,16},{19,17},{4,6},{5,7... | collective-permute-start | bytes 393224 | tf_op jit(solution)/shard_map/ppermute | solution.py:340
  36.3 6.0 %collective-permute-start.11 = (f32[2,128,128]{2,1,0:T(8,128)S(1)}, f32[2,128,128]{2,1,0:T(8,128)S(1)}, u32[]{:S(2)}, u32[]{:S(2)}) collective-permute-start(f32[2,128,128]{2,1,0:T(8,128)S(1)} %get-tuple-element.113), channel_id=1, source_target_pairs={{0,17},{1,16},{2,19},{3,18},{16,1},{17,0},{18,3},{19,2},{4,21},{5,... | collective-permute-start | bytes 393224 | tf_op jit(solution)/shard_map/ppermute | solution.py:340
  37.1 6.8 %collective-permute-start.12 = (f32[2,128,128]{2,1,0:T(8,128)S(1)}, f32[2,128,128]{2,1,0:T(8,128)S(1)}, u32[]{:S(2)}, u32[]{:S(2)}) collective-permute-start(f32[2,128,128]{2,1,0:T(8,128)S(1)} %get-tuple-element.114), channel_id=1, source_target_pairs={{0,19},{1,18},{2,17},{3,16},{16,3},{17,2},{18,1},{19,0},{4,23},{5,... | collective-permute-start | bytes 393224 | tf_op jit(solution)/shard_map/ppermute | solution.py:340
  39.1 4.7 %collective-permute-start.14 = (f32[1,2,128,128]{3,2,1,0:T(8,128)S(1)}, f32[1,2,128,128]{3,2,1,0:T(8,128)S(1)}, u32[]{:S(2)}, u32[]{:S(2)}) collective-permute-start(f32[1,2,128,128]{3,2,1,0:T(8,128)S(1)} %sibling_state.5), channel_id=1, source_target_pairs={{0,8},{8,0},{1,9},{9,1},{2,10},{10,2},{3,11},{11,3},{4,12},{12,4},... | collective-permute-start | bytes 393224 | tf_op jit(solution)/shard_map/ppermute | solution.py:326
  39.7 4.2 %collective-permute-start.16 = (f32[1,2,128,128]{3,2,1,0:T(8,128)S(1)}, f32[1,2,128,128]{3,2,1,0:T(8,128)S(1)}, u32[]{:S(2)}, u32[]{:S(2)}) collective-permute-start(f32[1,2,128,128]{3,2,1,0:T(8,128)S(1)} %sibling_state.6), channel_id=1, source_target_pairs={{0,8},{8,0},{1,9},{9,1},{2,10},{10,2},{3,11},{11,3},{4,12},{12,4},... | collective-permute-start | bytes 393224 | tf_op jit(solution)/shard_map/ppermute | solution.py:326
  40.2 3.7 %collective-permute-start.18 = (f32[1,2,128,128]{3,2,1,0:T(8,128)S(1)}, f32[1,2,128,128]{3,2,1,0:T(8,128)S(1)}, u32[]{:S(2)}, u32[]{:S(2)}) collective-permute-start(f32[1,2,128,128]{3,2,1,0:T(8,128)S(1)} %sibling_state.7), channel_id=1, source_target_pairs={{0,8},{8,0},{1,9},{9,1},{2,10},{10,2},{3,11},{11,3},{4,12},{12,4},... | collective-permute-start | bytes 393224 | tf_op jit(solution)/shard_map/ppermute | solution.py:326
  42.3 1.6 %collective-permute-start.20 = (f32[1,2,128,128]{3,2,1,0:T(8,128)S(1)}, f32[1,2,128,128]{3,2,1,0:T(8,128)S(1)}, u32[]{:S(2)}, u32[]{:S(2)}) collective-permute-start(f32[1,2,128,128]{3,2,1,0:T(8,128)S(1)} %sibling_state.8), channel_id=1, source_target_pairs={{0,8},{8,0},{1,9},{9,1},{2,10},{10,2},{3,11},{11,3},{4,12},{12,4},... | collective-permute-start | bytes 393224 | tf_op jit(solution)/shard_map/ppermute | solution.py:326
  44.0 2.0 %collective-permute-start.21 = (f32[4,2,128,128]{3,2,1,0:T(8,128)S(1)}, f32[4,2,128,128]{3,2,1,0:T(8,128)S(1)}, u32[]{:S(2)}, u32[]{:S(2)}) collective-permute-start(f32[4,2,128,128]{3,2,1,0:T(8,128)S(1)} %sibling_state.9), channel_id=1, source_target_pairs={{0,8},{8,0},{1,9},{9,1},{2,10},{10,2},{3,11},{11,3},{4,12},{12,4},... | collective-permute-start | bytes 1572872 | tf_op jit(solution)/shard_map/ppermute | solution.py:326
  (2 other events, 33.7 us)

commit v7 on v6

--- a/solution.py
+++ b/solution.py
@@ -65,8 +65,9 @@
     half, me = core[0], me[0]
     if first:
         pos, *sources = refs[:5]
-        cos_ref, sin_ref, *nearby = refs[5:11]
-        outs, (place, *inputs), sems = refs[11:13], refs[13:18], refs[18]
+        cos_ref, sin_ref, *fetched = refs[5:15]
+        inputs, nearby = fetched[:4], fetched[4:]
+        outs, place, sems = refs[15:17], refs[17], refs[18]
         width = inputs[0].shape[1]
         pos_copy = pltpu.make_async_copy(pos, place, sems.at[8])
         pos_copy.start()
@@ -112,12 +113,12 @@
     work = (4 * heads * rows * D * D, heads * D * (8 * rows + 8 * D))
     if first:
         piece = (rows, heads * D)
-        scratch = [pltpu.VMEM((1, rows), jnp.int32)] + [pltpu.VMEM(piece, BF16)] * 4 + [pltpu.SemaphoreType.DMA((9,))]
+        scratch = [pltpu.VMEM((1, rows), jnp.int32), pltpu.SemaphoreType.DMA((9,))]
         out = call(
-            body, [table] * 2 + [in_vmem(piece, BF16)] * 4 + results, [SMEM] * 4 + [HBM] * 5, [VMEM] * 8,
+            body, [table] * 2 + [in_vmem(piece, BF16)] * 8 + results, [SMEM] * 4 + [HBM] * 5, [VMEM] * 12,
             scratch, *work, "block_states",
         )(*who, tables_or_pos, *sources)
-        return out[:2], out[2:6], out[6:]
+        return out[:2], out[2:6], out[6:10], out[10:]
     return call(body, results, [SMEM] * 4 + [VMEM] * 6, [VMEM] * 2, [], *work, "block_states")(
         *who, *tables_or_pos, *sources
     )
@@ -202,17 +203,20 @@
     )(*who, *pieces)
 
 
-def local_body(q_ref, k_ref, v_ref, g_ref, cos_ref, sin_ref, rot_ref, part_ref, sc_ref):
+def local_body(*refs):
+    halves, (cos_ref, sin_ref, rot_ref, part_ref, sc_ref) = (refs[:4], refs[4:8]), refs[8:]
     cosine, sine = cos_ref[...], sin_ref[...]
-    rows = q_ref.shape[0]
+    rows = cosine.shape[0]
     row = lax.broadcasted_iota(jnp.int32, (rows, rows), 0)
     col = lax.broadcasted_iota(jnp.int32, (rows, rows), 1)
+    heads = rot_ref.shape[0]
 
     def scores(a, b, kept):
         return jnp.where(kept, dot(a, b, 1, 1), 0.0).astype(BF16)
 
-    for h in range(rot_ref.shape[0]):
-        cols = slice(h * D, (h + 1) * D)
+    for h in range(heads):
+        k_ref, v_ref, q_ref, g_ref = halves[h // (heads // 2)]
+        cols = slice(h % (heads // 2) * D, (h % (heads // 2) + 1) * D)
         krot = rotate(k_ref[:, cols], cosine, sine).astype(BF16)
         qrot = rotate(q_ref[:, cols], cosine, sine).astype(BF16)
         v, g = v_ref[:, cols], g_ref[:, cols]
@@ -222,18 +226,19 @@
         sc_ref[h, 1] = scores(g, v, row >= col)
         sc_ref[h, 2] = scores(v, g, row <= col)
         sc_ref[h, 3] = scores(krot, qrot, row <= col)
-    for h in range(rot_ref.shape[0]):
+    for h in range(heads):
         for i, other in enumerate((2, 3, 0, 1)):
             part_ref[h, i] = dot(sc_ref[h, i], rot_ref[h, other], 1, 0)
 
 
-def local_parts(q, k, v, g, cosine, sine, heads):
-    rows = q.shape[0]
+def local_parts(near, far, tables, heads):
+    rows = near[0].shape[0]
     return call(
         local_body,
         [in_vmem((heads, 4, rows, D), BF16), in_vmem((heads, 4, rows, D))],
-        [VMEM] * 6, [VMEM] * 2, [pltpu.VMEM((heads, 4, rows, rows), BF16)], 16 * heads * rows * D * D, 16 * rows * heads * D * 2, "local_parts",
-    )(q, k, v, g, cosine, sine)
+        [VMEM] * 10, [VMEM] * 2, [pltpu.VMEM((heads, 4, rows, rows), BF16)], 16 * heads * rows * D * D,
+        16 * rows * heads * D * 2, "local_parts",
+    )(*near, *far, *tables)
 
 
 def outputs_body(scale, per, jobs, arrays, prior, spots, core, me, _, __, rot_ref, part_ref, cos_ref, sin_ref, *refs):
@@ -258,7 +263,7 @@
                     state = pieces[first][spot * per + i, side]
                 state_ref[n, side, at] = state.astype(BF16)
         before, after = state_ref[n, 0], state_ref[n, 1]
-        at = (core if mine else 1 - core) * half + head
+        at = head if mine else half + head
         att = part_ref[at, 0] + dot(rot_ref[at, 0], before, 1, 0)
         rqg = part_ref[at, 1] + dot(rot_ref[at, 1], before, 1, 1)
         rkg = part_ref[at, 2] + dot(rot_ref[at, 2], after, 1, 1)
@@ -267,8 +272,9 @@
         held[n, 1] = unrotate(scale * rqg, cosine, sine).astype(BF16)
         held[n, 2] = unrotate(scale * rkg, cosine, sine).astype(BF16)
         held[n, 3] = (scale * vg).astype(BF16)
+        column = ((core if mine else 1 - core) * half + head) * D
         for i in range(4):
-            cols = pl.ds(pl.multiple_of(at * D, D), D)
+            cols = pl.ds(pl.multiple_of(column, D), D)
             copies.append(pltpu.make_async_copy(held.at[n, i], outs[i].at[:, cols], sems.at[n, i]))
             copies[-1].start()
     for copy in copies:
@@ -374,15 +380,16 @@
     spots = {mask: (which, group.index(mask)) for which, group in enumerate(sets) for mask in group}
 
     sources = [pltpu.with_memory_space_constraint(a, pltpu.HBM) for a in (k, v, q, g)]
-    tables, nearby, far = states(who, True, per, sets, sources, pltpu.with_memory_space_constraint(pos, pltpu.HBM))
-    near_other = [swap(value, "core") for value in far]
+    tables, faraway, nearby, far = states(who, True, per, sets, sources, pltpu.with_memory_space_constraint(pos, pltpu.HBM))
     near = states(who, False, per, sets, nearby, tables)
+    held_back, near = barrier(far[1], near)
+    near_other = [swap(far[0], "core"), swap(held_back, "core")]
     summed = [add(*pair) for pair in zip(near, near_other)]
     pieces = {mask * per + i: summed[which][n * per + i] for mask, (which, n) in spots.items() for i in range(per)}
     pieces = [pieces[m] for m in range(members)]
     pieces[order[0]], tables = barrier(pieces[order[0]], tables)
     arrived = exchange(pieces, order)
-    rot, local = local_parts(q, k, v, g, *tables, heads)
+    rot, local = local_parts(nearby, faraway, tables, heads)
     listed, rot, local = barrier([arrived[m] for m in order], rot, local)
     arrived = [pieces[0]] + [listed[order.index(m)] for m in range(1, members)]
 

time: 47.4 us -> 47.2 us (level)
  transfers between devices with their start and end apart: 22 -> 22, of which waited for: 10 -> 11; matrix products, arithmetic and copies ran while one was open for 0% -> 0% of each run, Pallas kernels for 13% -> 13%
where the time goes in v7:
time: 47.2 us; the launch traced here: 47.1 us
  starting transfers between devices  24.7 us (52%)
  waiting for transfers between devices  12.1 us (26%)
  Pallas kernels  9.52 us (20%)
  between operations  0.78 us (2%)
    ppermute x14, starting transfers between devices, send_to(): return lax.ppermute(value, AXES, pairs)  20.7 us
    ppermute x14, waiting for transfers between devices, send_to(): return lax.ppermute(value, AXES, pairs)  8.22 us
    pallas_call x3, Pallas kernels, outputs(): call(functools.partial(outputs_body, scale, per, jobs, len(pieces), len(p...  4.18 us
    ppermute x8, starting transfers between devices, swap(): return lax.ppermute(value, axis, [(0, 1), (1, 0)])  3.99 us
    ppermute x8, waiting for transfers between devices, swap(): return lax.ppermute(value, axis, [(0, 1), (1, 0)])  3.84 us
    pallas_call x1, Pallas kernels, local_parts(): call(local_body, [in_vmem((heads, 4, rows, D), BF16), in_vmem((heads, 4,...  2.2 us
    pallas_call x1, Pallas kernels, states(): call(body, [table] * 2 + [in_vmem(piece, BF16)] * 8 + results, [SMEM] * 4...  1.87 us
  transfers between devices with their start and end apart: 22, of which 11 were waited for; matrix products, arithmetic and copies ran while one was open for 0% of the time, Pallas kernels for 13%

profile of v7, /device:TPU:0, one launch (start us, length us, event | category | flops | bytes accessed | tf_op | source)
XLA Modules:
  0.0 47.1 jit_solution(18215746282178294649)
XLA Ops:
  0.6 1.9 %block_states.2 = (f32[128,128]{1,0:T(8,128)S(1)}, f32[128,128]{1,0:T(8,128)S(1)}, bf16[128,1024]{1,0:T(8,128)(2,1)S(1)}, bf16[128,1024]{1,0:T(8,128)(2,1)S(1)},...) custom-call(s32[1]{0:T(128)} %bitcast._.core.___.__, ...), custom_call_target="tpu_custom_call" | custom-call | flops 67108864 | bytes 2097152 | tf_op jit(solution)/shard_map/block_states/pallas_call | solution.py:117
  2.5 0.5 %collective-permute-start = (f32[4,2,128,128]{3,2,1,0:T(8,128)S(1)}, f32[4,2,128,128]{3,2,1,0:T(8,128)S(1)}, u32[]{:S(2)}, u32[]{:S(2)}) collective-permute-start(f32[4,2,128,128]{3,2,1,0:T(8,128)S(1)} %get-tuple-element.89), channel_id=1, source_target_pairs={{0,8},{8,0},{1,9},{9,1},{2,10},{10,2},{3,11},{11,3},{4,12},{12,4},... | collective-permute-start | bytes 1572872 | tf_op jit(solution)/shard_map/ppermute | solution.py:332
  3.0 0.7 %block_states.3 = (f32[4,2,128,128]{3,2,1,0:T(8,128)S(1)}, f32[4,2,128,128]{3,2,1,0:T(8,128)S(1)}) custom-call(s32[1]{0:T(128)} %bitcast._.core.___.__, s32[1]{0:T(128)} %bitcast.1.me.__._, s32[1]{0:T(128)} %bitcast.2.__.group._, s32[1]{0:T(128)} %bitcast._.core.___.__, f32[128,128]{1,0:T(8,128)S(1)} %get-tuple-element.104.refs_0_.refs_8_.cos_ref, ...), custom_call_target="tpu_custom_call" | custom-call | flops 67108864 | bytes 2097152 | tf_op jit(solution)/shard_map/block_states/pallas_call | solution.py:122
  3.8 0.8 %collective-permute-done.b_ref.refs_0_ = f32[4,2,128,128]{3,2,1,0:T(8,128)S(1)} collective-permute-done((f32[4,2,128,128]{3,2,1,0:T(8,128)S(1)}, f32[4,2,128,128]{3,2,1,0:T(8,128)S(1)}, u32[]{:S(2)}, u32[]{:S(2)}) %collective-permute-start) | collective-permute-done | bytes 524320 | tf_op jit(solution)/shard_map/ppermute | solution.py:332
  4.6 2.9 %collective-permute-start.1 = (f32[2,128,128]{2,1,0:T(8,128)S(1)}, f32[2,128,128]{2,1,0:T(8,128)S(1)}, u32[]{:S(2)}, u32[]{:S(2)}) collective-permute-start(f32[2,128,128]{2,1,0:T(8,128)S(1)} %get-tuple-element.91), channel_id=1, source_target_pairs={{0,16},{1,17},{2,18},{3,19},{16,0},{17,1},{18,2},{19,3},{4,20},{5,... | collective-permute-start | bytes 393224 | tf_op jit(solution)/shard_map/ppermute | solution.py:346
  7.6 2.5 %collective-permute-start.2 = (f32[2,128,128]{2,1,0:T(8,128)S(1)}, f32[2,128,128]{2,1,0:T(8,128)S(1)}, u32[]{:S(2)}, u32[]{:S(2)}) collective-permute-start(f32[2,128,128]{2,1,0:T(8,128)S(1)} %get-tuple-element.92), channel_id=1, source_target_pairs={{0,3},{1,2},{2,1},{3,0},{16,19},{17,18},{18,17},{19,16},{4,7},{5,6... | collective-permute-start | bytes 393224 | tf_op jit(solution)/shard_map/ppermute | solution.py:346
  10.7 2.0 %collective-permute-start.6 = (f32[2,128,128]{2,1,0:T(8,128)S(1)}, f32[2,128,128]{2,1,0:T(8,128)S(1)}, u32[]{:S(2)}, u32[]{:S(2)}) collective-permute-start(f32[2,128,128]{2,1,0:T(8,128)S(1)} %get-tuple-element.97), channel_id=1, source_target_pairs={{0,2},{1,3},{2,0},{3,1},{16,18},{17,19},{18,16},{19,17},{4,6},{5,7... | collective-permute-start | bytes 393224 | tf_op jit(solution)/shard_map/ppermute | solution.py:346
  12.7 2.5 %collective-permute-start.7 = (f32[2,128,128]{2,1,0:T(8,128)S(1)}, f32[2,128,128]{2,1,0:T(8,128)S(1)}, u32[]{:S(2)}, u32[]{:S(2)}) collective-permute-start(f32[2,128,128]{2,1,0:T(8,128)S(1)} %get-tuple-element.98), channel_id=1, source_target_pairs={{0,17},{1,16},{2,19},{3,18},{16,1},{17,0},{18,3},{19,2},{4,21},{5,... | collective-permute-start | bytes 393224 | tf_op jit(solution)/shard_map/ppermute | solution.py:346
  15.2 2.2 %collective-permute-start.8 = (f32[2,128,128]{2,1,0:T(8,128)S(1)}, f32[2,128,128]{2,1,0:T(8,128)S(1)}, u32[]{:S(2)}, u32[]{:S(2)}) collective-permute-start(f32[2,128,128]{2,1,0:T(8,128)S(1)} %get-tuple-element.99), channel_id=1, source_target_pairs={{0,19},{1,18},{2,17},{3,16},{16,3},{17,2},{18,1},{19,0},{4,23},{5,... | collective-permute-start | bytes 393224 | tf_op jit(solution)/shard_map/ppermute | solution.py:346
  17.3 2.2 %local_parts.1 = (bf16[16,4,128,128]{3,2,1,0:T(8,128)(2,1)S(1)}, f32[16,4,128,128]{3,2,1,0:T(8,128)S(1)}) custom-call(bf16[128,1024]{1,0:T(8,128)(2,1)S(1)} %get-tuple-element.82.refs_2_.refs_0_, bf16[128,1024]{1,0:T(8,128)(2,1)S(1)} %get-tuple-element.83.refs_3_.refs_1_, bf16[128,1024]{1,0:T(8,128)(2,1)S(1)} %get-tuple-element.84.refs_4_.refs_2_, ...), custom_call_target="tpu_custom_call" | custom-call | flops 536870912 | bytes 8388608 | tf_op jit(solution)/shard_map/local_parts/pallas_call | solution.py:236
  19.6 0.9 %collective-permute-done.6.refs_4_ = f32[2,128,128]{2,1,0:T(8,128)S(1)} collective-permute-done((f32[2,128,128]{2,1,0:T(8,128)S(1)}, f32[2,128,128]{2,1,0:T(8,128)S(1)}, u32[]{:S(2)}, u32[]{:S(2)}) %collective-permute-start.6) | collective-permute-done | bytes 131104 | tf_op jit(solution)/shard_map/ppermute | solution.py:346
  20.5 0.8 %collective-permute-done.7.refs_3_ = f32[2,128,128]{2,1,0:T(8,128)S(1)} collective-permute-done((f32[2,128,128]{2,1,0:T(8,128)S(1)}, f32[2,128,128]{2,1,0:T(8,128)S(1)}, u32[]{:S(2)}, u32[]{:S(2)}) %collective-permute-start.7) | collective-permute-done | bytes 131104 | tf_op jit(solution)/shard_map/ppermute | solution.py:346
  21.4 1.4 %collective-permute-done.8.refs_7_ = f32[2,128,128]{2,1,0:T(8,128)S(1)} collective-permute-done((f32[2,128,128]{2,1,0:T(8,128)S(1)}, f32[2,128,128]{2,1,0:T(8,128)S(1)}, u32[]{:S(2)}, u32[]{:S(2)}) %collective-permute-start.8) | collective-permute-done | bytes 131104 | tf_op jit(solution)/shard_map/ppermute | solution.py:346
  22.8 2.7 %collective-permute-start.9 = (f32[1,128,128]{2,1,0:T(8,128)S(1)}, f32[1,128,128]{2,1,0:T(8,128)S(1)}, u32[]{:S(2)}, u32[]{:S(2)}) collective-permute-start(f32[1,128,128]{2,1,0:T(8,128)S(1)} %block_total.1), channel_id=1, source_target_pairs={{0,4},{4,0},{1,5},{5,1},{2,6},{6,2},{3,7},{7,3},{8,12},{12,8},{9,1... | collective-permute-start | bytes 196616 | tf_op jit(solution)/shard_map/ppermute | solution.py:332
  25.7 3.1 %collective-permute-done.9.passed_ref = f32[1,128,128]{2,1,0:T(8,128)S(1)} collective-permute-done((f32[1,128,128]{2,1,0:T(8,128)S(1)}, f32[1,128,128]{2,1,0:T(8,128)S(1)}, u32[]{:S(2)}, u32[]{:S(2)}) %collective-permute-start.9) | collective-permute-done | bytes 65568 | tf_op jit(solution)/shard_map/ppermute | solution.py:332
  29.1 2.6 %collective-permute-start.15 = (f32[2,128,128]{2,1,0:T(8,128)S(1)}, f32[2,128,128]{2,1,0:T(8,128)S(1)}, u32[]{:S(2)}, u32[]{:S(2)}) collective-permute-start(f32[2,128,128]{2,1,0:T(8,128)S(1)} %get-tuple-element.131), channel_id=1, source_target_pairs={{0,3},{1,2},{2,1},{3,0},{16,19},{17,18},{18,17},{19,16},{4,7},{5,6... | collective-permute-start | bytes 393224 | tf_op jit(solution)/shard_map/ppermute | solution.py:346
  32.1 1.8 %collective-permute-start.19 = (f32[2,128,128]{2,1,0:T(8,128)S(1)}, f32[2,128,128]{2,1,0:T(8,128)S(1)}, u32[]{:S(2)}, u32[]{:S(2)}) collective-permute-start(f32[2,128,128]{2,1,0:T(8,128)S(1)} %get-tuple-element.133), channel_id=1, source_target_pairs={{0,18},{1,19},{2,16},{3,17},{16,2},{17,3},{18,0},{19,1},{4,22},{5,... | collective-permute-start | bytes 393224 | tf_op jit(solution)/shard_map/ppermute | solution.py:346
  34.2 2.0 %collective-permute-done.13.refs_0_.refs_3_ = f32[2,128,128]{2,1,0:T(8,128)S(1)} collective-permute-done((f32[2,128,128]{2,1,0:T(8,128)S(1)}, f32[2,128,128]{2,1,0:T(8,128)S(1)}, u32[]{:S(2)}, u32[]{:S(2)}) %collective-permute-start.13) | collective-permute-done | bytes 131104 | tf_op jit(solution)/shard_map/ppermute | solution.py:346
  36.2 0.6 %collective-permute-start.11 = (f32[2,128,128]{2,1,0:T(8,128)S(1)}, f32[2,128,128]{2,1,0:T(8,128)S(1)}, u32[]{:S(2)}, u32[]{:S(2)}) collective-permute-start(f32[2,128,128]{2,1,0:T(8,128)S(1)} %get-tuple-element.127), channel_id=1, source_target_pairs={{0,17},{1,16},{2,19},{3,18},{16,1},{17,0},{18,3},{19,2},{4,21},{5,... | collective-permute-start | bytes 393224 | tf_op jit(solution)/shard_map/ppermute | solution.py:346
  36.9 2.0 %collective-permute-start.12 = (f32[2,128,128]{2,1,0:T(8,128)S(1)}, f32[2,128,128]{2,1,0:T(8,128)S(1)}, u32[]{:S(2)}, u32[]{:S(2)}) collective-permute-start(f32[2,128,128]{2,1,0:T(8,128)S(1)} %get-tuple-element.128), channel_id=1, source_target_pairs={{0,19},{1,18},{2,17},{3,16},{16,3},{17,2},{18,1},{19,0},{4,23},{5,... | collective-permute-start | bytes 393224 | tf_op jit(solution)/shard_map/ppermute | solution.py:346
  40.1 2.0 %collective-permute-done.11.refs_1_.refs_3_ = f32[2,128,128]{2,1,0:T(8,128)S(1)} collective-permute-done((f32[2,128,128]{2,1,0:T(8,128)S(1)}, f32[2,128,128]{2,1,0:T(8,128)S(1)}, u32[]{:S(2)}, u32[]{:S(2)}) %collective-permute-start.11) | collective-permute-done | bytes 131104 | tf_op jit(solution)/shard_map/ppermute | solution.py:346
  42.1 1.4 %block_outputs.3 = (bf16[128,2048]{1,0:T(8,128)(2,1)}, bf16[128,2048]{1,0:T(8,128)(2,1)}, bf16[128,2048]{1,0:T(8,128)(2,1)}, bf16[128,2048]{1,0:T(8,128)(2,1)}) custom-call(s32[1]{0:T(128)} %bitcast._.core.___.__, s32[1]{0:T(128)} %bitcast.1.me.__._, s32[1]{0:T(128)} %bitcast.2.__.group._, s32[1]{0:T(128)} %bitcast._.core.___.__, ...), custom_call_target="tpu_custom_call" | custom-call | flops 83886080 | bytes 2621440 | tf_op jit(solution)/shard_map/block_outputs/pallas_call | solution.py:294
  44.2 1.6 %block_outputs.4 = (bf16[128,2048]{1,0:T(8,128)(2,1)}, bf16[128,2048]{1,0:T(8,128)(2,1)}, bf16[128,2048]{1,0:T(8,128)(2,1)}, bf16[128,2048]{1,0:T(8,128)(2,1)}) custom-call(s32[1]{0:T(128)} %bitcast._.core.___.__, s32[1]{0:T(128)} %bitcast.1.me.__._, ...), custom_call_target="tpu_custom_call", output_to_operand_aliasing={{0}: (17, {}), {1}: (18, {}), {2}: (19, {}), {3}: (20, {})} | custom-call | flops 117440512 | bytes 3670016 | tf_op jit(solution)/shard_map/block_outputs/pallas_call | solution.py:294
  45.8 1.3 %block_outputs.5 = (bf16[128,2048]{1,0:T(8,128)(2,1)}, bf16[128,2048]{1,0:T(8,128)(2,1)}, bf16[128,2048]{1,0:T(8,128)(2,1)}, bf16[128,2048]{1,0:T(8,128)(2,1)}) custom-call(s32[1]{0:T(128)} %bitcast._.core.___.__, s32[1]{0:T(128)} %bitcast.1.me.__._, ...), custom_call_target="tpu_custom_call", output_to_operand_aliasing={{0}: (11, {}), {1}: (12, {}), {2}: (13, {}), {3}: (14, {})} | custom-call | flops 67108864 | bytes 2097152 | tf_op jit(solution)/shard_map/block_outputs/pallas_call | solution.py:294
  (36 shorter events, 4.0 us)
Async XLA Ops:
  2.5 2.1 %collective-permute-start = (f32[4,2,128,128]{3,2,1,0:T(8,128)S(1)}, f32[4,2,128,128]{3,2,1,0:T(8,128)S(1)}, u32[]{:S(2)}, u32[]{:S(2)}) collective-permute-start(f32[4,2,128,128]{3,2,1,0:T(8,128)S(1)} %get-tuple-element.89), channel_id=1, source_target_pairs={{0,8},{8,0},{1,9},{9,1},{2,10},{10,2},{3,11},{11,3},{4,12},{12,4},... | collective-permute-start | bytes 1572872 | tf_op jit(solution)/shard_map/ppermute | solution.py:332
  3.7 6.9 %collective-permute-start.5 = (f32[4,2,128,128]{3,2,1,0:T(8,128)S(1)}, f32[4,2,128,128]{3,2,1,0:T(8,128)S(1)}, u32[]{:S(2)}, u32[]{:S(2)}) collective-permute-start(f32[4,2,128,128]{3,2,1,0:T(8,128)S(1)} %get-tuple-element.96), channel_id=1, source_target_pairs={{0,8},{8,0},{1,9},{9,1},{2,10},{10,2},{3,11},{11,3},{4,12},{12,4},... | collective-permute-start | bytes 1572872 | tf_op jit(solution)/shard_map/ppermute | solution.py:332
  4.6 8.1 %collective-permute-start.1 = (f32[2,128,128]{2,1,0:T(8,128)S(1)}, f32[2,128,128]{2,1,0:T(8,128)S(1)}, u32[]{:S(2)}, u32[]{:S(2)}) collective-permute-start(f32[2,128,128]{2,1,0:T(8,128)S(1)} %get-tuple-element.91), channel_id=1, source_target_pairs={{0,16},{1,17},{2,18},{3,19},{16,0},{17,1},{18,2},{19,3},{4,20},{5,... | collective-permute-start | bytes 393224 | tf_op jit(solution)/shard_map/ppermute | solution.py:346
  7.6 7.6 %collective-permute-start.2 = (f32[2,128,128]{2,1,0:T(8,128)S(1)}, f32[2,128,128]{2,1,0:T(8,128)S(1)}, u32[]{:S(2)}, u32[]{:S(2)}) collective-permute-start(f32[2,128,128]{2,1,0:T(8,128)S(1)} %get-tuple-element.92), channel_id=1, source_target_pairs={{0,3},{1,2},{2,1},{3,0},{16,19},{17,18},{18,17},{19,16},{4,7},{5,6... | collective-permute-start | bytes 393224 | tf_op jit(solution)/shard_map/ppermute | solution.py:346
  10.1 9.5 %collective-permute-start.3 = (f32[2,128,128]{2,1,0:T(8,128)S(1)}, f32[2,128,128]{2,1,0:T(8,128)S(1)}, u32[]{:S(2)}, u32[]{:S(2)}) collective-permute-start(f32[2,128,128]{2,1,0:T(8,128)S(1)} %get-tuple-element.93), channel_id=1, source_target_pairs={{0,1},{1,0},{2,3},{3,2},{16,17},{17,16},{18,19},{19,18},{4,5},{5,4... | collective-permute-start | bytes 393224 | tf_op jit(solution)/shard_map/ppermute | solution.py:346
  10.6 9.0 %collective-permute-start.4 = (f32[2,128,128]{2,1,0:T(8,128)S(1)}, f32[2,128,128]{2,1,0:T(8,128)S(1)}, u32[]{:S(2)}, u32[]{:S(2)}) collective-permute-start(f32[2,128,128]{2,1,0:T(8,128)S(1)} %get-tuple-element.94), channel_id=1, source_target_pairs={{0,18},{1,19},{2,16},{3,17},{16,2},{17,3},{18,0},{19,1},{4,22},{5,... | collective-permute-start | bytes 393224 | tf_op jit(solution)/shard_map/ppermute | solution.py:346
  10.7 9.8 %collective-permute-start.6 = (f32[2,128,128]{2,1,0:T(8,128)S(1)}, f32[2,128,128]{2,1,0:T(8,128)S(1)}, u32[]{:S(2)}, u32[]{:S(2)}) collective-permute-start(f32[2,128,128]{2,1,0:T(8,128)S(1)} %get-tuple-element.97), channel_id=1, source_target_pairs={{0,2},{1,3},{2,0},{3,1},{16,18},{17,19},{18,16},{19,17},{4,6},{5,7... | collective-permute-start | bytes 393224 | tf_op jit(solution)/shard_map/ppermute | solution.py:346
  12.7 8.6 %collective-permute-start.7 = (f32[2,128,128]{2,1,0:T(8,128)S(1)}, f32[2,128,128]{2,1,0:T(8,128)S(1)}, u32[]{:S(2)}, u32[]{:S(2)}) collective-permute-start(f32[2,128,128]{2,1,0:T(8,128)S(1)} %get-tuple-element.98), channel_id=1, source_target_pairs={{0,17},{1,16},{2,19},{3,18},{16,1},{17,0},{18,3},{19,2},{4,21},{5,... | collective-permute-start | bytes 393224 | tf_op jit(solution)/shard_map/ppermute | solution.py:346
  15.2 7.6 %collective-permute-start.8 = (f32[2,128,128]{2,1,0:T(8,128)S(1)}, f32[2,128,128]{2,1,0:T(8,128)S(1)}, u32[]{:S(2)}, u32[]{:S(2)}) collective-permute-start(f32[2,128,128]{2,1,0:T(8,128)S(1)} %get-tuple-element.99), channel_id=1, source_target_pairs={{0,19},{1,18},{2,17},{3,16},{16,3},{17,2},{18,1},{19,0},{4,23},{5,... | collective-permute-start | bytes 393224 | tf_op jit(solution)/shard_map/ppermute | solution.py:346
  22.8 5.9 %collective-permute-start.9 = (f32[1,128,128]{2,1,0:T(8,128)S(1)}, f32[1,128,128]{2,1,0:T(8,128)S(1)}, u32[]{:S(2)}, u32[]{:S(2)}) collective-permute-start(f32[1,128,128]{2,1,0:T(8,128)S(1)} %block_total.1), channel_id=1, source_target_pairs={{0,4},{4,0},{1,5},{5,1},{2,6},{6,2},{3,7},{7,3},{8,12},{12,8},{9,1... | collective-permute-start | bytes 196616 | tf_op jit(solution)/shard_map/ppermute | solution.py:332
  28.9 7.3 %collective-permute-start.13 = (f32[2,128,128]{2,1,0:T(8,128)S(1)}, f32[2,128,128]{2,1,0:T(8,128)S(1)}, u32[]{:S(2)}, u32[]{:S(2)}) collective-permute-start(f32[2,128,128]{2,1,0:T(8,128)S(1)} %get-tuple-element.130), channel_id=1, source_target_pairs={{0,16},{1,17},{2,18},{3,19},{16,0},{17,1},{18,2},{19,3},{4,20},{5,... | collective-permute-start | bytes 393224 | tf_op jit(solution)/shard_map/ppermute | solution.py:346
  29.1 7.9 %collective-permute-start.15 = (f32[2,128,128]{2,1,0:T(8,128)S(1)}, f32[2,128,128]{2,1,0:T(8,128)S(1)}, u32[]{:S(2)}, u32[]{:S(2)}) collective-permute-start(f32[2,128,128]{2,1,0:T(8,128)S(1)} %get-tuple-element.131), channel_id=1, source_target_pairs={{0,3},{1,2},{2,1},{3,0},{16,19},{17,18},{18,17},{19,16},{4,7},{5,6... | collective-permute-start | bytes 393224 | tf_op jit(solution)/shard_map/ppermute | solution.py:346
  31.6 7.4 %collective-permute-start.17 = (f32[2,128,128]{2,1,0:T(8,128)S(1)}, f32[2,128,128]{2,1,0:T(8,128)S(1)}, u32[]{:S(2)}, u32[]{:S(2)}) collective-permute-start(f32[2,128,128]{2,1,0:T(8,128)S(1)} %get-tuple-element.132), channel_id=1, source_target_pairs={{0,1},{1,0},{2,3},{3,2},{16,17},{17,16},{18,19},{19,18},{4,5},{5,4... | collective-permute-start | bytes 393224 | tf_op jit(solution)/shard_map/ppermute | solution.py:346
  32.1 7.4 %collective-permute-start.19 = (f32[2,128,128]{2,1,0:T(8,128)S(1)}, f32[2,128,128]{2,1,0:T(8,128)S(1)}, u32[]{:S(2)}, u32[]{:S(2)}) collective-permute-start(f32[2,128,128]{2,1,0:T(8,128)S(1)} %get-tuple-element.133), channel_id=1, source_target_pairs={{0,18},{1,19},{2,16},{3,17},{16,2},{17,3},{18,0},{19,1},{4,22},{5,... | collective-permute-start | bytes 393224 | tf_op jit(solution)/shard_map/ppermute | solution.py:346
  33.9 6.2 %collective-permute-start.10 = (f32[2,128,128]{2,1,0:T(8,128)S(1)}, f32[2,128,128]{2,1,0:T(8,128)S(1)}, u32[]{:S(2)}, u32[]{:S(2)}) collective-permute-start(f32[2,128,128]{2,1,0:T(8,128)S(1)} %get-tuple-element.126), channel_id=1, source_target_pairs={{0,2},{1,3},{2,0},{3,1},{16,18},{17,19},{18,16},{19,17},{4,6},{5,7... | collective-permute-start | bytes 393224 | tf_op jit(solution)/shard_map/ppermute | solution.py:346
  36.2 5.9 %collective-permute-start.11 = (f32[2,128,128]{2,1,0:T(8,128)S(1)}, f32[2,128,128]{2,1,0:T(8,128)S(1)}, u32[]{:S(2)}, u32[]{:S(2)}) collective-permute-start(f32[2,128,128]{2,1,0:T(8,128)S(1)} %get-tuple-element.127), channel_id=1, source_target_pairs={{0,17},{1,16},{2,19},{3,18},{16,1},{17,0},{18,3},{19,2},{4,21},{5,... | collective-permute-start | bytes 393224 | tf_op jit(solution)/shard_map/ppermute | solution.py:346
  36.9 6.8 %collective-permute-start.12 = (f32[2,128,128]{2,1,0:T(8,128)S(1)}, f32[2,128,128]{2,1,0:T(8,128)S(1)}, u32[]{:S(2)}, u32[]{:S(2)}) collective-permute-start(f32[2,128,128]{2,1,0:T(8,128)S(1)} %get-tuple-element.128), channel_id=1, source_target_pairs={{0,19},{1,18},{2,17},{3,16},{16,3},{17,2},{18,1},{19,0},{4,23},{5,... | collective-permute-start | bytes 393224 | tf_op jit(solution)/shard_map/ppermute | solution.py:346
  39.0 4.7 %collective-permute-start.14 = (f32[1,2,128,128]{3,2,1,0:T(8,128)S(1)}, f32[1,2,128,128]{3,2,1,0:T(8,128)S(1)}, u32[]{:S(2)}, u32[]{:S(2)}) collective-permute-start(f32[1,2,128,128]{3,2,1,0:T(8,128)S(1)} %sibling_state.5), channel_id=1, source_target_pairs={{0,8},{8,0},{1,9},{9,1},{2,10},{10,2},{3,11},{11,3},{4,12},{12,4},... | collective-permute-start | bytes 393224 | tf_op jit(solution)/shard_map/ppermute | solution.py:332
  39.5 4.2 %collective-permute-start.16 = (f32[1,2,128,128]{3,2,1,0:T(8,128)S(1)}, f32[1,2,128,128]{3,2,1,0:T(8,128)S(1)}, u32[]{:S(2)}, u32[]{:S(2)}) collective-permute-start(f32[1,2,128,128]{3,2,1,0:T(8,128)S(1)} %sibling_state.6), channel_id=1, source_target_pairs={{0,8},{8,0},{1,9},{9,1},{2,10},{10,2},{3,11},{11,3},{4,12},{12,4},... | collective-permute-start | bytes 393224 | tf_op jit(solution)/shard_map/ppermute | solution.py:332
  40.1 3.7 %collective-permute-start.18 = (f32[1,2,128,128]{3,2,1,0:T(8,128)S(1)}, f32[1,2,128,128]{3,2,1,0:T(8,128)S(1)}, u32[]{:S(2)}, u32[]{:S(2)}) collective-permute-start(f32[1,2,128,128]{3,2,1,0:T(8,128)S(1)} %sibling_state.7), channel_id=1, source_target_pairs={{0,8},{8,0},{1,9},{9,1},{2,10},{10,2},{3,11},{11,3},{4,12},{12,4},... | collective-permute-start | bytes 393224 | tf_op jit(solution)/shard_map/ppermute | solution.py:332
  42.1 1.6 %collective-permute-start.20 = (f32[1,2,128,128]{3,2,1,0:T(8,128)S(1)}, f32[1,2,128,128]{3,2,1,0:T(8,128)S(1)}, u32[]{:S(2)}, u32[]{:S(2)}) collective-permute-start(f32[1,2,128,128]{3,2,1,0:T(8,128)S(1)} %sibling_state.8), channel_id=1, source_target_pairs={{0,8},{8,0},{1,9},{9,1},{2,10},{10,2},{3,11},{11,3},{4,12},{12,4},... | collective-permute-start | bytes 393224 | tf_op jit(solution)/shard_map/ppermute | solution.py:332
  43.8 2.0 %collective-permute-start.21 = (f32[4,2,128,128]{3,2,1,0:T(8,128)S(1)}, f32[4,2,128,128]{3,2,1,0:T(8,128)S(1)}, u32[]{:S(2)}, u32[]{:S(2)}) collective-permute-start(f32[4,2,128,128]{3,2,1,0:T(8,128)S(1)} %sibling_state.9), channel_id=1, source_target_pairs={{0,8},{8,0},{1,9},{9,1},{2,10},{10,2},{3,11},{11,3},{4,12},{12,4},... | collective-permute-start | bytes 1572872 | tf_op jit(solution)/shard_map/ppermute | solution.py:332

commit v8 on v7

--- a/solution.py
+++ b/solution.py
@@ -52,13 +52,11 @@
 def rotary_tables(positions):
     rows = positions.shape[1]
     half = D // 2
-    lane = lax.broadcasted_iota(jnp.int32, (rows, D), 1)
-    index = jnp.where(lane < half, lane, lane - half).astype(F32)
+    index = lax.broadcasted_iota(jnp.int32, (half, rows), 0).astype(F32)
     frequency = jnp.exp(index * (-2.0 * math.log(500000.0) / D))
-    place = jnp.broadcast_to(positions.astype(F32), (D, rows)).T
-    angle = place * frequency
-    sine = jnp.sin(angle)
-    return jnp.cos(angle), jnp.where(lane < half, -sine, sine)
+    angle = positions.astype(F32) * frequency
+    cosine, sine = jnp.cos(angle), jnp.sin(angle)
+    return jnp.concatenate([cosine, cosine], 0).T, jnp.concatenate([-sine, sine], 0).T
 
 
 def states_body(first, per, sets, _, me, __, core, *refs):
@@ -371,10 +369,9 @@
     per = members // part
     pos = positions.reshape(1, rows)
 
-    order = []
-    for m in sorted(range(1, members - 1), key=lambda m: (bin(m).count("1"), m))[: members // 2 - 1]:
-        order += [m, members - 1 - m]
-    order.append(members - 1)
+    short = sorted(range(1, members - 1), key=lambda m: (bin(m).count("1"), m))[: members // 2 - 1]
+    order = [route for m in short for route in (m, members - 1 - m)] + [members - 1]
+    back = [route for m in short[:1] + short[:0:-1] for route in (m, members - 1 - m)] + [members - 1]
     masks = list(dict.fromkeys([m // per for m in order] + [0]))
     sets = masks[: part // 2], masks[part // 2 :]
     spots = {mask: (which, group.index(mask)) for which, group in enumerate(sets) for mask in group}
@@ -402,7 +399,7 @@
         wanted = jnp.where(jnp.arange(2)[:, None, None] == 0, place < group, place > group)
         passed = jnp.sum(jnp.where(wanted, every, 0.0), axis=0)
     pieces = offset(who, scan(who, arrived), passed)
-    whole = exchange(pieces, order)
+    whole = exchange(pieces, back)
 
     whole = {mask: [whole[mask * per + i] for i in range(per)] for mask in masks}
 
@@ -410,7 +407,8 @@
         listed = [piece for mask in chosen for piece in whole[mask]]
         return chosen, swap(relay(per, chosen, spots, who, near, listed), "core")
 
-    early, late = masks[: part // 2], masks[part // 2 :]
+    returned = list(dict.fromkeys([m // per for m in back] + [0]))
+    early, late = returned[: part // 2], returned[part // 2 :]
     soon = list(dict.fromkeys([0, *early]))
     first = [pass_on([mask]) for mask in early]
     finish = functools.partial(outputs, scale, per, spots, who, rot, local, tables, near_other)

time: 47.2 us -> 46.9 us (level)
  waiting for transfers between devices: 12.1 us -> 9.91 us
  starting transfers between devices: 24.7 us -> 26.6 us
    ppermute x14, waiting for transfers between devices: 8.22 us -> 5.76 us  [send_to(): return lax.ppermute(value, AXES, pairs)]
    ppermute x14, starting transfers between devices: 20.7 us -> 22.1 us  [send_to(): return lax.ppermute(value, AXES, pairs)]
    ppermute x8, starting transfers between devices: 3.99 us -> 4.5 us  [swap(): return lax.ppermute(value, axis, [(0, 1), (1, 0)])]
  transfers between devices with their start and end apart: 22 -> 22, of which waited for: 11 -> 9; matrix products, arithmetic and copies ran while one was open for 0% -> 0% of each run, Pallas kernels for 13% -> 13%
where the time goes in v8:
time: 46.9 us; the launch traced here: 46.8 us
  starting transfers between devices  26.6 us (57%)
  waiting for transfers between devices  9.91 us (21%)
  Pallas kernels  9.52 us (20%)
  between operations  0.8 us (2%)
    ppermute x14, starting transfers between devices, send_to(): return lax.ppermute(value, AXES, pairs)  22.1 us
    ppermute x14, waiting for transfers between devices, send_to(): return lax.ppermute(value, AXES, pairs)  5.76 us
    ppermute x8, starting transfers between devices, swap(): return lax.ppermute(value, axis, [(0, 1), (1, 0)])  4.5 us
    pallas_call x3, Pallas kernels, outputs(): call(functools.partial(outputs_body, scale, per, jobs, len(pieces), len(p...  4.18 us
    ppermute x8, waiting for transfers between devices, swap(): return lax.ppermute(value, axis, [(0, 1), (1, 0)])  4.14 us
    pallas_call x1, Pallas kernels, local_parts(): call(local_body, [in_vmem((heads, 4, rows, D), BF16), in_vmem((heads, 4,...  2.2 us
    pallas_call x1, Pallas kernels, states(): call(body, [table] * 2 + [in_vmem(piece, BF16)] * 8 + results, [SMEM] * 4...  1.87 us
  transfers between devices with their start and end apart: 22, of which 9 were waited for; matrix products, arithmetic and copies ran while one was open for 0% of the time, Pallas kernels for 13%

profile of v8, /device:TPU:0, one launch (start us, length us, event | category | flops | bytes accessed | tf_op | source)
XLA Modules:
  0.0 46.8 jit_solution(16998677199745434125)
XLA Ops:
  0.6 1.9 %block_states.2 = (f32[128,128]{1,0:T(8,128)S(1)}, f32[128,128]{1,0:T(8,128)S(1)}, bf16[128,1024]{1,0:T(8,128)(2,1)S(1)}, bf16[128,1024]{1,0:T(8,128)(2,1)S(1)},...) custom-call(s32[1]{0:T(128)} %bitcast._.core.___.__, ...), custom_call_target="tpu_custom_call" | custom-call | flops 67108864 | bytes 2097152 | tf_op jit(solution)/shard_map/block_states/pallas_call | solution.py:115
  3.0 0.7 %block_states.3 = (f32[4,2,128,128]{3,2,1,0:T(8,128)S(1)}, f32[4,2,128,128]{3,2,1,0:T(8,128)S(1)}) custom-call(s32[1]{0:T(128)} %bitcast._.core.___.__, s32[1]{0:T(128)} %bitcast.1.me.__._, s32[1]{0:T(128)} %bitcast.2.__.group._, s32[1]{0:T(128)} %bitcast._.core.___.__, f32[128,128]{1,0:T(8,128)S(1)} %get-tuple-element.104.refs_0_.refs_8_.cos_ref, ...), custom_call_target="tpu_custom_call" | custom-call | flops 67108864 | bytes 2097152 | tf_op jit(solution)/shard_map/block_states/pallas_call | solution.py:120
  3.8 0.8 %collective-permute-done.b_ref.refs_0_ = f32[4,2,128,128]{3,2,1,0:T(8,128)S(1)} collective-permute-done((f32[4,2,128,128]{3,2,1,0:T(8,128)S(1)}, f32[4,2,128,128]{3,2,1,0:T(8,128)S(1)}, u32[]{:S(2)}, u32[]{:S(2)}) %collective-permute-start) | collective-permute-done | bytes 524320 | tf_op jit(solution)/shard_map/ppermute | solution.py:330
  4.6 2.9 %collective-permute-start.1 = (f32[2,128,128]{2,1,0:T(8,128)S(1)}, f32[2,128,128]{2,1,0:T(8,128)S(1)}, u32[]{:S(2)}, u32[]{:S(2)}) collective-permute-start(f32[2,128,128]{2,1,0:T(8,128)S(1)} %get-tuple-element.91), channel_id=1, source_target_pairs={{0,16},{1,17},{2,18},{3,19},{16,0},{17,1},{18,2},{19,3},{4,20},{5,... | collective-permute-start | bytes 393224 | tf_op jit(solution)/shard_map/ppermute | solution.py:344
  7.6 2.5 %collective-permute-start.2 = (f32[2,128,128]{2,1,0:T(8,128)S(1)}, f32[2,128,128]{2,1,0:T(8,128)S(1)}, u32[]{:S(2)}, u32[]{:S(2)}) collective-permute-start(f32[2,128,128]{2,1,0:T(8,128)S(1)} %get-tuple-element.92), channel_id=1, source_target_pairs={{0,3},{1,2},{2,1},{3,0},{16,19},{17,18},{18,17},{19,16},{4,7},{5,6... | collective-permute-start | bytes 393224 | tf_op jit(solution)/shard_map/ppermute | solution.py:344
  10.7 2.0 %collective-permute-start.6 = (f32[2,128,128]{2,1,0:T(8,128)S(1)}, f32[2,128,128]{2,1,0:T(8,128)S(1)}, u32[]{:S(2)}, u32[]{:S(2)}) collective-permute-start(f32[2,128,128]{2,1,0:T(8,128)S(1)} %get-tuple-element.97), channel_id=1, source_target_pairs={{0,2},{1,3},{2,0},{3,1},{16,18},{17,19},{18,16},{19,17},{4,6},{5,7... | collective-permute-start | bytes 393224 | tf_op jit(solution)/shard_map/ppermute | solution.py:344
  12.7 2.5 %collective-permute-start.7 = (f32[2,128,128]{2,1,0:T(8,128)S(1)}, f32[2,128,128]{2,1,0:T(8,128)S(1)}, u32[]{:S(2)}, u32[]{:S(2)}) collective-permute-start(f32[2,128,128]{2,1,0:T(8,128)S(1)} %get-tuple-element.98), channel_id=1, source_target_pairs={{0,17},{1,16},{2,19},{3,18},{16,1},{17,0},{18,3},{19,2},{4,21},{5,... | collective-permute-start | bytes 393224 | tf_op jit(solution)/shard_map/ppermute | solution.py:344
  15.2 2.2 %collective-permute-start.8 = (f32[2,128,128]{2,1,0:T(8,128)S(1)}, f32[2,128,128]{2,1,0:T(8,128)S(1)}, u32[]{:S(2)}, u32[]{:S(2)}) collective-permute-start(f32[2,128,128]{2,1,0:T(8,128)S(1)} %get-tuple-element.99), channel_id=1, source_target_pairs={{0,19},{1,18},{2,17},{3,16},{16,3},{17,2},{18,1},{19,0},{4,23},{5,... | collective-permute-start | bytes 393224 | tf_op jit(solution)/shard_map/ppermute | solution.py:344
  17.3 2.2 %local_parts.1 = (bf16[16,4,128,128]{3,2,1,0:T(8,128)(2,1)S(1)}, f32[16,4,128,128]{3,2,1,0:T(8,128)S(1)}) custom-call(bf16[128,1024]{1,0:T(8,128)(2,1)S(1)} %get-tuple-element.82.refs_2_.refs_0_, bf16[128,1024]{1,0:T(8,128)(2,1)S(1)} %get-tuple-element.83.refs_3_.refs_1_, bf16[128,1024]{1,0:T(8,128)(2,1)S(1)} %get-tuple-element.84.refs_4_.refs_2_, ...), custom_call_target="tpu_custom_call" | custom-call | flops 536870912 | bytes 8388608 | tf_op jit(solution)/shard_map/local_parts/pallas_call | solution.py:234
  19.6 1.0 %collective-permute-done.6.refs_4_ = f32[2,128,128]{2,1,0:T(8,128)S(1)} collective-permute-done((f32[2,128,128]{2,1,0:T(8,128)S(1)}, f32[2,128,128]{2,1,0:T(8,128)S(1)}, u32[]{:S(2)}, u32[]{:S(2)}) %collective-permute-start.6) | collective-permute-done | bytes 131104 | tf_op jit(solution)/shard_map/ppermute | solution.py:344
  20.5 0.9 %collective-permute-done.7.refs_3_ = f32[2,128,128]{2,1,0:T(8,128)S(1)} collective-permute-done((f32[2,128,128]{2,1,0:T(8,128)S(1)}, f32[2,128,128]{2,1,0:T(8,128)S(1)}, u32[]{:S(2)}, u32[]{:S(2)}) %collective-permute-start.7) | collective-permute-done | bytes 131104 | tf_op jit(solution)/shard_map/ppermute | solution.py:344
  21.4 1.4 %collective-permute-done.8.refs_7_ = f32[2,128,128]{2,1,0:T(8,128)S(1)} collective-permute-done((f32[2,128,128]{2,1,0:T(8,128)S(1)}, f32[2,128,128]{2,1,0:T(8,128)S(1)}, u32[]{:S(2)}, u32[]{:S(2)}) %collective-permute-start.8) | collective-permute-done | bytes 131104 | tf_op jit(solution)/shard_map/ppermute | solution.py:344
  22.8 2.7 %collective-permute-start.9 = (f32[1,128,128]{2,1,0:T(8,128)S(1)}, f32[1,128,128]{2,1,0:T(8,128)S(1)}, u32[]{:S(2)}, u32[]{:S(2)}) collective-permute-start(f32[1,128,128]{2,1,0:T(8,128)S(1)} %block_total.1), channel_id=1, source_target_pairs={{0,4},{4,0},{1,5},{5,1},{2,6},{6,2},{3,7},{7,3},{8,12},{12,8},{9,1... | collective-permute-start | bytes 196616 | tf_op jit(solution)/shard_map/ppermute | solution.py:330
  25.7 3.1 %collective-permute-done.9.passed_ref = f32[1,128,128]{2,1,0:T(8,128)S(1)} collective-permute-done((f32[1,128,128]{2,1,0:T(8,128)S(1)}, f32[1,128,128]{2,1,0:T(8,128)S(1)}, u32[]{:S(2)}, u32[]{:S(2)}) %collective-permute-start.9) | collective-permute-done | bytes 65568 | tf_op jit(solution)/shard_map/ppermute | solution.py:330
  29.0 2.6 %collective-permute-start.15 = (f32[2,128,128]{2,1,0:T(8,128)S(1)}, f32[2,128,128]{2,1,0:T(8,128)S(1)}, u32[]{:S(2)}, u32[]{:S(2)}) collective-permute-start(f32[2,128,128]{2,1,0:T(8,128)S(1)} %get-tuple-element.131), channel_id=1, source_target_pairs={{0,3},{1,2},{2,1},{3,0},{16,19},{17,18},{18,17},{19,16},{4,7},{5,6... | collective-permute-start | bytes 393224 | tf_op jit(solution)/shard_map/ppermute | solution.py:344
  32.0 1.8 %collective-permute-start.19 = (f32[2,128,128]{2,1,0:T(8,128)S(1)}, f32[2,128,128]{2,1,0:T(8,128)S(1)}, u32[]{:S(2)}, u32[]{:S(2)}) collective-permute-start(f32[2,128,128]{2,1,0:T(8,128)S(1)} %get-tuple-element.133), channel_id=1, source_target_pairs={{0,17},{1,16},{2,19},{3,18},{16,1},{17,0},{18,3},{19,2},{4,21},{5,... | collective-permute-start | bytes 393224 | tf_op jit(solution)/shard_map/ppermute | solution.py:344
  34.1 0.7 %collective-permute-done.13.refs_0_.refs_3_ = f32[2,128,128]{2,1,0:T(8,128)S(1)} collective-permute-done((f32[2,128,128]{2,1,0:T(8,128)S(1)}, f32[2,128,128]{2,1,0:T(8,128)S(1)}, u32[]{:S(2)}, u32[]{:S(2)}) %collective-permute-start.13) | collective-permute-done | bytes 131104 | tf_op jit(solution)/shard_map/ppermute | solution.py:344
  34.8 1.8 %collective-permute-start.11 = (f32[2,128,128]{2,1,0:T(8,128)S(1)}, f32[2,128,128]{2,1,0:T(8,128)S(1)}, u32[]{:S(2)}, u32[]{:S(2)}) collective-permute-start(f32[2,128,128]{2,1,0:T(8,128)S(1)} %get-tuple-element.127), channel_id=1, source_target_pairs={{0,18},{1,19},{2,16},{3,17},{16,2},{17,3},{18,0},{19,1},{4,22},{5,... | collective-permute-start | bytes 393224 | tf_op jit(solution)/shard_map/ppermute | solution.py:344
  36.6 2.4 %collective-permute-start.12 = (f32[2,128,128]{2,1,0:T(8,128)S(1)}, f32[2,128,128]{2,1,0:T(8,128)S(1)}, u32[]{:S(2)}, u32[]{:S(2)}) collective-permute-start(f32[2,128,128]{2,1,0:T(8,128)S(1)} %get-tuple-element.128), channel_id=1, source_target_pairs={{0,19},{1,18},{2,17},{3,16},{16,3},{17,2},{18,1},{19,0},{4,23},{5,... | collective-permute-start | bytes 393224 | tf_op jit(solution)/shard_map/ppermute | solution.py:344
  39.8 0.9 %collective-permute-done.10.refs_0_.refs_2_ = f32[2,128,128]{2,1,0:T(8,128)S(1)} collective-permute-done((f32[2,128,128]{2,1,0:T(8,128)S(1)}, f32[2,128,128]{2,1,0:T(8,128)S(1)}, u32[]{:S(2)}, u32[]{:S(2)}) %collective-permute-start.10) | collective-permute-done | bytes 131104 | tf_op jit(solution)/shard_map/ppermute | solution.py:344
  41.2 1.4 %block_outputs.3 = (bf16[128,2048]{1,0:T(8,128)(2,1)}, bf16[128,2048]{1,0:T(8,128)(2,1)}, bf16[128,2048]{1,0:T(8,128)(2,1)}, bf16[128,2048]{1,0:T(8,128)(2,1)}) custom-call(s32[1]{0:T(128)} %bitcast._.core.___.__, s32[1]{0:T(128)} %bitcast.1.me.__._, s32[1]{0:T(128)} %bitcast.2.__.group._, s32[1]{0:T(128)} %bitcast._.core.___.__, ...), custom_call_target="tpu_custom_call" | custom-call | flops 83886080 | bytes 2621440 | tf_op jit(solution)/shard_map/block_outputs/pallas_call | solution.py:292
  42.6 0.9 %collective-permute-done.12.refs_2_.refs_4_ = f32[2,128,128]{2,1,0:T(8,128)S(1)} collective-permute-done((f32[2,128,128]{2,1,0:T(8,128)S(1)}, f32[2,128,128]{2,1,0:T(8,128)S(1)}, u32[]{:S(2)}, u32[]{:S(2)}) %collective-permute-start.12) | collective-permute-done | bytes 131104 | tf_op jit(solution)/shard_map/ppermute | solution.py:344
  43.6 1.6 %block_outputs.4 = (bf16[128,2048]{1,0:T(8,128)(2,1)}, bf16[128,2048]{1,0:T(8,128)(2,1)}, bf16[128,2048]{1,0:T(8,128)(2,1)}, bf16[128,2048]{1,0:T(8,128)(2,1)}) custom-call(s32[1]{0:T(128)} %bitcast._.core.___.__, s32[1]{0:T(128)} %bitcast.1.me.__._, ...), custom_call_target="tpu_custom_call", output_to_operand_aliasing={{0}: (17, {}), {1}: (18, {}), {2}: (19, {}), {3}: (20, {})} | custom-call | flops 117440512 | bytes 3670016 | tf_op jit(solution)/shard_map/block_outputs/pallas_call | solution.py:292
  45.5 1.2 %block_outputs.5 = (bf16[128,2048]{1,0:T(8,128)(2,1)}, bf16[128,2048]{1,0:T(8,128)(2,1)}, bf16[128,2048]{1,0:T(8,128)(2,1)}, bf16[128,2048]{1,0:T(8,128)(2,1)}) custom-call(s32[1]{0:T(128)} %bitcast._.core.___.__, s32[1]{0:T(128)} %bitcast.1.me.__._, ...), custom_call_target="tpu_custom_call", output_to_operand_aliasing={{0}: (11, {}), {1}: (12, {}), {2}: (13, {}), {3}: (14, {})} | custom-call | flops 67108864 | bytes 2097152 | tf_op jit(solution)/shard_map/block_outputs/pallas_call | solution.py:292
  (36 shorter events, 4.1 us)
Async XLA Ops:
  2.5 2.1 %collective-permute-start = (f32[4,2,128,128]{3,2,1,0:T(8,128)S(1)}, f32[4,2,128,128]{3,2,1,0:T(8,128)S(1)}, u32[]{:S(2)}, u32[]{:S(2)}) collective-permute-start(f32[4,2,128,128]{3,2,1,0:T(8,128)S(1)} %get-tuple-element.89), channel_id=1, source_target_pairs={{0,8},{8,0},{1,9},{9,1},{2,10},{10,2},{3,11},{11,3},{4,12},{12,4},... | collective-permute-start | bytes 1572872 | tf_op jit(solution)/shard_map/ppermute | solution.py:330
  3.7 6.9 %collective-permute-start.5 = (f32[4,2,128,128]{3,2,1,0:T(8,128)S(1)}, f32[4,2,128,128]{3,2,1,0:T(8,128)S(1)}, u32[]{:S(2)}, u32[]{:S(2)}) collective-permute-start(f32[4,2,128,128]{3,2,1,0:T(8,128)S(1)} %get-tuple-element.96), channel_id=1, source_target_pairs={{0,8},{8,0},{1,9},{9,1},{2,10},{10,2},{3,11},{11,3},{4,12},{12,4},... | collective-permute-start | bytes 1572872 | tf_op jit(solution)/shard_map/ppermute | solution.py:330
  4.6 8.1 %collective-permute-start.1 = (f32[2,128,128]{2,1,0:T(8,128)S(1)}, f32[2,128,128]{2,1,0:T(8,128)S(1)}, u32[]{:S(2)}, u32[]{:S(2)}) collective-permute-start(f32[2,128,128]{2,1,0:T(8,128)S(1)} %get-tuple-element.91), channel_id=1, source_target_pairs={{0,16},{1,17},{2,18},{3,19},{16,0},{17,1},{18,2},{19,3},{4,20},{5,... | collective-permute-start | bytes 393224 | tf_op jit(solution)/shard_map/ppermute | solution.py:344
  7.6 7.6 %collective-permute-start.2 = (f32[2,128,128]{2,1,0:T(8,128)S(1)}, f32[2,128,128]{2,1,0:T(8,128)S(1)}, u32[]{:S(2)}, u32[]{:S(2)}) collective-permute-start(f32[2,128,128]{2,1,0:T(8,128)S(1)} %get-tuple-element.92), channel_id=1, source_target_pairs={{0,3},{1,2},{2,1},{3,0},{16,19},{17,18},{18,17},{19,16},{4,7},{5,6... | collective-permute-start | bytes 393224 | tf_op jit(solution)/shard_map/ppermute | solution.py:344
  10.1 9.5 %collective-permute-start.3 = (f32[2,128,128]{2,1,0:T(8,128)S(1)}, f32[2,128,128]{2,1,0:T(8,128)S(1)}, u32[]{:S(2)}, u32[]{:S(2)}) collective-permute-start(f32[2,128,128]{2,1,0:T(8,128)S(1)} %get-tuple-element.93), channel_id=1, source_target_pairs={{0,1},{1,0},{2,3},{3,2},{16,17},{17,16},{18,19},{19,18},{4,5},{5,4... | collective-permute-start | bytes 393224 | tf_op jit(solution)/shard_map/ppermute | solution.py:344
  10.6 9.0 %collective-permute-start.4 = (f32[2,128,128]{2,1,0:T(8,128)S(1)}, f32[2,128,128]{2,1,0:T(8,128)S(1)}, u32[]{:S(2)}, u32[]{:S(2)}) collective-permute-start(f32[2,128,128]{2,1,0:T(8,128)S(1)} %get-tuple-element.94), channel_id=1, source_target_pairs={{0,18},{1,19},{2,16},{3,17},{16,2},{17,3},{18,0},{19,1},{4,22},{5,... | collective-permute-start | bytes 393224 | tf_op jit(solution)/shard_map/ppermute | solution.py:344
  10.7 9.8 %collective-permute-start.6 = (f32[2,128,128]{2,1,0:T(8,128)S(1)}, f32[2,128,128]{2,1,0:T(8,128)S(1)}, u32[]{:S(2)}, u32[]{:S(2)}) collective-permute-start(f32[2,128,128]{2,1,0:T(8,128)S(1)} %get-tuple-element.97), channel_id=1, source_target_pairs={{0,2},{1,3},{2,0},{3,1},{16,18},{17,19},{18,16},{19,17},{4,6},{5,7... | collective-permute-start | bytes 393224 | tf_op jit(solution)/shard_map/ppermute | solution.py:344
  12.7 8.6 %collective-permute-start.7 = (f32[2,128,128]{2,1,0:T(8,128)S(1)}, f32[2,128,128]{2,1,0:T(8,128)S(1)}, u32[]{:S(2)}, u32[]{:S(2)}) collective-permute-start(f32[2,128,128]{2,1,0:T(8,128)S(1)} %get-tuple-element.98), channel_id=1, source_target_pairs={{0,17},{1,16},{2,19},{3,18},{16,1},{17,0},{18,3},{19,2},{4,21},{5,... | collective-permute-start | bytes 393224 | tf_op jit(solution)/shard_map/ppermute | solution.py:344
  15.2 7.6 %collective-permute-start.8 = (f32[2,128,128]{2,1,0:T(8,128)S(1)}, f32[2,128,128]{2,1,0:T(8,128)S(1)}, u32[]{:S(2)}, u32[]{:S(2)}) collective-permute-start(f32[2,128,128]{2,1,0:T(8,128)S(1)} %get-tuple-element.99), channel_id=1, source_target_pairs={{0,19},{1,18},{2,17},{3,16},{16,3},{17,2},{18,1},{19,0},{4,23},{5,... | collective-permute-start | bytes 393224 | tf_op jit(solution)/shard_map/ppermute | solution.py:344
  22.8 5.9 %collective-permute-start.9 = (f32[1,128,128]{2,1,0:T(8,128)S(1)}, f32[1,128,128]{2,1,0:T(8,128)S(1)}, u32[]{:S(2)}, u32[]{:S(2)}) collective-permute-start(f32[1,128,128]{2,1,0:T(8,128)S(1)} %block_total.1), channel_id=1, source_target_pairs={{0,4},{4,0},{1,5},{5,1},{2,6},{6,2},{3,7},{7,3},{8,12},{12,8},{9,1... | collective-permute-start | bytes 196616 | tf_op jit(solution)/shard_map/ppermute | solution.py:330
  28.9 5.9 %collective-permute-start.13 = (f32[2,128,128]{2,1,0:T(8,128)S(1)}, f32[2,128,128]{2,1,0:T(8,128)S(1)}, u32[]{:S(2)}, u32[]{:S(2)}) collective-permute-start(f32[2,128,128]{2,1,0:T(8,128)S(1)} %get-tuple-element.130), channel_id=1, source_target_pairs={{0,16},{1,17},{2,18},{3,19},{16,0},{17,1},{18,2},{19,3},{4,20},{5,... | collective-permute-start | bytes 393224 | tf_op jit(solution)/shard_map/ppermute | solution.py:344
  29.0 7.6 %collective-permute-start.15 = (f32[2,128,128]{2,1,0:T(8,128)S(1)}, f32[2,128,128]{2,1,0:T(8,128)S(1)}, u32[]{:S(2)}, u32[]{:S(2)}) collective-permute-start(f32[2,128,128]{2,1,0:T(8,128)S(1)} %get-tuple-element.131), channel_id=1, source_target_pairs={{0,3},{1,2},{2,1},{3,0},{16,19},{17,18},{18,17},{19,16},{4,7},{5,6... | collective-permute-start | bytes 393224 | tf_op jit(solution)/shard_map/ppermute | solution.py:344
  31.6 7.4 %collective-permute-start.17 = (f32[2,128,128]{2,1,0:T(8,128)S(1)}, f32[2,128,128]{2,1,0:T(8,128)S(1)}, u32[]{:S(2)}, u32[]{:S(2)}) collective-permute-start(f32[2,128,128]{2,1,0:T(8,128)S(1)} %get-tuple-element.132), channel_id=1, source_target_pairs={{0,2},{1,3},{2,0},{3,1},{16,18},{17,19},{18,16},{19,17},{4,6},{5,7... | collective-permute-start | bytes 393224 | tf_op jit(solution)/shard_map/ppermute | solution.py:344
  32.0 7.2 %collective-permute-start.19 = (f32[2,128,128]{2,1,0:T(8,128)S(1)}, f32[2,128,128]{2,1,0:T(8,128)S(1)}, u32[]{:S(2)}, u32[]{:S(2)}) collective-permute-start(f32[2,128,128]{2,1,0:T(8,128)S(1)} %get-tuple-element.133), channel_id=1, source_target_pairs={{0,17},{1,16},{2,19},{3,18},{16,1},{17,0},{18,3},{19,2},{4,21},{5,... | collective-permute-start | bytes 393224 | tf_op jit(solution)/shard_map/ppermute | solution.py:344
  33.9 6.8 %collective-permute-start.10 = (f32[2,128,128]{2,1,0:T(8,128)S(1)}, f32[2,128,128]{2,1,0:T(8,128)S(1)}, u32[]{:S(2)}, u32[]{:S(2)}) collective-permute-start(f32[2,128,128]{2,1,0:T(8,128)S(1)} %get-tuple-element.126), channel_id=1, source_target_pairs={{0,1},{1,0},{2,3},{3,2},{16,17},{17,16},{18,19},{19,18},{4,5},{5,4... | collective-permute-start | bytes 393224 | tf_op jit(solution)/shard_map/ppermute | solution.py:344
  34.8 5.9 %collective-permute-start.11 = (f32[2,128,128]{2,1,0:T(8,128)S(1)}, f32[2,128,128]{2,1,0:T(8,128)S(1)}, u32[]{:S(2)}, u32[]{:S(2)}) collective-permute-start(f32[2,128,128]{2,1,0:T(8,128)S(1)} %get-tuple-element.127), channel_id=1, source_target_pairs={{0,18},{1,19},{2,16},{3,17},{16,2},{17,3},{18,0},{19,1},{4,22},{5,... | collective-permute-start | bytes 393224 | tf_op jit(solution)/shard_map/ppermute | solution.py:344
  36.6 6.8 %collective-permute-start.12 = (f32[2,128,128]{2,1,0:T(8,128)S(1)}, f32[2,128,128]{2,1,0:T(8,128)S(1)}, u32[]{:S(2)}, u32[]{:S(2)}) collective-permute-start(f32[2,128,128]{2,1,0:T(8,128)S(1)} %get-tuple-element.128), channel_id=1, source_target_pairs={{0,19},{1,18},{2,17},{3,16},{16,3},{17,2},{18,1},{19,0},{4,23},{5,... | collective-permute-start | bytes 393224 | tf_op jit(solution)/shard_map/ppermute | solution.py:344
  39.1 4.4 %collective-permute-start.14 = (f32[1,2,128,128]{3,2,1,0:T(8,128)S(1)}, f32[1,2,128,128]{3,2,1,0:T(8,128)S(1)}, u32[]{:S(2)}, u32[]{:S(2)}) collective-permute-start(f32[1,2,128,128]{3,2,1,0:T(8,128)S(1)} %sibling_state.5), channel_id=1, source_target_pairs={{0,8},{8,0},{1,9},{9,1},{2,10},{10,2},{3,11},{11,3},{4,12},{12,4},... | collective-permute-start | bytes 393224 | tf_op jit(solution)/shard_map/ppermute | solution.py:330
  39.2 4.3 %collective-permute-start.16 = (f32[1,2,128,128]{3,2,1,0:T(8,128)S(1)}, f32[1,2,128,128]{3,2,1,0:T(8,128)S(1)}, u32[]{:S(2)}, u32[]{:S(2)}) collective-permute-start(f32[1,2,128,128]{3,2,1,0:T(8,128)S(1)} %sibling_state.6), channel_id=1, source_target_pairs={{0,8},{8,0},{1,9},{9,1},{2,10},{10,2},{3,11},{11,3},{4,12},{12,4},... | collective-permute-start | bytes 393224 | tf_op jit(solution)/shard_map/ppermute | solution.py:330
  40.7 2.8 %collective-permute-start.18 = (f32[1,2,128,128]{3,2,1,0:T(8,128)S(1)}, f32[1,2,128,128]{3,2,1,0:T(8,128)S(1)}, u32[]{:S(2)}, u32[]{:S(2)}) collective-permute-start(f32[1,2,128,128]{3,2,1,0:T(8,128)S(1)} %sibling_state.7), channel_id=1, source_target_pairs={{0,8},{8,0},{1,9},{9,1},{2,10},{10,2},{3,11},{11,3},{4,12},{12,4},... | collective-permute-start | bytes 393224 | tf_op jit(solution)/shard_map/ppermute | solution.py:330
  40.7 2.8 %collective-permute-start.20 = (f32[1,2,128,128]{3,2,1,0:T(8,128)S(1)}, f32[1,2,128,128]{3,2,1,0:T(8,128)S(1)}, u32[]{:S(2)}, u32[]{:S(2)}) collective-permute-start(f32[1,2,128,128]{3,2,1,0:T(8,128)S(1)} %sibling_state.8), channel_id=1, source_target_pairs={{0,8},{8,0},{1,9},{9,1},{2,10},{10,2},{3,11},{11,3},{4,12},{12,4},... | collective-permute-start | bytes 393224 | tf_op jit(solution)/shard_map/ppermute | solution.py:330
  43.6 2.0 %collective-permute-start.21 = (f32[4,2,128,128]{3,2,1,0:T(8,128)S(1)}, f32[4,2,128,128]{3,2,1,0:T(8,128)S(1)}, u32[]{:S(2)}, u32[]{:S(2)}) collective-permute-start(f32[4,2,128,128]{3,2,1,0:T(8,128)S(1)} %sibling_state.9), channel_id=1, source_target_pairs={{0,8},{8,0},{1,9},{9,1},{2,10},{10,2},{3,11},{11,3},{4,12},{12,4},... | collective-permute-start | bytes 1572872 | tf_op jit(solution)/shard_map/ppermute | solution.py:330

commit v9 on v8

--- a/solution.py
+++ b/solution.py
@@ -370,7 +370,8 @@
     pos = positions.reshape(1, rows)
 
     short = sorted(range(1, members - 1), key=lambda m: (bin(m).count("1"), m))[: members // 2 - 1]
-    order = [route for m in short for route in (m, members - 1 - m)] + [members - 1]
+    order = [route for m in short[:-1] for route in (m, members - 1 - m)]
+    order += [members - 1 - short[-1], short[-1], members - 1]
     back = [route for m in short[:1] + short[:0:-1] for route in (m, members - 1 - m)] + [members - 1]
     masks = list(dict.fromkeys([m // per for m in order] + [0]))
     sets = masks[: part // 2], masks[part // 2 :]

time: 46.9 us -> 46.9 us (level)
  no operation moved by 1% of the time
where the time goes in v9:
time: 46.9 us; the launch traced here: 46.8 us
  starting transfers between devices  26.7 us (57%)
  waiting for transfers between devices  9.78 us (21%)
  Pallas kernels  9.52 us (20%)
  between operations  0.78 us (2%)
    ppermute x14, starting transfers between devices, send_to(): return lax.ppermute(value, AXES, pairs)  22.2 us
    ppermute x14, waiting for transfers between devices, send_to(): return lax.ppermute(value, AXES, pairs)  5.64 us
    ppermute x8, starting transfers between devices, swap(): return lax.ppermute(value, axis, [(0, 1), (1, 0)])  4.5 us
    pallas_call x3, Pallas kernels, outputs(): call(functools.partial(outputs_body, scale, per, jobs, len(pieces), len(p...  4.18 us
    ppermute x8, waiting for transfers between devices, swap(): return lax.ppermute(value, axis, [(0, 1), (1, 0)])  4.14 us
    pallas_call x1, Pallas kernels, local_parts(): call(local_body, [in_vmem((heads, 4, rows, D), BF16), in_vmem((heads, 4,...  2.2 us
    pallas_call x1, Pallas kernels, states(): call(body, [table] * 2 + [in_vmem(piece, BF16)] * 8 + results, [SMEM] * 4...  1.87 us
  transfers between devices with their start and end apart: 22, of which 9 were waited for; matrix products, arithmetic and copies ran while one was open for 0% of the time, Pallas kernels for 13%

profile of v9, /device:TPU:0, one launch (start us, length us, event | category | flops | bytes accessed | tf_op | source)
XLA Modules:
  0.0 46.8 jit_solution(17212637495659222850)
XLA Ops:
  0.6 1.9 %block_states.2 = (f32[128,128]{1,0:T(8,128)S(1)}, f32[128,128]{1,0:T(8,128)S(1)}, bf16[128,1024]{1,0:T(8,128)(2,1)S(1)}, bf16[128,1024]{1,0:T(8,128)(2,1)S(1)},...) custom-call(s32[1]{0:T(128)} %bitcast._.core.___.__, ...), custom_call_target="tpu_custom_call" | custom-call | flops 67108864 | bytes 2097152 | tf_op jit(solution)/shard_map/block_states/pallas_call | solution.py:115
  3.0 0.7 %block_states.3 = (f32[4,2,128,128]{3,2,1,0:T(8,128)S(1)}, f32[4,2,128,128]{3,2,1,0:T(8,128)S(1)}) custom-call(s32[1]{0:T(128)} %bitcast._.core.___.__, s32[1]{0:T(128)} %bitcast.1.me.__._, s32[1]{0:T(128)} %bitcast.2.__.group._, s32[1]{0:T(128)} %bitcast._.core.___.__, f32[128,128]{1,0:T(8,128)S(1)} %get-tuple-element.104.refs_0_.refs_8_.cos_ref, ...), custom_call_target="tpu_custom_call" | custom-call | flops 67108864 | bytes 2097152 | tf_op jit(solution)/shard_map/block_states/pallas_call | solution.py:120
  3.8 0.8 %collective-permute-done.b_ref.refs_0_ = f32[4,2,128,128]{3,2,1,0:T(8,128)S(1)} collective-permute-done((f32[4,2,128,128]{3,2,1,0:T(8,128)S(1)}, f32[4,2,128,128]{3,2,1,0:T(8,128)S(1)}, u32[]{:S(2)}, u32[]{:S(2)}) %collective-permute-start) | collective-permute-done | bytes 524320 | tf_op jit(solution)/shard_map/ppermute | solution.py:330
  4.6 2.9 %collective-permute-start.1 = (f32[2,128,128]{2,1,0:T(8,128)S(1)}, f32[2,128,128]{2,1,0:T(8,128)S(1)}, u32[]{:S(2)}, u32[]{:S(2)}) collective-permute-start(f32[2,128,128]{2,1,0:T(8,128)S(1)} %get-tuple-element.91), channel_id=1, source_target_pairs={{0,16},{1,17},{2,18},{3,19},{16,0},{17,1},{18,2},{19,3},{4,20},{5,... | collective-permute-start | bytes 393224 | tf_op jit(solution)/shard_map/ppermute | solution.py:344
  7.6 2.5 %collective-permute-start.2 = (f32[2,128,128]{2,1,0:T(8,128)S(1)}, f32[2,128,128]{2,1,0:T(8,128)S(1)}, u32[]{:S(2)}, u32[]{:S(2)}) collective-permute-start(f32[2,128,128]{2,1,0:T(8,128)S(1)} %get-tuple-element.92), channel_id=1, source_target_pairs={{0,3},{1,2},{2,1},{3,0},{16,19},{17,18},{18,17},{19,16},{4,7},{5,6... | collective-permute-start | bytes 393224 | tf_op jit(solution)/shard_map/ppermute | solution.py:344
  10.7 2.9 %collective-permute-start.6 = (f32[2,128,128]{2,1,0:T(8,128)S(1)}, f32[2,128,128]{2,1,0:T(8,128)S(1)}, u32[]{:S(2)}, u32[]{:S(2)}) collective-permute-start(f32[2,128,128]{2,1,0:T(8,128)S(1)} %get-tuple-element.97), channel_id=1, source_target_pairs={{0,17},{1,16},{2,19},{3,18},{16,1},{17,0},{18,3},{19,2},{4,21},{5,... | collective-permute-start | bytes 393224 | tf_op jit(solution)/shard_map/ppermute | solution.py:344
  13.6 1.6 %collective-permute-start.7 = (f32[2,128,128]{2,1,0:T(8,128)S(1)}, f32[2,128,128]{2,1,0:T(8,128)S(1)}, u32[]{:S(2)}, u32[]{:S(2)}) collective-permute-start(f32[2,128,128]{2,1,0:T(8,128)S(1)} %get-tuple-element.98), channel_id=1, source_target_pairs={{0,2},{1,3},{2,0},{3,1},{16,18},{17,19},{18,16},{19,17},{4,6},{5,7... | collective-permute-start | bytes 393224 | tf_op jit(solution)/shard_map/ppermute | solution.py:344
  15.2 2.2 %collective-permute-start.8 = (f32[2,128,128]{2,1,0:T(8,128)S(1)}, f32[2,128,128]{2,1,0:T(8,128)S(1)}, u32[]{:S(2)}, u32[]{:S(2)}) collective-permute-start(f32[2,128,128]{2,1,0:T(8,128)S(1)} %get-tuple-element.99), channel_id=1, source_target_pairs={{0,19},{1,18},{2,17},{3,16},{16,3},{17,2},{18,1},{19,0},{4,23},{5,... | collective-permute-start | bytes 393224 | tf_op jit(solution)/shard_map/ppermute | solution.py:344
  17.4 2.2 %local_parts.1 = (bf16[16,4,128,128]{3,2,1,0:T(8,128)(2,1)S(1)}, f32[16,4,128,128]{3,2,1,0:T(8,128)S(1)}) custom-call(bf16[128,1024]{1,0:T(8,128)(2,1)S(1)} %get-tuple-element.82.refs_2_.refs_0_, bf16[128,1024]{1,0:T(8,128)(2,1)S(1)} %get-tuple-element.83.refs_3_.refs_1_, bf16[128,1024]{1,0:T(8,128)(2,1)S(1)} %get-tuple-element.84.refs_4_.refs_2_, ...), custom_call_target="tpu_custom_call" | custom-call | flops 536870912 | bytes 8388608 | tf_op jit(solution)/shard_map/local_parts/pallas_call | solution.py:234
  19.6 0.8 %collective-permute-done.3.refs_2_ = f32[2,128,128]{2,1,0:T(8,128)S(1)} collective-permute-done((f32[2,128,128]{2,1,0:T(8,128)S(1)}, f32[2,128,128]{2,1,0:T(8,128)S(1)}, u32[]{:S(2)}, u32[]{:S(2)}) %collective-permute-start.3) | collective-permute-done | bytes 131104 | tf_op jit(solution)/shard_map/ppermute | solution.py:344
  20.5 2.3 %collective-permute-done.8.refs_7_ = f32[2,128,128]{2,1,0:T(8,128)S(1)} collective-permute-done((f32[2,128,128]{2,1,0:T(8,128)S(1)}, f32[2,128,128]{2,1,0:T(8,128)S(1)}, u32[]{:S(2)}, u32[]{:S(2)}) %collective-permute-start.8) | collective-permute-done | bytes 131104 | tf_op jit(solution)/shard_map/ppermute | solution.py:344
  22.9 2.7 %collective-permute-start.9 = (f32[1,128,128]{2,1,0:T(8,128)S(1)}, f32[1,128,128]{2,1,0:T(8,128)S(1)}, u32[]{:S(2)}, u32[]{:S(2)}) collective-permute-start(f32[1,128,128]{2,1,0:T(8,128)S(1)} %block_total.1), channel_id=1, source_target_pairs={{0,4},{4,0},{1,5},{5,1},{2,6},{6,2},{3,7},{7,3},{8,12},{12,8},{9,1... | collective-permute-start | bytes 196616 | tf_op jit(solution)/shard_map/ppermute | solution.py:330
  25.7 3.1 %collective-permute-done.9.passed_ref = f32[1,128,128]{2,1,0:T(8,128)S(1)} collective-permute-done((f32[1,128,128]{2,1,0:T(8,128)S(1)}, f32[1,128,128]{2,1,0:T(8,128)S(1)}, u32[]{:S(2)}, u32[]{:S(2)}) %collective-permute-start.9) | collective-permute-done | bytes 65568 | tf_op jit(solution)/shard_map/ppermute | solution.py:330
  29.1 2.5 %collective-permute-start.15 = (f32[2,128,128]{2,1,0:T(8,128)S(1)}, f32[2,128,128]{2,1,0:T(8,128)S(1)}, u32[]{:S(2)}, u32[]{:S(2)}) collective-permute-start(f32[2,128,128]{2,1,0:T(8,128)S(1)} %get-tuple-element.131), channel_id=1, source_target_pairs={{0,3},{1,2},{2,1},{3,0},{16,19},{17,18},{18,17},{19,16},{4,7},{5,6... | collective-permute-start | bytes 393224 | tf_op jit(solution)/shard_map/ppermute | solution.py:344
  32.0 1.9 %collective-permute-start.19 = (f32[2,128,128]{2,1,0:T(8,128)S(1)}, f32[2,128,128]{2,1,0:T(8,128)S(1)}, u32[]{:S(2)}, u32[]{:S(2)}) collective-permute-start(f32[2,128,128]{2,1,0:T(8,128)S(1)} %get-tuple-element.133), channel_id=1, source_target_pairs={{0,17},{1,16},{2,19},{3,18},{16,1},{17,0},{18,3},{19,2},{4,21},{5,... | collective-permute-start | bytes 393224 | tf_op jit(solution)/shard_map/ppermute | solution.py:344
  34.1 0.7 %collective-permute-done.13.refs_0_.refs_3_ = f32[2,128,128]{2,1,0:T(8,128)S(1)} collective-permute-done((f32[2,128,128]{2,1,0:T(8,128)S(1)}, f32[2,128,128]{2,1,0:T(8,128)S(1)}, u32[]{:S(2)}, u32[]{:S(2)}) %collective-permute-start.13) | collective-permute-done | bytes 131104 | tf_op jit(solution)/shard_map/ppermute | solution.py:344
  34.8 1.8 %collective-permute-start.11 = (f32[2,128,128]{2,1,0:T(8,128)S(1)}, f32[2,128,128]{2,1,0:T(8,128)S(1)}, u32[]{:S(2)}, u32[]{:S(2)}) collective-permute-start(f32[2,128,128]{2,1,0:T(8,128)S(1)} %get-tuple-element.127), channel_id=1, source_target_pairs={{0,18},{1,19},{2,16},{3,17},{16,2},{17,3},{18,0},{19,1},{4,22},{5,... | collective-permute-start | bytes 393224 | tf_op jit(solution)/shard_map/ppermute | solution.py:344
  36.6 2.5 %collective-permute-start.12 = (f32[2,128,128]{2,1,0:T(8,128)S(1)}, f32[2,128,128]{2,1,0:T(8,128)S(1)}, u32[]{:S(2)}, u32[]{:S(2)}) collective-permute-start(f32[2,128,128]{2,1,0:T(8,128)S(1)} %get-tuple-element.128), channel_id=1, source_target_pairs={{0,19},{1,18},{2,17},{3,16},{16,3},{17,2},{18,1},{19,0},{4,23},{5,... | collective-permute-start | bytes 393224 | tf_op jit(solution)/shard_map/ppermute | solution.py:344
  39.3 0.6 %collective-permute-start.16 = (f32[1,2,128,128]{3,2,1,0:T(8,128)S(1)}, f32[1,2,128,128]{3,2,1,0:T(8,128)S(1)}, u32[]{:S(2)}, u32[]{:S(2)}) collective-permute-start(f32[1,2,128,128]{3,2,1,0:T(8,128)S(1)} %sibling_state.6), channel_id=1, source_target_pairs={{0,8},{8,0},{1,9},{9,1},{2,10},{10,2},{3,11},{11,3},{4,12},{12,4},... | collective-permute-start | bytes 393224 | tf_op jit(solution)/shard_map/ppermute | solution.py:330
  39.9 0.8 %collective-permute-done.10.refs_0_.refs_2_ = f32[2,128,128]{2,1,0:T(8,128)S(1)} collective-permute-done((f32[2,128,128]{2,1,0:T(8,128)S(1)}, f32[2,128,128]{2,1,0:T(8,128)S(1)}, u32[]{:S(2)}, u32[]{:S(2)}) %collective-permute-start.10) | collective-permute-done | bytes 131104 | tf_op jit(solution)/shard_map/ppermute | solution.py:344
  41.2 1.4 %block_outputs.3 = (bf16[128,2048]{1,0:T(8,128)(2,1)}, bf16[128,2048]{1,0:T(8,128)(2,1)}, bf16[128,2048]{1,0:T(8,128)(2,1)}, bf16[128,2048]{1,0:T(8,128)(2,1)}) custom-call(s32[1]{0:T(128)} %bitcast._.core.___.__, s32[1]{0:T(128)} %bitcast.1.me.__._, s32[1]{0:T(128)} %bitcast.2.__.group._, s32[1]{0:T(128)} %bitcast._.core.___.__, ...), custom_call_target="tpu_custom_call" | custom-call | flops 83886080 | bytes 2621440 | tf_op jit(solution)/shard_map/block_outputs/pallas_call | solution.py:292
  42.6 0.9 %collective-permute-done.12.refs_2_.refs_4_ = f32[2,128,128]{2,1,0:T(8,128)S(1)} collective-permute-done((f32[2,128,128]{2,1,0:T(8,128)S(1)}, f32[2,128,128]{2,1,0:T(8,128)S(1)}, u32[]{:S(2)}, u32[]{:S(2)}) %collective-permute-start.12) | collective-permute-done | bytes 131104 | tf_op jit(solution)/shard_map/ppermute | solution.py:344
  43.6 1.6 %block_outputs.4 = (bf16[128,2048]{1,0:T(8,128)(2,1)}, bf16[128,2048]{1,0:T(8,128)(2,1)}, bf16[128,2048]{1,0:T(8,128)(2,1)}, bf16[128,2048]{1,0:T(8,128)(2,1)}) custom-call(s32[1]{0:T(128)} %bitcast._.core.___.__, s32[1]{0:T(128)} %bitcast.1.me.__._, ...), custom_call_target="tpu_custom_call", output_to_operand_aliasing={{0}: (17, {}), {1}: (18, {}), {2}: (19, {}), {3}: (20, {})} | custom-call | flops 117440512 | bytes 3670016 | tf_op jit(solution)/shard_map/block_outputs/pallas_call | solution.py:292
  45.5 1.2 %block_outputs.5 = (bf16[128,2048]{1,0:T(8,128)(2,1)}, bf16[128,2048]{1,0:T(8,128)(2,1)}, bf16[128,2048]{1,0:T(8,128)(2,1)}, bf16[128,2048]{1,0:T(8,128)(2,1)}) custom-call(s32[1]{0:T(128)} %bitcast._.core.___.__, s32[1]{0:T(128)} %bitcast.1.me.__._, ...), custom_call_target="tpu_custom_call", output_to_operand_aliasing={{0}: (11, {}), {1}: (12, {}), {2}: (13, {}), {3}: (14, {})} | custom-call | flops 67108864 | bytes 2097152 | tf_op jit(solution)/shard_map/block_outputs/pallas_call | solution.py:292
  (36 shorter events, 3.8 us)
Async XLA Ops:
  2.5 2.1 %collective-permute-start = (f32[4,2,128,128]{3,2,1,0:T(8,128)S(1)}, f32[4,2,128,128]{3,2,1,0:T(8,128)S(1)}, u32[]{:S(2)}, u32[]{:S(2)}) collective-permute-start(f32[4,2,128,128]{3,2,1,0:T(8,128)S(1)} %get-tuple-element.89), channel_id=1, source_target_pairs={{0,8},{8,0},{1,9},{9,1},{2,10},{10,2},{3,11},{11,3},{4,12},{12,4},... | collective-permute-start | bytes 1572872 | tf_op jit(solution)/shard_map/ppermute | solution.py:330
  3.7 6.9 %collective-permute-start.5 = (f32[4,2,128,128]{3,2,1,0:T(8,128)S(1)}, f32[4,2,128,128]{3,2,1,0:T(8,128)S(1)}, u32[]{:S(2)}, u32[]{:S(2)}) collective-permute-start(f32[4,2,128,128]{3,2,1,0:T(8,128)S(1)} %get-tuple-element.96), channel_id=1, source_target_pairs={{0,8},{8,0},{1,9},{9,1},{2,10},{10,2},{3,11},{11,3},{4,12},{12,4},... | collective-permute-start | bytes 1572872 | tf_op jit(solution)/shard_map/ppermute | solution.py:330
  4.6 9.0 %collective-permute-start.1 = (f32[2,128,128]{2,1,0:T(8,128)S(1)}, f32[2,128,128]{2,1,0:T(8,128)S(1)}, u32[]{:S(2)}, u32[]{:S(2)}) collective-permute-start(f32[2,128,128]{2,1,0:T(8,128)S(1)} %get-tuple-element.91), channel_id=1, source_target_pairs={{0,16},{1,17},{2,18},{3,19},{16,0},{17,1},{18,2},{19,3},{4,20},{5,... | collective-permute-start | bytes 393224 | tf_op jit(solution)/shard_map/ppermute | solution.py:344
  7.6 7.6 %collective-permute-start.2 = (f32[2,128,128]{2,1,0:T(8,128)S(1)}, f32[2,128,128]{2,1,0:T(8,128)S(1)}, u32[]{:S(2)}, u32[]{:S(2)}) collective-permute-start(f32[2,128,128]{2,1,0:T(8,128)S(1)} %get-tuple-element.92), channel_id=1, source_target_pairs={{0,3},{1,2},{2,1},{3,0},{16,19},{17,18},{18,17},{19,16},{4,7},{5,6... | collective-permute-start | bytes 393224 | tf_op jit(solution)/shard_map/ppermute | solution.py:344
  10.1 10.3 %collective-permute-start.3 = (f32[2,128,128]{2,1,0:T(8,128)S(1)}, f32[2,128,128]{2,1,0:T(8,128)S(1)}, u32[]{:S(2)}, u32[]{:S(2)}) collective-permute-start(f32[2,128,128]{2,1,0:T(8,128)S(1)} %get-tuple-element.93), channel_id=1, source_target_pairs={{0,1},{1,0},{2,3},{3,2},{16,17},{17,16},{18,19},{19,18},{4,5},{5,4... | collective-permute-start | bytes 393224 | tf_op jit(solution)/shard_map/ppermute | solution.py:344
  10.6 9.7 %collective-permute-start.4 = (f32[2,128,128]{2,1,0:T(8,128)S(1)}, f32[2,128,128]{2,1,0:T(8,128)S(1)}, u32[]{:S(2)}, u32[]{:S(2)}) collective-permute-start(f32[2,128,128]{2,1,0:T(8,128)S(1)} %get-tuple-element.94), channel_id=1, source_target_pairs={{0,18},{1,19},{2,16},{3,17},{16,2},{17,3},{18,0},{19,1},{4,22},{5,... | collective-permute-start | bytes 393224 | tf_op jit(solution)/shard_map/ppermute | solution.py:344
  10.7 9.7 %collective-permute-start.6 = (f32[2,128,128]{2,1,0:T(8,128)S(1)}, f32[2,128,128]{2,1,0:T(8,128)S(1)}, u32[]{:S(2)}, u32[]{:S(2)}) collective-permute-start(f32[2,128,128]{2,1,0:T(8,128)S(1)} %get-tuple-element.97), channel_id=1, source_target_pairs={{0,17},{1,16},{2,19},{3,18},{16,1},{17,0},{18,3},{19,2},{4,21},{5,... | collective-permute-start | bytes 393224 | tf_op jit(solution)/shard_map/ppermute | solution.py:344
  13.6 6.9 %collective-permute-start.7 = (f32[2,128,128]{2,1,0:T(8,128)S(1)}, f32[2,128,128]{2,1,0:T(8,128)S(1)}, u32[]{:S(2)}, u32[]{:S(2)}) collective-permute-start(f32[2,128,128]{2,1,0:T(8,128)S(1)} %get-tuple-element.98), channel_id=1, source_target_pairs={{0,2},{1,3},{2,0},{3,1},{16,18},{17,19},{18,16},{19,17},{4,6},{5,7... | collective-permute-start | bytes 393224 | tf_op jit(solution)/shard_map/ppermute | solution.py:344
  15.2 7.6 %collective-permute-start.8 = (f32[2,128,128]{2,1,0:T(8,128)S(1)}, f32[2,128,128]{2,1,0:T(8,128)S(1)}, u32[]{:S(2)}, u32[]{:S(2)}) collective-permute-start(f32[2,128,128]{2,1,0:T(8,128)S(1)} %get-tuple-element.99), channel_id=1, source_target_pairs={{0,19},{1,18},{2,17},{3,16},{16,3},{17,2},{18,1},{19,0},{4,23},{5,... | collective-permute-start | bytes 393224 | tf_op jit(solution)/shard_map/ppermute | solution.py:344
  22.9 5.9 %collective-permute-start.9 = (f32[1,128,128]{2,1,0:T(8,128)S(1)}, f32[1,128,128]{2,1,0:T(8,128)S(1)}, u32[]{:S(2)}, u32[]{:S(2)}) collective-permute-start(f32[1,128,128]{2,1,0:T(8,128)S(1)} %block_total.1), channel_id=1, source_target_pairs={{0,4},{4,0},{1,5},{5,1},{2,6},{6,2},{3,7},{7,3},{8,12},{12,8},{9,1... | collective-permute-start | bytes 196616 | tf_op jit(solution)/shard_map/ppermute | solution.py:330
  28.9 5.9 %collective-permute-start.13 = (f32[2,128,128]{2,1,0:T(8,128)S(1)}, f32[2,128,128]{2,1,0:T(8,128)S(1)}, u32[]{:S(2)}, u32[]{:S(2)}) collective-permute-start(f32[2,128,128]{2,1,0:T(8,128)S(1)} %get-tuple-element.130), channel_id=1, source_target_pairs={{0,16},{1,17},{2,18},{3,19},{16,0},{17,1},{18,2},{19,3},{4,20},{5,... | collective-permute-start | bytes 393224 | tf_op jit(solution)/shard_map/ppermute | solution.py:344
  29.1 7.5 %collective-permute-start.15 = (f32[2,128,128]{2,1,0:T(8,128)S(1)}, f32[2,128,128]{2,1,0:T(8,128)S(1)}, u32[]{:S(2)}, u32[]{:S(2)}) collective-permute-start(f32[2,128,128]{2,1,0:T(8,128)S(1)} %get-tuple-element.131), channel_id=1, source_target_pairs={{0,3},{1,2},{2,1},{3,0},{16,19},{17,18},{18,17},{19,16},{4,7},{5,6... | collective-permute-start | bytes 393224 | tf_op jit(solution)/shard_map/ppermute | solution.py:344
  31.6 7.5 %collective-permute-start.17 = (f32[2,128,128]{2,1,0:T(8,128)S(1)}, f32[2,128,128]{2,1,0:T(8,128)S(1)}, u32[]{:S(2)}, u32[]{:S(2)}) collective-permute-start(f32[2,128,128]{2,1,0:T(8,128)S(1)} %get-tuple-element.132), channel_id=1, source_target_pairs={{0,2},{1,3},{2,0},{3,1},{16,18},{17,19},{18,16},{19,17},{4,6},{5,7... | collective-permute-start | bytes 393224 | tf_op jit(solution)/shard_map/ppermute | solution.py:344
  32.0 7.3 %collective-permute-start.19 = (f32[2,128,128]{2,1,0:T(8,128)S(1)}, f32[2,128,128]{2,1,0:T(8,128)S(1)}, u32[]{:S(2)}, u32[]{:S(2)}) collective-permute-start(f32[2,128,128]{2,1,0:T(8,128)S(1)} %get-tuple-element.133), channel_id=1, source_target_pairs={{0,17},{1,16},{2,19},{3,18},{16,1},{17,0},{18,3},{19,2},{4,21},{5,... | collective-permute-start | bytes 393224 | tf_op jit(solution)/shard_map/ppermute | solution.py:344
  33.9 6.8 %collective-permute-start.10 = (f32[2,128,128]{2,1,0:T(8,128)S(1)}, f32[2,128,128]{2,1,0:T(8,128)S(1)}, u32[]{:S(2)}, u32[]{:S(2)}) collective-permute-start(f32[2,128,128]{2,1,0:T(8,128)S(1)} %get-tuple-element.126), channel_id=1, source_target_pairs={{0,1},{1,0},{2,3},{3,2},{16,17},{17,16},{18,19},{19,18},{4,5},{5,4... | collective-permute-start | bytes 393224 | tf_op jit(solution)/shard_map/ppermute | solution.py:344
  34.8 5.9 %collective-permute-start.11 = (f32[2,128,128]{2,1,0:T(8,128)S(1)}, f32[2,128,128]{2,1,0:T(8,128)S(1)}, u32[]{:S(2)}, u32[]{:S(2)}) collective-permute-start(f32[2,128,128]{2,1,0:T(8,128)S(1)} %get-tuple-element.127), channel_id=1, source_target_pairs={{0,18},{1,19},{2,16},{3,17},{16,2},{17,3},{18,0},{19,1},{4,22},{5,... | collective-permute-start | bytes 393224 | tf_op jit(solution)/shard_map/ppermute | solution.py:344
  36.6 6.8 %collective-permute-start.12 = (f32[2,128,128]{2,1,0:T(8,128)S(1)}, f32[2,128,128]{2,1,0:T(8,128)S(1)}, u32[]{:S(2)}, u32[]{:S(2)}) collective-permute-start(f32[2,128,128]{2,1,0:T(8,128)S(1)} %get-tuple-element.128), channel_id=1, source_target_pairs={{0,19},{1,18},{2,17},{3,16},{16,3},{17,2},{18,1},{19,0},{4,23},{5,... | collective-permute-start | bytes 393224 | tf_op jit(solution)/shard_map/ppermute | solution.py:344
  39.2 4.3 %collective-permute-start.14 = (f32[1,2,128,128]{3,2,1,0:T(8,128)S(1)}, f32[1,2,128,128]{3,2,1,0:T(8,128)S(1)}, u32[]{:S(2)}, u32[]{:S(2)}) collective-permute-start(f32[1,2,128,128]{3,2,1,0:T(8,128)S(1)} %sibling_state.5), channel_id=1, source_target_pairs={{0,8},{8,0},{1,9},{9,1},{2,10},{10,2},{3,11},{11,3},{4,12},{12,4},... | collective-permute-start | bytes 393224 | tf_op jit(solution)/shard_map/ppermute | solution.py:330
  39.3 4.2 %collective-permute-start.16 = (f32[1,2,128,128]{3,2,1,0:T(8,128)S(1)}, f32[1,2,128,128]{3,2,1,0:T(8,128)S(1)}, u32[]{:S(2)}, u32[]{:S(2)}) collective-permute-start(f32[1,2,128,128]{3,2,1,0:T(8,128)S(1)} %sibling_state.6), channel_id=1, source_target_pairs={{0,8},{8,0},{1,9},{9,1},{2,10},{10,2},{3,11},{11,3},{4,12},{12,4},... | collective-permute-start | bytes 393224 | tf_op jit(solution)/shard_map/ppermute | solution.py:330
  40.7 2.7 %collective-permute-start.18 = (f32[1,2,128,128]{3,2,1,0:T(8,128)S(1)}, f32[1,2,128,128]{3,2,1,0:T(8,128)S(1)}, u32[]{:S(2)}, u32[]{:S(2)}) collective-permute-start(f32[1,2,128,128]{3,2,1,0:T(8,128)S(1)} %sibling_state.7), channel_id=1, source_target_pairs={{0,8},{8,0},{1,9},{9,1},{2,10},{10,2},{3,11},{11,3},{4,12},{12,4},... | collective-permute-start | bytes 393224 | tf_op jit(solution)/shard_map/ppermute | solution.py:330
  40.7 2.7 %collective-permute-start.20 = (f32[1,2,128,128]{3,2,1,0:T(8,128)S(1)}, f32[1,2,128,128]{3,2,1,0:T(8,128)S(1)}, u32[]{:S(2)}, u32[]{:S(2)}) collective-permute-start(f32[1,2,128,128]{3,2,1,0:T(8,128)S(1)} %sibling_state.8), channel_id=1, source_target_pairs={{0,8},{8,0},{1,9},{9,1},{2,10},{10,2},{3,11},{11,3},{4,12},{12,4},... | collective-permute-start | bytes 393224 | tf_op jit(solution)/shard_map/ppermute | solution.py:330
  43.6 2.0 %collective-permute-start.21 = (f32[4,2,128,128]{3,2,1,0:T(8,128)S(1)}, f32[4,2,128,128]{3,2,1,0:T(8,128)S(1)}, u32[]{:S(2)}, u32[]{:S(2)}) collective-permute-start(f32[4,2,128,128]{3,2,1,0:T(8,128)S(1)} %sibling_state.9), channel_id=1, source_target_pairs={{0,8},{8,0},{1,9},{9,1},{2,10},{10,2},{3,11},{11,3},{4,12},{12,4},... | collective-permute-start | bytes 1572872 | tf_op jit(solution)/shard_map/ppermute | solution.py:330

commit v10 on v8

--- a/solution.py
+++ b/solution.py
@@ -371,7 +371,8 @@
 
     short = sorted(range(1, members - 1), key=lambda m: (bin(m).count("1"), m))[: members // 2 - 1]
     order = [route for m in short for route in (m, members - 1 - m)] + [members - 1]
-    back = [route for m in short[:1] + short[:0:-1] for route in (m, members - 1 - m)] + [members - 1]
+    back = [route for m in short[:1] + short[:1:-1] for route in (m, members - 1 - m)]
+    back += [members - 1 - short[1], short[1], members - 1]
     masks = list(dict.fromkeys([m // per for m in order] + [0]))
     sets = masks[: part // 2], masks[part // 2 :]
     spots = {mask: (which, group.index(mask)) for which, group in enumerate(sets) for mask in group}

time: 46.9 us -> 46.9 us (level)
  starting transfers between devices: 26.6 us -> 25.4 us
  waiting for transfers between devices: 9.91 us -> 11.1 us
    ppermute x14, waiting for transfers between devices: 5.76 us -> 6.94 us  [send_to(): return lax.ppermute(value, AXES, pairs)]
    ppermute x14, starting transfers between devices: 22.1 us -> 21.5 us  [send_to(): return lax.ppermute(value, AXES, pairs)]
    ppermute x8, starting transfers between devices: 4.5 us -> 3.95 us  [swap(): return lax.ppermute(value, axis, [(0, 1), (1, 0)])]
  transfers between devices with their start and end apart: 22 -> 22, of which waited for: 9 -> 11; matrix products, arithmetic and copies ran while one was open for 0% -> 0% of each run, Pallas kernels for 13% -> 13%
where the time goes in v10:
time: 46.9 us; the launch traced here: 46.8 us
  starting transfers between devices  25.4 us (54%)
  waiting for transfers between devices  11.1 us (24%)
  Pallas kernels  9.51 us (20%)
  between operations  0.78 us (2%)
    ppermute x14, starting transfers between devices, send_to(): return lax.ppermute(value, AXES, pairs)  21.5 us
    ppermute x14, waiting for transfers between devices, send_to(): return lax.ppermute(value, AXES, pairs)  6.94 us
    pallas_call x3, Pallas kernels, outputs(): call(functools.partial(outputs_body, scale, per, jobs, len(pieces), len(p...  4.18 us
    ppermute x8, waiting for transfers between devices, swap(): return lax.ppermute(value, axis, [(0, 1), (1, 0)])  4.14 us
    ppermute x8, starting transfers between devices, swap(): return lax.ppermute(value, axis, [(0, 1), (1, 0)])  3.95 us
    pallas_call x1, Pallas kernels, local_parts(): call(local_body, [in_vmem((heads, 4, rows, D), BF16), in_vmem((heads, 4,...  2.2 us
    pallas_call x1, Pallas kernels, states(): call(body, [table] * 2 + [in_vmem(piece, BF16)] * 8 + results, [SMEM] * 4...  1.87 us
  transfers between devices with their start and end apart: 22, of which 11 were waited for; matrix products, arithmetic and copies ran while one was open for 0% of the time, Pallas kernels for 13%

profile of v10, /device:TPU:0, one launch (start us, length us, event | category | flops | bytes accessed | tf_op | source)
XLA Modules:
  0.0 46.8 jit_solution(2320425939136899269)
XLA Ops:
  0.6 1.9 %block_states.2 = (f32[128,128]{1,0:T(8,128)S(1)}, f32[128,128]{1,0:T(8,128)S(1)}, bf16[128,1024]{1,0:T(8,128)(2,1)S(1)}, bf16[128,1024]{1,0:T(8,128)(2,1)S(1)},...) custom-call(s32[1]{0:T(128)} %bitcast._.core.___.__, ...), custom_call_target="tpu_custom_call" | custom-call | flops 67108864 | bytes 2097152 | tf_op jit(solution)/shard_map/block_states/pallas_call | solution.py:115
  3.8 0.8 %collective-permute-done.b_ref.refs_0_ = f32[4,2,128,128]{3,2,1,0:T(8,128)S(1)} collective-permute-done((f32[4,2,128,128]{3,2,1,0:T(8,128)S(1)}, f32[4,2,128,128]{3,2,1,0:T(8,128)S(1)}, u32[]{:S(2)}, u32[]{:S(2)}) %collective-permute-start) | collective-permute-done | bytes 524320 | tf_op jit(solution)/shard_map/ppermute | solution.py:330
  4.6 2.9 %collective-permute-start.1 = (f32[2,128,128]{2,1,0:T(8,128)S(1)}, f32[2,128,128]{2,1,0:T(8,128)S(1)}, u32[]{:S(2)}, u32[]{:S(2)}) collective-permute-start(f32[2,128,128]{2,1,0:T(8,128)S(1)} %get-tuple-element.91), channel_id=1, source_target_pairs={{0,16},{1,17},{2,18},{3,19},{16,0},{17,1},{18,2},{19,3},{4,20},{5,... | collective-permute-start | bytes 393224 | tf_op jit(solution)/shard_map/ppermute | solution.py:344
  7.6 2.5 %collective-permute-start.2 = (f32[2,128,128]{2,1,0:T(8,128)S(1)}, f32[2,128,128]{2,1,0:T(8,128)S(1)}, u32[]{:S(2)}, u32[]{:S(2)}) collective-permute-start(f32[2,128,128]{2,1,0:T(8,128)S(1)} %get-tuple-element.92), channel_id=1, source_target_pairs={{0,3},{1,2},{2,1},{3,0},{16,19},{17,18},{18,17},{19,16},{4,7},{5,6... | collective-permute-start | bytes 393224 | tf_op jit(solution)/shard_map/ppermute | solution.py:344
  10.7 2.0 %collective-permute-start.6 = (f32[2,128,128]{2,1,0:T(8,128)S(1)}, f32[2,128,128]{2,1,0:T(8,128)S(1)}, u32[]{:S(2)}, u32[]{:S(2)}) collective-permute-start(f32[2,128,128]{2,1,0:T(8,128)S(1)} %get-tuple-element.97), channel_id=1, source_target_pairs={{0,2},{1,3},{2,0},{3,1},{16,18},{17,19},{18,16},{19,17},{4,6},{5,7... | collective-permute-start | bytes 393224 | tf_op jit(solution)/shard_map/ppermute | solution.py:344
  12.7 2.5 %collective-permute-start.7 = (f32[2,128,128]{2,1,0:T(8,128)S(1)}, f32[2,128,128]{2,1,0:T(8,128)S(1)}, u32[]{:S(2)}, u32[]{:S(2)}) collective-permute-start(f32[2,128,128]{2,1,0:T(8,128)S(1)} %get-tuple-element.98), channel_id=1, source_target_pairs={{0,17},{1,16},{2,19},{3,18},{16,1},{17,0},{18,3},{19,2},{4,21},{5,... | collective-permute-start | bytes 393224 | tf_op jit(solution)/shard_map/ppermute | solution.py:344
  15.2 2.2 %collective-permute-start.8 = (f32[2,128,128]{2,1,0:T(8,128)S(1)}, f32[2,128,128]{2,1,0:T(8,128)S(1)}, u32[]{:S(2)}, u32[]{:S(2)}) collective-permute-start(f32[2,128,128]{2,1,0:T(8,128)S(1)} %get-tuple-element.99), channel_id=1, source_target_pairs={{0,19},{1,18},{2,17},{3,16},{16,3},{17,2},{18,1},{19,0},{4,23},{5,... | collective-permute-start | bytes 393224 | tf_op jit(solution)/shard_map/ppermute | solution.py:344
  17.3 2.2 %local_parts.1 = (bf16[16,4,128,128]{3,2,1,0:T(8,128)(2,1)S(1)}, f32[16,4,128,128]{3,2,1,0:T(8,128)S(1)}) custom-call(bf16[128,1024]{1,0:T(8,128)(2,1)S(1)} %get-tuple-element.82.refs_2_.refs_0_, bf16[128,1024]{1,0:T(8,128)(2,1)S(1)} %get-tuple-element.83.refs_3_.refs_1_, bf16[128,1024]{1,0:T(8,128)(2,1)S(1)} %get-tuple-element.84.refs_4_.refs_2_, ...), custom_call_target="tpu_custom_call" | custom-call | flops 536870912 | bytes 8388608 | tf_op jit(solution)/shard_map/local_parts/pallas_call | solution.py:234
  19.6 1.0 %collective-permute-done.6.refs_4_ = f32[2,128,128]{2,1,0:T(8,128)S(1)} collective-permute-done((f32[2,128,128]{2,1,0:T(8,128)S(1)}, f32[2,128,128]{2,1,0:T(8,128)S(1)}, u32[]{:S(2)}, u32[]{:S(2)}) %collective-permute-start.6) | collective-permute-done | bytes 131104 | tf_op jit(solution)/shard_map/ppermute | solution.py:344
  20.5 0.9 %collective-permute-done.7.refs_3_ = f32[2,128,128]{2,1,0:T(8,128)S(1)} collective-permute-done((f32[2,128,128]{2,1,0:T(8,128)S(1)}, f32[2,128,128]{2,1,0:T(8,128)S(1)}, u32[]{:S(2)}, u32[]{:S(2)}) %collective-permute-start.7) | collective-permute-done | bytes 131104 | tf_op jit(solution)/shard_map/ppermute | solution.py:344
  21.4 1.4 %collective-permute-done.8.refs_7_ = f32[2,128,128]{2,1,0:T(8,128)S(1)} collective-permute-done((f32[2,128,128]{2,1,0:T(8,128)S(1)}, f32[2,128,128]{2,1,0:T(8,128)S(1)}, u32[]{:S(2)}, u32[]{:S(2)}) %collective-permute-start.8) | collective-permute-done | bytes 131104 | tf_op jit(solution)/shard_map/ppermute | solution.py:344
  22.8 2.7 %collective-permute-start.9 = (f32[1,128,128]{2,1,0:T(8,128)S(1)}, f32[1,128,128]{2,1,0:T(8,128)S(1)}, u32[]{:S(2)}, u32[]{:S(2)}) collective-permute-start(f32[1,128,128]{2,1,0:T(8,128)S(1)} %block_total.1), channel_id=1, source_target_pairs={{0,4},{4,0},{1,5},{5,1},{2,6},{6,2},{3,7},{7,3},{8,12},{12,8},{9,1... | collective-permute-start | bytes 196616 | tf_op jit(solution)/shard_map/ppermute | solution.py:330
  25.7 3.1 %collective-permute-done.9.passed_ref = f32[1,128,128]{2,1,0:T(8,128)S(1)} collective-permute-done((f32[1,128,128]{2,1,0:T(8,128)S(1)}, f32[1,128,128]{2,1,0:T(8,128)S(1)}, u32[]{:S(2)}, u32[]{:S(2)}) %collective-permute-start.9) | collective-permute-done | bytes 65568 | tf_op jit(solution)/shard_map/ppermute | solution.py:330
  29.0 2.6 %collective-permute-start.15 = (f32[2,128,128]{2,1,0:T(8,128)S(1)}, f32[2,128,128]{2,1,0:T(8,128)S(1)}, u32[]{:S(2)}, u32[]{:S(2)}) collective-permute-start(f32[2,128,128]{2,1,0:T(8,128)S(1)} %get-tuple-element.131), channel_id=1, source_target_pairs={{0,3},{1,2},{2,1},{3,0},{16,19},{17,18},{18,17},{19,16},{4,7},{5,6... | collective-permute-start | bytes 393224 | tf_op jit(solution)/shard_map/ppermute | solution.py:344
  32.0 1.8 %collective-permute-start.19 = (f32[2,128,128]{2,1,0:T(8,128)S(1)}, f32[2,128,128]{2,1,0:T(8,128)S(1)}, u32[]{:S(2)}, u32[]{:S(2)}) collective-permute-start(f32[2,128,128]{2,1,0:T(8,128)S(1)} %get-tuple-element.133), channel_id=1, source_target_pairs={{0,17},{1,16},{2,19},{3,18},{16,1},{17,0},{18,3},{19,2},{4,21},{5,... | collective-permute-start | bytes 393224 | tf_op jit(solution)/shard_map/ppermute | solution.py:344
  33.9 1.1 %collective-permute-start.10 = (f32[2,128,128]{2,1,0:T(8,128)S(1)}, f32[2,128,128]{2,1,0:T(8,128)S(1)}, u32[]{:S(2)}, u32[]{:S(2)}) collective-permute-start(f32[2,128,128]{2,1,0:T(8,128)S(1)} %get-tuple-element.126), channel_id=1, source_target_pairs={{0,18},{1,19},{2,16},{3,17},{16,2},{17,3},{18,0},{19,1},{4,22},{5,... | collective-permute-start | bytes 393224 | tf_op jit(solution)/shard_map/ppermute | solution.py:344
  35.0 0.7 %collective-permute-done.13.refs_0_.refs_3_ = f32[2,128,128]{2,1,0:T(8,128)S(1)} collective-permute-done((f32[2,128,128]{2,1,0:T(8,128)S(1)}, f32[2,128,128]{2,1,0:T(8,128)S(1)}, u32[]{:S(2)}, u32[]{:S(2)}) %collective-permute-start.13) | collective-permute-done | bytes 131104 | tf_op jit(solution)/shard_map/ppermute | solution.py:344
  35.8 0.8 %collective-permute-start.11 = (f32[2,128,128]{2,1,0:T(8,128)S(1)}, f32[2,128,128]{2,1,0:T(8,128)S(1)}, u32[]{:S(2)}, u32[]{:S(2)}) collective-permute-start(f32[2,128,128]{2,1,0:T(8,128)S(1)} %get-tuple-element.127), channel_id=1, source_target_pairs={{0,1},{1,0},{2,3},{3,2},{16,17},{17,16},{18,19},{19,18},{4,5},{5,4... | collective-permute-start | bytes 393224 | tf_op jit(solution)/shard_map/ppermute | solution.py:344
  36.6 1.8 %collective-permute-start.12 = (f32[2,128,128]{2,1,0:T(8,128)S(1)}, f32[2,128,128]{2,1,0:T(8,128)S(1)}, u32[]{:S(2)}, u32[]{:S(2)}) collective-permute-start(f32[2,128,128]{2,1,0:T(8,128)S(1)} %get-tuple-element.128), channel_id=1, source_target_pairs={{0,19},{1,18},{2,17},{3,16},{16,3},{17,2},{18,1},{19,0},{4,23},{5,... | collective-permute-start | bytes 393224 | tf_op jit(solution)/shard_map/ppermute | solution.py:344
  39.2 0.7 %collective-permute-done.10.refs_0_.refs_2_ = f32[2,128,128]{2,1,0:T(8,128)S(1)} collective-permute-done((f32[2,128,128]{2,1,0:T(8,128)S(1)}, f32[2,128,128]{2,1,0:T(8,128)S(1)}, u32[]{:S(2)}, u32[]{:S(2)}) %collective-permute-start.10) | collective-permute-done | bytes 131104 | tf_op jit(solution)/shard_map/ppermute | solution.py:344
  40.0 1.5 %collective-permute-done.11.refs_1_.refs_3_ = f32[2,128,128]{2,1,0:T(8,128)S(1)} collective-permute-done((f32[2,128,128]{2,1,0:T(8,128)S(1)}, f32[2,128,128]{2,1,0:T(8,128)S(1)}, u32[]{:S(2)}, u32[]{:S(2)}) %collective-permute-start.11) | collective-permute-done | bytes 131104 | tf_op jit(solution)/shard_map/ppermute | solution.py:344
  41.5 1.4 %block_outputs.3 = (bf16[128,2048]{1,0:T(8,128)(2,1)}, bf16[128,2048]{1,0:T(8,128)(2,1)}, bf16[128,2048]{1,0:T(8,128)(2,1)}, bf16[128,2048]{1,0:T(8,128)(2,1)}) custom-call(s32[1]{0:T(128)} %bitcast._.core.___.__, s32[1]{0:T(128)} %bitcast.1.me.__._, s32[1]{0:T(128)} %bitcast.2.__.group._, s32[1]{0:T(128)} %bitcast._.core.___.__, ...), custom_call_target="tpu_custom_call" | custom-call | flops 83886080 | bytes 2621440 | tf_op jit(solution)/shard_map/block_outputs/pallas_call | solution.py:292
  43.6 1.6 %block_outputs.4 = (bf16[128,2048]{1,0:T(8,128)(2,1)}, bf16[128,2048]{1,0:T(8,128)(2,1)}, bf16[128,2048]{1,0:T(8,128)(2,1)}, bf16[128,2048]{1,0:T(8,128)(2,1)}) custom-call(s32[1]{0:T(128)} %bitcast._.core.___.__, s32[1]{0:T(128)} %bitcast.1.me.__._, ...), custom_call_target="tpu_custom_call", output_to_operand_aliasing={{0}: (17, {}), {1}: (18, {}), {2}: (19, {}), {3}: (20, {})} | custom-call | flops 117440512 | bytes 3670016 | tf_op jit(solution)/shard_map/block_outputs/pallas_call | solution.py:292
  45.5 1.2 %block_outputs.5 = (bf16[128,2048]{1,0:T(8,128)(2,1)}, bf16[128,2048]{1,0:T(8,128)(2,1)}, bf16[128,2048]{1,0:T(8,128)(2,1)}, bf16[128,2048]{1,0:T(8,128)(2,1)}) custom-call(s32[1]{0:T(128)} %bitcast._.core.___.__, s32[1]{0:T(128)} %bitcast.1.me.__._, ...), custom_call_target="tpu_custom_call", output_to_operand_aliasing={{0}: (11, {}), {1}: (12, {}), {2}: (13, {}), {3}: (14, {})} | custom-call | flops 67108864 | bytes 2097152 | tf_op jit(solution)/shard_map/block_outputs/pallas_call | solution.py:292
  (36 shorter events, 4.8 us)
Async XLA Ops:
  2.5 2.1 %collective-permute-start = (f32[4,2,128,128]{3,2,1,0:T(8,128)S(1)}, f32[4,2,128,128]{3,2,1,0:T(8,128)S(1)}, u32[]{:S(2)}, u32[]{:S(2)}) collective-permute-start(f32[4,2,128,128]{3,2,1,0:T(8,128)S(1)} %get-tuple-element.89), channel_id=1, source_target_pairs={{0,8},{8,0},{1,9},{9,1},{2,10},{10,2},{3,11},{11,3},{4,12},{12,4},... | collective-permute-start | bytes 1572872 | tf_op jit(solution)/shard_map/ppermute | solution.py:330
  3.7 6.9 %collective-permute-start.5 = (f32[4,2,128,128]{3,2,1,0:T(8,128)S(1)}, f32[4,2,128,128]{3,2,1,0:T(8,128)S(1)}, u32[]{:S(2)}, u32[]{:S(2)}) collective-permute-start(f32[4,2,128,128]{3,2,1,0:T(8,128)S(1)} %get-tuple-element.96), channel_id=1, source_target_pairs={{0,8},{8,0},{1,9},{9,1},{2,10},{10,2},{3,11},{11,3},{4,12},{12,4},... | collective-permute-start | bytes 1572872 | tf_op jit(solution)/shard_map/ppermute | solution.py:330
  4.6 8.1 %collective-permute-start.1 = (f32[2,128,128]{2,1,0:T(8,128)S(1)}, f32[2,128,128]{2,1,0:T(8,128)S(1)}, u32[]{:S(2)}, u32[]{:S(2)}) collective-permute-start(f32[2,128,128]{2,1,0:T(8,128)S(1)} %get-tuple-element.91), channel_id=1, source_target_pairs={{0,16},{1,17},{2,18},{3,19},{16,0},{17,1},{18,2},{19,3},{4,20},{5,... | collective-permute-start | bytes 393224 | tf_op jit(solution)/shard_map/ppermute | solution.py:344
  7.6 7.6 %collective-permute-start.2 = (f32[2,128,128]{2,1,0:T(8,128)S(1)}, f32[2,128,128]{2,1,0:T(8,128)S(1)}, u32[]{:S(2)}, u32[]{:S(2)}) collective-permute-start(f32[2,128,128]{2,1,0:T(8,128)S(1)} %get-tuple-element.92), channel_id=1, source_target_pairs={{0,3},{1,2},{2,1},{3,0},{16,19},{17,18},{18,17},{19,16},{4,7},{5,6... | collective-permute-start | bytes 393224 | tf_op jit(solution)/shard_map/ppermute | solution.py:344
  10.1 9.5 %collective-permute-start.3 = (f32[2,128,128]{2,1,0:T(8,128)S(1)}, f32[2,128,128]{2,1,0:T(8,128)S(1)}, u32[]{:S(2)}, u32[]{:S(2)}) collective-permute-start(f32[2,128,128]{2,1,0:T(8,128)S(1)} %get-tuple-element.93), channel_id=1, source_target_pairs={{0,1},{1,0},{2,3},{3,2},{16,17},{17,16},{18,19},{19,18},{4,5},{5,4... | collective-permute-start | bytes 393224 | tf_op jit(solution)/shard_map/ppermute | solution.py:344
  10.6 9.0 %collective-permute-start.4 = (f32[2,128,128]{2,1,0:T(8,128)S(1)}, f32[2,128,128]{2,1,0:T(8,128)S(1)}, u32[]{:S(2)}, u32[]{:S(2)}) collective-permute-start(f32[2,128,128]{2,1,0:T(8,128)S(1)} %get-tuple-element.94), channel_id=1, source_target_pairs={{0,18},{1,19},{2,16},{3,17},{16,2},{17,3},{18,0},{19,1},{4,22},{5,... | collective-permute-start | bytes 393224 | tf_op jit(solution)/shard_map/ppermute | solution.py:344
  10.7 9.8 %collective-permute-start.6 = (f32[2,128,128]{2,1,0:T(8,128)S(1)}, f32[2,128,128]{2,1,0:T(8,128)S(1)}, u32[]{:S(2)}, u32[]{:S(2)}) collective-permute-start(f32[2,128,128]{2,1,0:T(8,128)S(1)} %get-tuple-element.97), channel_id=1, source_target_pairs={{0,2},{1,3},{2,0},{3,1},{16,18},{17,19},{18,16},{19,17},{4,6},{5,7... | collective-permute-start | bytes 393224 | tf_op jit(solution)/shard_map/ppermute | solution.py:344
  12.7 8.6 %collective-permute-start.7 = (f32[2,128,128]{2,1,0:T(8,128)S(1)}, f32[2,128,128]{2,1,0:T(8,128)S(1)}, u32[]{:S(2)}, u32[]{:S(2)}) collective-permute-start(f32[2,128,128]{2,1,0:T(8,128)S(1)} %get-tuple-element.98), channel_id=1, source_target_pairs={{0,17},{1,16},{2,19},{3,18},{16,1},{17,0},{18,3},{19,2},{4,21},{5,... | collective-permute-start | bytes 393224 | tf_op jit(solution)/shard_map/ppermute | solution.py:344
  15.2 7.6 %collective-permute-start.8 = (f32[2,128,128]{2,1,0:T(8,128)S(1)}, f32[2,128,128]{2,1,0:T(8,128)S(1)}, u32[]{:S(2)}, u32[]{:S(2)}) collective-permute-start(f32[2,128,128]{2,1,0:T(8,128)S(1)} %get-tuple-element.99), channel_id=1, source_target_pairs={{0,19},{1,18},{2,17},{3,16},{16,3},{17,2},{18,1},{19,0},{4,23},{5,... | collective-permute-start | bytes 393224 | tf_op jit(solution)/shard_map/ppermute | solution.py:344
  22.8 5.9 %collective-permute-start.9 = (f32[1,128,128]{2,1,0:T(8,128)S(1)}, f32[1,128,128]{2,1,0:T(8,128)S(1)}, u32[]{:S(2)}, u32[]{:S(2)}) collective-permute-start(f32[1,128,128]{2,1,0:T(8,128)S(1)} %block_total.1), channel_id=1, source_target_pairs={{0,4},{4,0},{1,5},{5,1},{2,6},{6,2},{3,7},{7,3},{8,12},{12,8},{9,1... | collective-permute-start | bytes 196616 | tf_op jit(solution)/shard_map/ppermute | solution.py:330
  28.9 6.9 %collective-permute-start.13 = (f32[2,128,128]{2,1,0:T(8,128)S(1)}, f32[2,128,128]{2,1,0:T(8,128)S(1)}, u32[]{:S(2)}, u32[]{:S(2)}) collective-permute-start(f32[2,128,128]{2,1,0:T(8,128)S(1)} %get-tuple-element.130), channel_id=1, source_target_pairs={{0,16},{1,17},{2,18},{3,19},{16,0},{17,1},{18,2},{19,3},{4,20},{5,... | collective-permute-start | bytes 393224 | tf_op jit(solution)/shard_map/ppermute | solution.py:344
  29.0 7.6 %collective-permute-start.15 = (f32[2,128,128]{2,1,0:T(8,128)S(1)}, f32[2,128,128]{2,1,0:T(8,128)S(1)}, u32[]{:S(2)}, u32[]{:S(2)}) collective-permute-start(f32[2,128,128]{2,1,0:T(8,128)S(1)} %get-tuple-element.131), channel_id=1, source_target_pairs={{0,3},{1,2},{2,1},{3,0},{16,19},{17,18},{18,17},{19,16},{4,7},{5,6... | collective-permute-start | bytes 393224 | tf_op jit(solution)/shard_map/ppermute | solution.py:344
  31.6 7.0 %collective-permute-start.17 = (f32[2,128,128]{2,1,0:T(8,128)S(1)}, f32[2,128,128]{2,1,0:T(8,128)S(1)}, u32[]{:S(2)}, u32[]{:S(2)}) collective-permute-start(f32[2,128,128]{2,1,0:T(8,128)S(1)} %get-tuple-element.132), channel_id=1, source_target_pairs={{0,2},{1,3},{2,0},{3,1},{16,18},{17,19},{18,16},{19,17},{4,6},{5,7... | collective-permute-start | bytes 393224 | tf_op jit(solution)/shard_map/ppermute | solution.py:344
  32.0 6.6 %collective-permute-start.19 = (f32[2,128,128]{2,1,0:T(8,128)S(1)}, f32[2,128,128]{2,1,0:T(8,128)S(1)}, u32[]{:S(2)}, u32[]{:S(2)}) collective-permute-start(f32[2,128,128]{2,1,0:T(8,128)S(1)} %get-tuple-element.133), channel_id=1, source_target_pairs={{0,17},{1,16},{2,19},{3,18},{16,1},{17,0},{18,3},{19,2},{4,21},{5,... | collective-permute-start | bytes 393224 | tf_op jit(solution)/shard_map/ppermute | solution.py:344
  33.9 6.1 %collective-permute-start.10 = (f32[2,128,128]{2,1,0:T(8,128)S(1)}, f32[2,128,128]{2,1,0:T(8,128)S(1)}, u32[]{:S(2)}, u32[]{:S(2)}) collective-permute-start(f32[2,128,128]{2,1,0:T(8,128)S(1)} %get-tuple-element.126), channel_id=1, source_target_pairs={{0,18},{1,19},{2,16},{3,17},{16,2},{17,3},{18,0},{19,1},{4,22},{5,... | collective-permute-start | bytes 393224 | tf_op jit(solution)/shard_map/ppermute | solution.py:344
  35.8 5.7 %collective-permute-start.11 = (f32[2,128,128]{2,1,0:T(8,128)S(1)}, f32[2,128,128]{2,1,0:T(8,128)S(1)}, u32[]{:S(2)}, u32[]{:S(2)}) collective-permute-start(f32[2,128,128]{2,1,0:T(8,128)S(1)} %get-tuple-element.127), channel_id=1, source_target_pairs={{0,1},{1,0},{2,3},{3,2},{16,17},{17,16},{18,19},{19,18},{4,5},{5,4... | collective-permute-start | bytes 393224 | tf_op jit(solution)/shard_map/ppermute | solution.py:344
  36.6 6.8 %collective-permute-start.12 = (f32[2,128,128]{2,1,0:T(8,128)S(1)}, f32[2,128,128]{2,1,0:T(8,128)S(1)}, u32[]{:S(2)}, u32[]{:S(2)}) collective-permute-start(f32[2,128,128]{2,1,0:T(8,128)S(1)} %get-tuple-element.128), channel_id=1, source_target_pairs={{0,19},{1,18},{2,17},{3,16},{16,3},{17,2},{18,1},{19,0},{4,23},{5,... | collective-permute-start | bytes 393224 | tf_op jit(solution)/shard_map/ppermute | solution.py:344
  38.6 4.9 %collective-permute-start.14 = (f32[1,2,128,128]{3,2,1,0:T(8,128)S(1)}, f32[1,2,128,128]{3,2,1,0:T(8,128)S(1)}, u32[]{:S(2)}, u32[]{:S(2)}) collective-permute-start(f32[1,2,128,128]{3,2,1,0:T(8,128)S(1)} %sibling_state.5), channel_id=1, source_target_pairs={{0,8},{8,0},{1,9},{9,1},{2,10},{10,2},{3,11},{11,3},{4,12},{12,4},... | collective-permute-start | bytes 393224 | tf_op jit(solution)/shard_map/ppermute | solution.py:330
  38.6 4.8 %collective-permute-start.16 = (f32[1,2,128,128]{3,2,1,0:T(8,128)S(1)}, f32[1,2,128,128]{3,2,1,0:T(8,128)S(1)}, u32[]{:S(2)}, u32[]{:S(2)}) collective-permute-start(f32[1,2,128,128]{3,2,1,0:T(8,128)S(1)} %sibling_state.6), channel_id=1, source_target_pairs={{0,8},{8,0},{1,9},{9,1},{2,10},{10,2},{3,11},{11,3},{4,12},{12,4},... | collective-permute-start | bytes 393224 | tf_op jit(solution)/shard_map/ppermute | solution.py:330
  40.0 3.5 %collective-permute-start.18 = (f32[1,2,128,128]{3,2,1,0:T(8,128)S(1)}, f32[1,2,128,128]{3,2,1,0:T(8,128)S(1)}, u32[]{:S(2)}, u32[]{:S(2)}) collective-permute-start(f32[1,2,128,128]{3,2,1,0:T(8,128)S(1)} %sibling_state.7), channel_id=1, source_target_pairs={{0,8},{8,0},{1,9},{9,1},{2,10},{10,2},{3,11},{11,3},{4,12},{12,4},... | collective-permute-start | bytes 393224 | tf_op jit(solution)/shard_map/ppermute | solution.py:330
  41.5 2.0 %collective-permute-start.20 = (f32[1,2,128,128]{3,2,1,0:T(8,128)S(1)}, f32[1,2,128,128]{3,2,1,0:T(8,128)S(1)}, u32[]{:S(2)}, u32[]{:S(2)}) collective-permute-start(f32[1,2,128,128]{3,2,1,0:T(8,128)S(1)} %sibling_state.8), channel_id=1, source_target_pairs={{0,8},{8,0},{1,9},{9,1},{2,10},{10,2},{3,11},{11,3},{4,12},{12,4},... | collective-permute-start | bytes 393224 | tf_op jit(solution)/shard_map/ppermute | solution.py:330
  43.6 2.0 %collective-permute-start.21 = (f32[4,2,128,128]{3,2,1,0:T(8,128)S(1)}, f32[4,2,128,128]{3,2,1,0:T(8,128)S(1)}, u32[]{:S(2)}, u32[]{:S(2)}) collective-permute-start(f32[4,2,128,128]{3,2,1,0:T(8,128)S(1)} %sibling_state.9), channel_id=1, source_target_pairs={{0,8},{8,0},{1,9},{9,1},{2,10},{10,2},{3,11},{11,3},{4,12},{12,4},... | collective-permute-start | bytes 1572872 | tf_op jit(solution)/shard_map/ppermute | solution.py:330
